TPU v7x, 32 devices: a whole 2x2x4 slice. The times are simulated.
32 devices in a mesh: pool: 4 (over x, core), dev: 8 (over z, y).
Axes of the slice: x: 2, y: 2, z: 4, core: 2. Of those that a mesh axis runs over, the one named last changes fastest.
Arguments:
- hidden_in: bfloat16 [32, 7168], P('pool', 'dev'), may hold values from -32 to 32
- in_gain: float32 [7168], P('dev'), may hold values from 0.25 to 1.75
- w_latent: bfloat16 [7168, 2560], P('dev'), may hold values from -0.0625 to 0.0625
- q_gain: float32 [2048], replicated, may hold values from 0.25 to 1.75
- w_query: bfloat16 [2048, 16384], P(None, 'dev'), may hold values from -0.125 to 0.125
- cache_keys: bfloat16 [32, 4096, 256], P('pool', 'dev'), may hold values from -240 to 240
- cache_values: bfloat16 [32, 4096, 256], P('pool', 'dev'), may hold values from -6 to 6
- lengths: int32 [32], P('pool'), may hold values from 1 to 4096, 65536 in all
- w_out: bfloat16 [16384, 7168], P('dev'), may hold values from -0.125 to 0.125
- post_gain: float32 [7168], P('dev'), may hold values from 0.25 to 1.75
- w_gate: bfloat16 [7168, 18432], P(None, ('pool', 'dev')), may hold values from -0.0625 to 0.0625
- w_up: bfloat16 [7168, 18432], P(None, ('pool', 'dev')), may hold values from -0.0625 to 0.0625
- w_down: bfloat16 [18432, 7168], P(('pool', 'dev')), may hold values from -0.078125 to 0.078125
Outputs:
- mixed: float32 [32, 7168], P('pool', 'dev')
All inputs are finite; a program needn't handle non-finite values. No bound on the sum of `lengths` on one device may be relied on, other than what follows from the above.
Results may differ from a plain program's by a relative error of at most 0.013.
Values may be sent and summed in bfloat16 or wider, within the bound.
No kernel may reach another device: no remote copies, remote signals or barrier semaphores. Data moves between devices by JAX's collectives and lax.ppermute only.
A program may use at most 128 MiB of HBM per device.

v0:
```python
import math

import jax
import jax.numpy as jnp
from jax import lax
from jax.sharding import PartitionSpec as P

D = 7168
H = 64
HD = 256
QR = 2048


EPS = 1e-05
NEG = -1e30


def merged(value, axis, join):
    pieces = jax.tree.map(lambda part: lax.all_gather(part, axis), value)
    head = jax.tree.map(lambda part: part[0], pieces)
    tail = jax.tree.map(lambda part: part[1:], pieces)
    so_far, _ = lax.scan(lambda so_far, section: (join(so_far, section), None), head, tail)
    return so_far


def combine_parts(left_part, right_part):
    highest = jnp.maximum(left_part[0], right_part[0])
    left_factor = jnp.exp(left_part[0] - highest)
    right_factor = jnp.exp(right_part[0] - highest)
    mass = left_part[1] * left_factor + right_part[1] * right_factor
    summed = left_part[2] * left_factor[..., None] + right_part[2] * right_factor[..., None]
    return (highest, mass, summed)


def local(
    hidden_in,
    in_gain,
    w_latent,
    q_gain,
    w_query,
    cache_keys,
    cache_values,
    lengths,
    w_out,
    post_gain,
    w_gate,
    w_up,
    w_down,
):
    n_dev = lax.axis_size("dev")
    n_pool = lax.axis_size("pool")
    rows_here = hidden_in.shape[0]
    local_pos = cache_keys.shape[1]
    head_cols = w_out.shape[0]
    scale_inv = 1.0 / math.sqrt(HD)
    hidden_f = hidden_in.astype(jnp.float32)
    scaled_in = (hidden_f * in_gain[None, :]).astype(jnp.bfloat16)
    latent_part = jnp.dot(scaled_in, w_latent, preferred_element_type=jnp.float32)
    square_part = jnp.sum(hidden_f * hidden_f, axis=1)
    latent, squares = lax.psum((latent_part, square_part), "dev")
    latent = latent * lax.rsqrt(squares / D + EPS)[:, None]
    query_latent = latent[:, :QR]
    key_new = latent[:, QR : QR + HD].astype(jnp.bfloat16)
    value_new = latent[:, QR + HD :].astype(jnp.bfloat16)
    latent_mean = jnp.mean(query_latent * query_latent, axis=1)
    query_normed = (query_latent * lax.rsqrt(latent_mean + EPS)[:, None] * q_gain[None, :]).astype(
        jnp.bfloat16
    )
    query_local = jnp.dot(query_normed, w_query, preferred_element_type=jnp.float32).astype(
        jnp.bfloat16
    )
    query_all = lax.all_gather(query_local, "dev", axis=1, tiled=True).reshape(rows_here, H, HD)
    scores = (
        jnp.einsum("rhd,rpd->rhp", query_all, cache_keys, preferred_element_type=jnp.float32)
        * scale_inv
    )
    positions = lax.axis_index("dev") * local_pos + jnp.arange(local_pos, dtype=jnp.int32)
    valid_mask = (positions[None, :] < lengths[:, None])[:, None, :]
    masked = jnp.where(valid_mask, scores, NEG)
    top_local = jnp.max(masked, axis=-1)
    weights = jnp.where(valid_mask, jnp.exp(masked - top_local[..., None]), 0.0)
    mass_local = jnp.sum(weights, axis=-1)
    weighted = jnp.einsum(
        "rhp,rpd->rhd",
        weights.astype(jnp.bfloat16),
        cache_values,
        preferred_element_type=jnp.float32,
    )
    score_new = (
        jnp.sum(query_all.astype(jnp.float32) * key_new.astype(jnp.float32)[:, None, :], axis=-1)
        * scale_inv
    )
    value_wide = value_new.astype(jnp.float32)[:, None, :]
    own_start = lax.axis_index("dev") * head_cols
    top_all, mass_all, weighted_all = merged(
        (top_local, mass_local, weighted), "dev", combine_parts
    )
    top_new = jnp.maximum(top_all, score_new)
    keep_factor = jnp.exp(top_all - top_new)
    fresh_weight = jnp.exp(score_new - top_new)
    mass_total = mass_all * keep_factor + fresh_weight
    numerator = (
        weighted_all * keep_factor[..., None]
        + fresh_weight.astype(jnp.bfloat16).astype(jnp.float32)[..., None] * value_wide
    )
    attended = (numerator / mass_total[..., None]).astype(jnp.bfloat16).reshape(rows_here, H * HD)
    own_heads = lax.dynamic_slice_in_dim(attended, own_start, head_cols, 1)
    head_sum = jnp.dot(own_heads, w_out, preferred_element_type=jnp.float32)
    attn_part = lax.psum_scatter(head_sum, "dev", scatter_dimension=1, tiled=True)
    residual = hidden_f + attn_part
    row_squares = lax.psum(jnp.sum(residual * residual, axis=1), "dev")
    normed = (residual * lax.rsqrt(row_squares / D + EPS)[:, None] * post_gain[None, :]).astype(
        jnp.bfloat16
    )
    slice_cols = normed.shape[1]
    ff_cols = w_gate.shape[1]
    gathered = lax.all_gather(normed, ("pool", "dev"), axis=0, tiled=True).reshape(
        n_pool, n_dev, rows_here, slice_cols
    )
    gate_out = jnp.einsum(
        "pdrc,dcf->prf",
        gathered,
        w_gate.reshape(n_dev, slice_cols, ff_cols),
        preferred_element_type=jnp.float32,
    )
    up_out = jnp.einsum(
        "pdrc,dcf->prf",
        gathered,
        w_up.reshape(n_dev, slice_cols, ff_cols),
        preferred_element_type=jnp.float32,
    )
    activated = (jax.nn.silu(gate_out) * up_out).astype(jnp.bfloat16)
    ffn_term = jnp.einsum(
        "prf,fdc->pdrc",
        activated,
        w_down.reshape(ff_cols, n_dev, slice_cols),
        preferred_element_type=jnp.float32,
    )
    ffn_term = ffn_term.reshape(n_pool * n_dev * rows_here, slice_cols)
    ffn_out = lax.psum_scatter(ffn_term, ("pool", "dev"), scatter_dimension=0, tiled=True)
    return residual + ffn_out


def solution(mesh):
    placed = (
        P("pool", "dev"),
        P("dev"),
        P("dev", None),
        P(),
        P(None, "dev"),
        P("pool", "dev", None),
        P("pool", "dev", None),
        P("pool"),
        P("dev", None),
        P("dev"),
        P(None, ("pool", "dev")),
        P(None, ("pool", "dev")),
        P(("pool", "dev"), None),
    )
    return jax.shard_map(
        local, mesh=mesh, in_specs=placed, out_specs=P("pool", "dev"), check_vma=False
    )
```

profile of v0, /device:TPU:0, one launch (start us, length us, event | category | flops | bytes accessed | tf_op | source)
XLA Modules:
  0.0 512.2 jit_solution(5900092178815213979)
XLA Ops:
  6.5 0.0 copy-start
  6.5 0.0 all-reduce.4.cloned.1.call-start
  6.5 3.8 fusion.30
  10.3 0.0 all-reduce.4.cloned.1.call-update
  10.4 0.0 all-gather.5.cloned.1.call-start
  10.4 0.8 fusion.29
  11.3 23.2 %psum.22 = f32[8]{0:T(128)S(1)} all-reduce(f32[8]{0:T(128)S(1)} %fusion.29), channel_id=1, replica_groups=mesh['pool'=4,'dev'=8] {'dev'}, use_global_device_ids=true, to_apply=%region_2.0 | all-reduce | flops 8 | bytes 64 | tf_op jit(solution)/shard_map/psum | solution.py:60
  34.4 0.7 broadcast_compare_fusion
  35.2 47.1 %all-reduce.4.cloned.1.call-done = f32[8,2560]{1,0:T(8,128)} async-done(((f32[8,2560]{1,0:T(8,128)}), f32[8,2560]{1,0:T(8,128)}) %all-reduce.4.cloned.1.call-update) | async-done | bytes 81936 | tf_op jit(solution)/shard_map/psum | solution.py:60
  82.3 1.0 fusion.38
  83.3 0.1 multiply_reduce_fusion.1
  83.4 0.0 copy-start.2
  83.4 4.8 convolution_convert_fusion
  88.2 30.8 %all_gather.24 = bf16[8,16384]{1,0:T(8,128)(2,1)S(1)} all-gather(bf16[8,2048]{1,0:T(8,128)(2,1)S(1)} %convolution_convert_fusion), channel_id=1, replica_groups=mesh['pool'=4,'dev'=8] {'dev'}, dimensions={1}, use_global_device_ids=true | all-gather | bytes 294912 | tf_op jit(solution)/shard_map/all_gather | solution.py:72
  119.0 0.0 copy-done
  119.0 0.8 fusion.39
  119.9 0.0 copy-done.2
  119.9 1.4 fusion.17
  121.2 0.0 all-gather.5.cloned.1.call-update
  121.3 0.0 reduce-scatter.2.cloned.1.call-start
  121.3 0.1 multiply_reduce_fusion
  121.5 0.1 copy.27
  121.5 30.7 %all-gather = f32[64,64]{1,0:T(8,128)S(1)} all-gather(f32[8,64]{1,0:T(8,128)S(1)} %get-tuple-element.72), channel_id=2, replica_groups=mesh['pool'=4,'dev'=8] {'dev'}, dimensions={0}, use_global_device_ids=true | all-gather | bytes 18432 | tf_op jit(solution)/shard_map/all_gather | solution.py:19
  152.3 0.3 fusion.16
  152.6 31.1 %all-gather.1 = f32[64,64]{1,0:T(8,128)S(1)} all-gather(f32[8,64]{1,0:T(8,128)S(1)} %fusion.16), channel_id=3, replica_groups=mesh['pool'=4,'dev'=8] {'dev'}, dimensions={0}, use_global_device_ids=true | all-gather | bytes 18432 | tf_op jit(solution)/shard_map/all_gather | solution.py:19
  183.7 11.3 %all-gather.5.cloned.1.call-done = f32[64,64,256]{2,1,0:T(8,128)} async-done(((f32[8,64,256]{2,1,0:T(8,128)}), f32[64,64,256]{2,1,0:T(8,128)}) %all-gather.5.cloned.1.call-update) | async-done | bytes 4194320 | tf_op jit(solution)/shard_map/all_gather | solution.py:19
  195.0 0.0 slice-start
  195.0 4.3 slice.50
  199.4 0.0 slice-done
  199.4 9.3 %while.14 = (s32[]{:T(128)}, f32[8,64]{1,0:T(8,128)S(1)}, f32[8,64]{1,0:T(8,128)S(1)}, f32[8,64,256]{2,1,0:T(8,128)S(1)}, f32[7,8,64]{2,1,0:T(8,128)S(1)}, /*ind...) while((s32[]{:T(128)}, f32[8,64]{1,0:T(8,128)S(1)}, f32[8,64]{1,0:T(8,128)S(1)}, ...), condition=%wide.region_7.8_spmd, body=%wide.region_6.7_spmd.sunk | while | flops 396290 | bytes 1593445 | solution.py:22
  199.4 1.3 fusion.51
  200.7 1.3 fusion.51
  202.1 1.3 fusion.51
  203.4 1.3 fusion.51
  204.7 1.3 fusion.51
  206.1 1.3 fusion.51
  207.4 1.3 fusion.51
  208.7 0.3 fusion.23
  209.0 0.2 copy.37
  209.1 0.0 copy-start.3
  209.1 0.0 copy-start.5
  209.2 12.0 %fusion.24 = f32[8,7168]{1,0:T(8,128)} fusion(bf16[2048,7168]{1,0:T(8,128)(2,1)} %param.23, bf16[8,16384]{1,0:T(8,128)(2,1)S(1)} %bitcast.103, s32[]{:T(128)S(6)} %select_n.12), kind=kOutput, calls=%fused_computation.42 | convolution fusion | flops 234881024 | bytes 29622276 | tf_op jit(solution)/shard_map/dot_general | solution.py:108
  221.2 0.0 reduce-scatter.2.cloned.1.call-update
  221.2 0.0 all-reduce.6.cloned.1.call-start
  221.3 52.9 %reduce-scatter.2.cloned.1.call-done = f32[8,896]{1,0:T(8,128)} async-done(((f32[8,7168]{1,0:T(8,128)}), f32[8,896]{1,0:T(8,128)}) %reduce-scatter.2.cloned.1.call-update) | async-done | bytes 28688 | tf_op jit(solution)/shard_map/reduce_scatter | solution.py:109
  274.2 0.0 copy-done.3
  274.2 0.9 multiply_reduce_fusion.2
  275.1 19.5 %psum.23 = f32[8]{0:T(128)S(1)} all-reduce(f32[8]{0:T(128)S(1)} %multiply_reduce_fusion.2), channel_id=1, replica_groups=mesh['pool'=4,'dev'=8] {'dev'}, use_global_device_ids=true, to_apply=%region_11.12 | all-reduce | flops 8 | bytes 64 | tf_op jit(solution)/shard_map/psum | solution.py:111
  294.5 0.0 copy-done.5
  294.6 0.8 multiply_convert_fusion.2
  295.4 66.3 %all_gather.31 = bf16[256,896]{1,0:T(8,128)(2,1)S(1)} all-gather(bf16[8,896]{1,0:T(8,128)(2,1)S(1)} %multiply_convert_fusion.2), channel_id=1, replica_groups=mesh['pool'=4,'dev'=8] {'pool','dev'}, dimensions={0}, use_global_device_ids=true | all-gather | bytes 473088 | tf_op jit(solution)/shard_map/all_gather | solution.py:117
  361.7 5.7 %fusion.10 = f32[4,8,576]{2,1,0:T(8,128)S(1)} fusion(bf16[4,8,8,896]{3,2,1,0:T(8,128)(2,1)S(1)} %bitcast.101, bf16[72,8,8,896]{3,2,1,0:T(8,128)(2,1)} %bitcast.104), kind=kOutput, calls=%fused_computation.20 | convolution fusion | flops 264241152 | bytes 8790016 | tf_op jit(solution)/shard_map/pdrc,dcf->prf/dot_general | solution.py:120
  367.4 0.0 slice-start.1
  367.4 0.0 slice-start.2
  367.4 5.9 %fusion.14 = bf16[4,8,576,1]{2,1,3,0:T(8,128)(2,1)S(1)} fusion(bf16[4,8,8,896]{3,2,1,0:T(8,128)(2,1)S(1)} %bitcast.102, bf16[72,8,8,896]{3,2,1,0:T(8,128)(2,1)} %bitcast.105, f32[4,8,576]{2,1,0:T(8,128)S(1)} %fusion.10), kind=kOutput, calls=%fused_computation.24 | convolution fusion | flops 264351744 | bytes 8826880 | tf_op jit(solution)/shard_map/pdrc,dcf->prf/dot_general | solution.py:126
  373.3 0.0 slice-done.1
  373.3 0.0 slice-done.2
  373.4 0.0 copy-start.4
  373.4 2.4 fusion.3
  375.8 0.0 all-reduce.6.cloned.1.call-update
  375.8 128.5 %all-reduce.6.cloned.1.call-done = f32[256,896]{1,0:T(8,128)} async-done(((f32[256,896]{1,0:T(8,128)}), f32[256,896]{1,0:T(8,128)}) %all-reduce.6.cloned.1.call-update) | async-done | bytes 917520
  504.3 0.0 copy-done.4
  504.3 1.4 dynamic-slice_add_fusion
  505.7 0.0 copy-done.1
  (19 shorter events, 0.2 us)
Async XLA Ops:
  6.5 112.5 %copy-start = (bf16[8,512,256]{2,1,0:T(8,128)(2,1)S(1)}, bf16[8,512,256]{2,1,0:T(8,128)(2,1)}, u32[]{:S(2)}) copy-start(bf16[8,512,256]{2,1,0:T(8,128)(2,1)} %param.20) | copy-start | bytes 6291460
  6.5 75.8 %all-reduce.4.cloned.1.call-start = ((), (), s32[]{:S(2)}) async-start(), calls=%async_computation.1 | async-start | bytes 163840 | tf_op jit(solution)/shard_map/psum | solution.py:60
  10.4 184.7 %all-gather.5.cloned.1.call-start = ((), (), s32[]{:S(2)}) async-start(), calls=%async_computation.3 | async-start | bytes 4718592 | tf_op jit(solution)/shard_map/all_gather | solution.py:19
  83.4 36.5 %copy-start.2 = (bf16[8,512,256]{2,1,0:T(8,128)(2,1)S(1)}, bf16[8,512,256]{2,1,0:T(8,128)(2,1)}, u32[]{:S(2)}) copy-start(bf16[8,512,256]{2,1,0:T(8,128)(2,1)} %param.21) | copy-start | bytes 6291460
  121.3 152.9 %reduce-scatter.2.cloned.1.call-start = ((), (), s32[]{:S(2)}) async-start(), calls=%async_computation.2 | async-start | bytes 258048 | tf_op jit(solution)/shard_map/reduce_scatter | solution.py:109
  195.0 4.3 slice-start
  209.1 65.1 %copy-start.3 = (bf16[8,896]{1,0:T(8,128)(2,1)S(1)}, bf16[8,896]{1,0:T(8,128)(2,1)}, u32[]{:S(2)}) copy-start(bf16[8,896]{1,0:T(8,128)(2,1)} %param.15) | copy-start | bytes 43012
  209.1 85.4 %copy-start.5 = (f32[896]{0:T(1024)S(1)}, f32[896]{0:T(1024)}, u32[]{:S(2)}) copy-start(f32[896]{0:T(1024)} %param.24) | copy-start | bytes 10756
  221.2 283.1 %all-reduce.6.cloned.1.call-start = ((), (), s32[]{:S(2)}) async-start(), calls=%async_computation.4 | async-start | bytes 1835008
  367.4 5.9 %slice-start.1 = ((s8[8257536]{0:T(1024)(128)(4,1)}), s8[4194304]{0:T(1024)(128)(4,1)S(1)}, s32[]{:S(2)}) async-start(s8[8257536]{0:T(1024)(128)(4,1)} %bitcast.106), calls=%async_computation.6 | async-start | bytes 8388608
  367.4 5.9 %slice-start.2 = ((s8[8257536]{0:T(1024)(128)(4,1)}), s8[4063232]{0:T(1024)(128)(4,1)S(1)}, s32[]{:S(2)}) async-start(s8[8257536]{0:T(1024)(128)(4,1)} %bitcast.106), calls=%async_computation.7 | async-start | bytes 8126464
  373.3 132.4 %copy-start.1 = (bf16[8,512,256]{2,1,0:T(8,128)(2,1)S(1)}, bf16[8,512,256]{2,1,0:T(8,128)(2,1)}, u32[]{:S(2)}) copy-start(bf16[8,512,256]{2,1,0:T(8,128)(2,1)} %param.20) | copy-start | bytes 6291460
  373.4 131.0 %copy-start.4 = (f32[8,896]{1,0:T(8,128)S(1)}, f32[8,896]{1,0:T(8,128)}, u32[]{:S(2)}) copy-start(f32[8,896]{1,0:T(8,128)} %reduce-scatter.2.cloned.1.call-done) | copy-start | bytes 86020
Sparse Core Ops, SparseCore 0:
  10.8 71.4 all-reduce.3
  121.4 73.6 all-gather.4
  221.4 52.8 reduce-scatter.1
  376.0 128.3 all-reduce.5
where the time goes:
time: 513 us; the launch traced here: 512 us
  waiting for transfers between devices  240 us (47%)
  blocking collectives  202 us (39%)
  matrix products  36.9 us (7%)
  other arithmetic  15.6 us (3%)
  between operations  13.3 us (3%)
    unnamed x5, waiting for transfers between devices  129 us
    all_gather x1, blocking collectives, local(): lax.all_gather(normed, ('pool', 'dev'), axis=0, tiled=True)  66.3 us
    all_gather x2, blocking collectives, merged(): pieces = jax.tree.map(lambda part: lax.all_gather(part, axis), value)  61.8 us
    reduce_scatter x1, waiting for transfers between devices, local(): lax.psum_scatter(head_sum, 'dev', scatter_dimension=1, tiled=True)  52.9 us
    psum x1, waiting for transfers between devices, local(): latent, squares = lax.psum((latent_part, square_part), 'dev')  47.1 us
    all_gather x1, blocking collectives, local(): lax.all_gather(query_local, 'dev', axis=1, tiled=True)  30.8 us
    psum x1, blocking collectives, local(): latent, squares = lax.psum((latent_part, square_part), 'dev')  23.2 us
    psum x1, blocking collectives, local(): row_squares = lax.psum(jnp.sum(residual * residual, axis=1), 'dev')  19.5 us
  transfers between devices with their start and end apart: 4, of which 4 were waited for; matrix products, arithmetic and copies ran while one was open for 0% of the time, Pallas kernels for 0%

commit v1 on v0

v1 whole, which is shorter than its diff:
```python
import functools
import math

import jax
import jax.numpy as jnp
from jax import lax
from jax.experimental import pallas as pl
from jax.experimental.pallas import tpu as pltpu
from jax.sharding import PartitionSpec as P

D = 7168
H = 64
HD = 256
QR = 2048
LATENT = QR + 2 * HD
LANES = 128
STATS = 16

EPS = 1e-05
NEG = -1e30

FAR, CORE, DEV = "far", "core", "dev"
POOL = (FAR, CORE)
F32, BF16 = jnp.float32, jnp.bfloat16
MIB = 1 << 20
VMEM = pl.BlockSpec(memory_space=pltpu.VMEM)
HBM = pl.BlockSpec(memory_space=pltpu.MemorySpace.HBM)


def dot(left, right, left_dim=1, right_dim=0):
    return lax.dot_general(
        left,
        right,
        (((left_dim,), (right_dim,)), ((), ())),
        preferred_element_type=F32,
    )


def whole(shape):
    return pl.BlockSpec(shape, lambda *_: (0,) * len(shape))


def params(mib):
    return pltpu.CompilerParams(vmem_limit_bytes=mib * MIB)


def streamed(weight):
    return pltpu.with_memory_space_constraint(weight, pltpu.MemorySpace.HBM)


def cost(flops, moved):
    return pl.CostEstimate(flops=flops, bytes_accessed=moved, transcendentals=0)


def started(source, target, sems, pieces, axis):
    width = source.shape[axis] // pieces
    copies = []
    for piece in range(pieces):
        span = pl.ds(piece * width, width)
        at = (slice(None),) * axis + (span,)
        copy = pltpu.make_async_copy(source.at[at], target.at[at], sems.at[piece])
        copy.start()
        copies.append(copy)
    return copies


def ahead_kernel(count, *refs):
    sources, targets = refs[1 : 1 + count], refs[1 + count : 1 + 2 * count]
    token_ref, sems = refs[-2:]
    copies = []
    for index, (source, target) in enumerate(zip(sources, targets)):
        copies.append(pltpu.make_async_copy(source.at[...], target, sems.at[index]))
        copies[-1].start()
    token_ref[...] = jnp.zeros_like(token_ref)
    for copy in copies:
        copy.wait()


def ahead(beside, weights):
    count = len(weights)
    shapes = [w.shape for w in weights]
    *copied, token = pl.pallas_call(
        functools.partial(ahead_kernel, count),
        in_specs=[pl.BlockSpec(memory_space=pl.ANY)] + [HBM] * count,
        out_specs=[VMEM] * (count + 1),
        out_shape=[pltpu.VMEM(shape, BF16) for shape in shapes]
        + [jax.ShapeDtypeStruct((8, LANES), F32)],
        scratch_shapes=[pltpu.SemaphoreType.DMA((count,))],
        compiler_params=params(1),
        cost_estimate=cost(0, sum(2 * math.prod(shape) for shape in shapes)),
    )(beside, *[streamed(w) for w in weights])
    return copied, token


def part_ahead(beside, weight, part, parts, height, held):
    def kernel(*refs):
        source, (target, token_ref, sem) = refs[1], refs[-3:]
        rows = pl.ds(part * height, height)
        copy = pltpu.make_async_copy(source.at[rows], target.at[rows], sem)
        copy.start()
        token_ref[...] = jnp.zeros_like(token_ref)
        copy.wait()

    buffers = [] if held is None else [held]
    return pl.pallas_call(
        kernel,
        in_specs=[pl.BlockSpec(memory_space=pl.ANY), HBM] + [VMEM] * len(buffers),
        out_specs=[VMEM] * 2,
        out_shape=[
            pltpu.VMEM((parts * height, weight.shape[1]), BF16),
            jax.ShapeDtypeStruct((8, LANES), F32),
        ],
        scratch_shapes=[pltpu.SemaphoreType.DMA],
        input_output_aliases={2: 0} if buffers else {},
        compiler_params=params(1),
        cost_estimate=cost(0, 2 * height * weight.shape[1]),
    )(beside, streamed(weight), *buffers)


def joined(left, right, token, add):
    def kernel(left_ref, right_ref, token_ref, out_ref):
        if add:
            out_ref[...] = left_ref[...] + right_ref[...]
        else:
            both = [left_ref[...].astype(F32), right_ref[...].astype(F32)]
            out_ref[...] = jnp.concatenate(both, axis=0).astype(out_ref.dtype)

    rows, cols = left.shape
    return pl.pallas_call(
        kernel,
        in_specs=[VMEM] * 3,
        out_specs=VMEM,
        out_shape=jax.ShapeDtypeStruct((rows if add else 2 * rows, cols), left.dtype),
        compiler_params=params(2),
        cost_estimate=cost(0, 3 * rows * cols * left.dtype.itemsize),
    )(left, right, token)


def query_kernel(left_ref, right_ref, token_ref, gain_ref, w_ref, query_ref, fresh_ref, wide_ref):
    sums_ref = left_ref[...] + right_ref[...]
    rows = sums_ref.shape[0]
    out = w_ref.shape[1]
    width = min(512, out)
    heads = query_ref.shape[0] // rows
    factor = lax.rsqrt(sums_ref[:, LATENT : LATENT + 1] / D + EPS)
    query_latent = sums_ref[:, :QR] * factor
    mean = jnp.sum(query_latent * query_latent, axis=1, keepdims=True) / QR
    normed = (query_latent * lax.rsqrt(mean + EPS) * gain_ref[...]).astype(BF16)
    fresh = sums_ref[:, QR:LATENT] * factor
    fresh_ref[...] = fresh.astype(BF16).astype(F32)
    for step in range(out // width):
        query = dot(normed, w_ref[:, step * width : (step + 1) * width])
        for part in range(width // HD):
            head = step * (width // HD) + part
            for row in range(rows):
                wide_ref[row * heads + head : row * heads + head + 1, :] = query[
                    row : row + 1, part * HD : (part + 1) * HD
                ]
    query_ref[...] = wide_ref[...].astype(BF16)


def queries(left, right, token, gain, w):
    rows = left.shape[0]
    out = w.shape[1]
    heads = out // HD
    return pl.pallas_call(
        query_kernel,
        in_specs=[VMEM] * 5,
        out_specs=[VMEM] * 2,
        out_shape=[
            jax.ShapeDtypeStruct((rows * heads, HD), BF16),
            jax.ShapeDtypeStruct((rows, 2 * HD), F32),
        ],
        scratch_shapes=[pltpu.VMEM((rows * heads, HD), F32)],
        compiler_params=params(2),
        cost_estimate=cost(2 * rows * QR * out, 2 * QR * out),
    )(left, right, token, gain.reshape(1, QR), w)


def attend_kernel(codes, place_ref, lengths_ref, token_ref, *refs):
    n_dev = len(codes)
    pieces, refs = refs[:-6], refs[-6:]
    keys_ref, values_ref, out_ref, wide_ref, parts_ref, weights_ref = refs
    rows, local_pos = keys_ref.shape[:2]
    heads = H // n_dev
    me = place_ref[0]
    at = 0
    for piece in pieces:
        size = piece.shape[0]
        wide_ref[at : at + size, :] = piece[...].astype(F32)
        at += size
    lane = lax.broadcasted_iota(jnp.int32, (H, LANES), 1)
    columns = lax.broadcasted_iota(jnp.int32, (H, local_pos), 1) + me * local_pos
    stats = jnp.zeros((H, LANES), F32)
    for row in range(rows):
        query = jnp.concatenate(
            [
                wide_ref[(g * rows + row) * heads : (g * rows + row + 1) * heads, :]
                for g in range(n_dev)
            ],
            axis=0,
        ).astype(BF16)
        scores = dot(query, keys_ref[row], 1, 1) * (1.0 / math.sqrt(HD))
        valid = columns < lengths_ref[row]
        masked = jnp.where(valid, scores, NEG)
        top = jnp.max(masked, axis=1, keepdims=True)
        weights = jnp.where(valid, jnp.exp(masked - top), 0.0)
        mass = jnp.sum(weights, axis=1, keepdims=True)
        weights_ref[row] = weights.astype(BF16)
        stats = jnp.where(lane == row, top, stats)
        stats = jnp.where(lane == rows + row, mass, stats)
    for row in range(rows):
        weighted = dot(weights_ref[row], values_ref[row])
        for g in range(n_dev):
            parts_ref[me ^ codes[g], row * heads : (row + 1) * heads, :] = weighted[
                g * heads : (g + 1) * heads, :
            ]
    high = stats.astype(BF16).astype(F32)
    rest = stats - high
    middle = rest.astype(BF16).astype(F32)
    low = rest - middle
    at = rows * heads
    parts_ref[:, at:, :] = jnp.zeros((n_dev, STATS, HD), F32)
    for g in range(n_dev):
        span = slice(g * heads, (g + 1) * heads)
        parts_ref[me ^ codes[g], at : at + heads, :LANES] = high[span]
        parts_ref[me ^ codes[g], at : at + heads, LANES:] = middle[span]
        parts_ref[me ^ codes[g], at + 8 : at + 8 + heads, :LANES] = low[span]
    out_ref[...] = parts_ref[...].astype(BF16)


def attend(codes, place, lengths, token, pieces, keys, values):
    rows, local_pos = keys.shape[:2]
    n_dev = len(codes)
    height = rows * H // n_dev + STATS
    smem = pl.BlockSpec(memory_space=pltpu.SMEM)
    return pl.pallas_call(
        functools.partial(attend_kernel, codes),
        in_specs=[smem, smem] + [VMEM] * (3 + len(pieces)),
        out_specs=VMEM,
        out_shape=jax.ShapeDtypeStruct((n_dev, height, HD), BF16),
        scratch_shapes=[
            pltpu.VMEM((rows * H, HD), F32),
            pltpu.VMEM((n_dev, height, HD), F32),
            pltpu.VMEM((rows, H, local_pos), BF16),
        ],
        compiler_params=params(5),
        cost_estimate=cost(4 * rows * H * local_pos * HD, 4 * rows * local_pos * HD),
    )(place, lengths, token, *pieces, keys, values)


def project_kernel(
    sent_ref, query_ref, fresh_ref, held_ref, w_hbm, out_ref, attended_ref, parts_ref, w_ref, sems
):
    n_dev = sent_ref.shape[0]
    held = held_ref.shape[0]
    copies = started(w_hbm.at[held : held + w_ref.shape[0]], w_ref, sems, out_ref.shape[0], 1)
    rows = fresh_ref.shape[0]
    heads = H // n_dev

    query = query_ref[...].astype(F32)
    parts_ref[...] = sent_ref[...].astype(F32)
    at = rows * heads
    stats = [
        parts_ref[d, at : at + heads, :LANES]
        + parts_ref[d, at : at + heads, LANES:]
        + parts_ref[d, at + 8 : at + 8 + heads, :LANES]
        for d in range(n_dev)
    ]
    for row in range(rows):
        span = slice(row * heads, (row + 1) * heads)
        key = fresh_ref[row : row + 1, :HD]
        value = fresh_ref[row : row + 1, HD:]
        score = jnp.sum(query[span] * key, axis=1, keepdims=True) * (1.0 / math.sqrt(HD))
        highest = score
        for d in range(n_dev):
            highest = jnp.maximum(highest, stats[d][:, row : row + 1])
        weight = jnp.exp(score - highest)
        mass = weight
        total = weight.astype(BF16).astype(F32) * value
        for d in range(n_dev):
            factor = jnp.exp(stats[d][:, row : row + 1] - highest)
            mass = mass + factor * stats[d][:, rows + row : rows + row + 1]
            total = total + factor * parts_ref[d, span, :]
        attended = total / mass
        for head in range(heads):
            attended_ref[row : row + 1, head * HD : (head + 1) * HD] = attended[
                head : head + 1, :
            ]

    width = out_ref.shape[2]
    attended = attended_ref[...].astype(BF16)
    for step, copy in enumerate(copies):
        columns = slice(step * width, (step + 1) * width)
        first = dot(attended[:, :held], held_ref[:, columns])
        copy.wait()
        out_ref[step] = first + dot(attended[:, held:], w_ref[:, columns])


def project(parts, query, fresh, held, w):
    rows = fresh.shape[0]
    depth = w.shape[0]
    width = D // 8
    return pl.pallas_call(
        project_kernel,
        in_specs=[VMEM] * 4 + [HBM],
        out_specs=VMEM,
        out_shape=jax.ShapeDtypeStruct((D // width, rows, width), F32),
        scratch_shapes=[
            pltpu.VMEM((rows, depth), F32),
            pltpu.VMEM(parts.shape, F32),
            pltpu.VMEM((depth - held.shape[0], D), BF16),
            pltpu.SemaphoreType.DMA((D // width,)),
        ],
        compiler_params=params(20),
        cost_estimate=cost(2 * rows * depth * D, 2 * depth * D),
    )(parts, query, fresh, held, streamed(w))


def ffn_kernel(*refs):
    pieces, refs = refs[:-6], refs[-6:]
    token_ref, gate_ref, up_ref, down_ref, out_ref, act_ref = refs
    rows = jnp.concatenate([piece[...] for piece in pieces], axis=0)
    units = gate_ref.shape[0]
    block = 144
    for step in range(units // block):
        span = slice(step * block, (step + 1) * block)
        gate = dot(gate_ref[span, :], rows, 1, 1)
        up = dot(up_ref[span, :], rows, 1, 1)
        act_ref[span, :] = gate / (1.0 + jnp.exp(-gate)) * up
    activated = act_ref[...].astype(BF16)
    width = down_ref.shape[1] // 8

    @pl.loop(0, 8)
    def _(step):
        columns = pl.ds(pl.multiple_of(step * width, width), width)
        out_ref[:, columns] = dot(activated, down_ref[:, columns], 0, 0)


def ffn(pieces, token, gate_t, up_t, down):
    rows = sum(piece.shape[0] for piece in pieces)
    units, depth = gate_t.shape
    return pl.pallas_call(
        ffn_kernel,
        in_specs=[VMEM] * (len(pieces) + 4),
        out_specs=VMEM,
        out_shape=jax.ShapeDtypeStruct((rows, depth), F32),
        scratch_shapes=[pltpu.VMEM((units, rows), F32)],
        compiler_params=params(6),
        cost_estimate=cost(6 * rows * units * depth, 6 * units * depth),
    )(*pieces, token, gate_t, up_t, down)


def swapped(value, axis, bit):
    size = lax.axis_size(axis)
    return lax.ppermute(value, axis, [(i, i ^ bit) for i in range(size)])


def gathered(value, axis):
    size = lax.axis_size(axis)
    return lax.all_to_all(jnp.broadcast_to(value[None], (size, *value.shape)), axis, 0, 0)


def local(
    hidden_in,
    in_gain,
    w_latent,
    q_gain,
    w_query,
    cache_keys,
    cache_values,
    lengths,
    w_out,
    post_gain,
    w_gate,
    w_up,
    w_down,
):
    n_dev = lax.axis_size(DEV)
    place = lax.axis_index(DEV).astype(jnp.int32).reshape(1)
    rows, cols = hidden_in.shape
    hidden_f = hidden_in.astype(F32)

    scaled = (hidden_f * in_gain[None, :]).astype(BF16)
    squares = jnp.sum(hidden_f * hidden_f, axis=1, keepdims=True)
    sums = jnp.concatenate(
        [dot(scaled, w_latent), jnp.broadcast_to(squares, (rows, LANES))], axis=1
    )
    copied = {}

    def copy_query(value):
        (copied["query"],), token = ahead(value, [w_query])
        return token

    def copy_out(part, value):
        height = w_out.shape[0] // 8
        copied["out"], token = part_ahead(value, w_out, part, 4, height, copied.get("out"))
        return token

    def copy_caches(value):
        copied["caches"], token = ahead(value, [cache_keys, cache_values])
        return token

    jobs = [copy_query] + [functools.partial(copy_out, part) for part in range(4)]
    jobs = jobs + [copy_caches]

    def exchanged(value, bit):
        arrived = swapped(value, DEV, bit)
        return arrived, jobs.pop(0)(value) if jobs else jnp.zeros((8, LANES), F32)

    bit = 1
    while bit < n_dev:
        arrived, token = exchanged(sums, bit)
        bit *= 2
        if bit < n_dev:
            sums = joined(sums, arrived, token, True)
    query, fresh = queries(sums, arrived, token, q_gain, copied["query"])

    held, codes = query, [0]
    bit = n_dev // 2
    while bit:
        arrived, token = exchanged(held, bit)
        codes = codes + [code ^ bit for code in codes]
        bit //= 2
        if bit:
            held = joined(held, arrived, token, False)
    parts = attend(codes, place, lengths, token, [held, arrived], *copied["caches"])
    parts = lax.all_to_all(parts, DEV, 0, 0)
    head_sum = project(parts, query, fresh, copied["out"], w_out)
    if cols != head_sum.shape[2]:
        head_sum = head_sum.transpose(1, 0, 2).reshape(rows, n_dev, cols).transpose(1, 0, 2)
    head_sum = lax.all_to_all(head_sum.astype(BF16), DEV, 0, 0)
    residual = hidden_f + jnp.sum(head_sum.astype(F32), axis=0)

    squares = jnp.sum(residual * residual, axis=1)
    packed = jnp.concatenate(
        [residual * post_gain[None, :], jnp.broadcast_to(squares[:, None], (rows, LANES))],
        axis=1,
    )
    packed = gathered(packed, DEV)
    factor = lax.rsqrt(jnp.sum(packed[:, :, cols], axis=0) / D + EPS)
    normed = (packed[:, :, :cols] * factor[None, :, None]).astype(BF16)
    normed = normed.transpose(1, 0, 2).reshape(rows, n_dev * cols)
    n_far = lax.axis_size(FAR)
    arrived = swapped(normed, FAR, 1)
    (gate_t, up_t), token = ahead(normed, [w_gate.T, w_up.T])
    mine = joined(normed, arrived, token, False)
    other = swapped(mine, CORE, 1)
    (down,), token = ahead(mine, [w_down])
    ffn_term = ffn([mine, other], token, gate_t, up_t, down)

    half = n_far * rows
    ffn_term = ffn_term[:half] + swapped(ffn_term[half:], CORE, 1)
    ffn_term = ffn_term.reshape(n_far, rows, n_dev, cols)
    far = lax.axis_index(FAR)
    ffn_term = jnp.stack([lax.dynamic_index_in_dim(ffn_term, far ^ f, 0, False) for f in range(n_far)])
    ffn_term = ffn_term.transpose(0, 2, 1, 3).reshape(n_far * n_dev, rows, cols)
    ffn_term = lax.all_to_all(ffn_term.astype(BF16), (FAR, DEV), 0, 0)
    ffn_out = jnp.sum(ffn_term.astype(F32), axis=0)
    return residual + ffn_out


def solution(mesh):
    sizes = mesh.devices.shape
    mesh = jax.sharding.Mesh(
        mesh.devices.reshape(sizes[0] // 2, 2, sizes[1]), (FAR, CORE, DEV)
    )
    placed = (
        P(POOL, DEV),
        P(DEV),
        P(DEV, None),
        P(),
        P(None, DEV),
        P(POOL, DEV, None),
        P(POOL, DEV, None),
        P(POOL),
        P(DEV, None),
        P(DEV),
        P(None, (*POOL, DEV)),
        P(None, (*POOL, DEV)),
        P((*POOL, DEV), None),
    )
    return jax.shard_map(
        local, mesh=mesh, in_specs=placed, out_specs=P(POOL, DEV), check_vma=False
    )
```

time: 513 us -> 126 us (0.25)
  waiting for transfers between devices: 240 us -> 4.66 us
  blocking collectives: 202 us -> 48.1 us
  Pallas kernels: 0 us -> 41.3 us
  matrix products: 36.9 us -> 3.03 us
  starting transfers between devices: 0.13 us -> 15.8 us
  other arithmetic: 15.6 us -> 1.96 us
  between operations: 13.3 us -> 0.24 us
  local copies, waits for them, and re-layouts: 4.6 us -> 10.6 us
    all_gather x4 -> x0, blocking collectives: 159 us -> none  [the longest x1 66.3 us: local(): lax.all_gather(normed, ('pool', 'dev'), axis=0, tiled=True)]
    unnamed x5 -> x0, waiting for transfers between devices: 129 us -> none
    reduce_scatter x1 -> x0, waiting for transfers between devices: 52.9 us -> none  [local(): lax.psum_scatter(head_sum, 'dev', scatter_dimension=1, tiled=True)]
    all_to_all x0 -> x4, blocking collectives: none -> 48.1 us  [the longest x1 13.3 us: local(): parts = lax.all_to_all(parts, DEV, 0, 0)]
    psum x1 -> x0, waiting for transfers between devices: 47.1 us -> none  [local(): latent, squares = lax.psum((latent_part, square_part), 'dev')]
    psum x2 -> x0, blocking collectives: 42.6 us -> none  [the longest x1 23.2 us: local(): latent, squares = lax.psum((latent_part, square_part), 'dev')]
    pallas_call x0 -> x17, Pallas kernels: none -> 41.3 us  [the longest x4 14.7 us: ahead(): pl.pallas_call(functools.partial(ahead_kernel, count), in_specs=[pl.Block...]
    dot_general x8 -> x1, matrix products: 36.9 us -> 3.03 us  [dot(): lax.dot_general(left, right, (((left_dim,), (right_dim,)), ((), ())), pre...]
  transfers between devices with their start and end apart: 4 -> 9, of which waited for: 4 -> 5; matrix products, arithmetic and copies ran while one was open for 0% -> 0% of each run, Pallas kernels for 0% -> 18%
where the time goes in v1:
time: 126 us
  blocking collectives  48.1 us (38%)
  Pallas kernels  41.3 us (33%)
  starting transfers between devices  15.8 us (13%)
  local copies, waits for them, and re-layouts  10.6 us (8%)
  waiting for transfers between devices  4.66 us (4%)
  matrix products  3.03 us (2%)
  other arithmetic  1.96 us (2%)
    ppermute x9, starting transfers between devices, swapped(): return lax.ppermute(value, axis, [(i, i ^ bit) for i in range(size)])  15.8 us
    pallas_call x4, Pallas kernels, ahead(): pl.pallas_call(functools.partial(ahead_kernel, count), in_specs=[pl.Block...  14.7 us
    all_to_all x1, blocking collectives, local(): parts = lax.all_to_all(parts, DEV, 0, 0)  13.3 us
    all_to_all x1, blocking collectives, local(): ffn_term = lax.all_to_all(ffn_term.astype(BF16), (FAR, DEV), 0, 0)  12.7 us
    all_to_all x1, blocking collectives, gathered(): lax.all_to_all(jnp.broadcast_to(value[None], (size, *value.shape)), axis,...  11.8 us
    unnamed x12, local copies, waits for them, and re-layouts  10.4 us
    all_to_all x1, blocking collectives, local(): head_sum = lax.all_to_all(head_sum.astype(BF16), DEV, 0, 0)  10.3 us
    pallas_call x1, Pallas kernels, project(): pl.pallas_call(project_kernel, in_specs=[VMEM] * 4 + [HBM], out_specs=VME...  8.22 us
  transfers between devices with their start and end apart: 9, of which 5 were waited for; matrix products, arithmetic and copies ran while one was open for 0% of the time, Pallas kernels for 18%

profile of v1, /device:TPU:0, one launch (start us, length us, event | category | flops | bytes accessed | tf_op | source)
XLA Modules:
  0.0 125.6 jit_solution(17501471999256379185)
XLA Ops:
  0.0 0.8 fusion.2
  0.8 3.0 %fusion.3 = f32[8,2560]{1,0:T(8,128)S(1)} fusion(bf16[896,2560]{1,0:T(8,128)(2,1)} %param.15, bf16[8,896]{1,0:T(8,128)(2,1)} %param.13, f32[896]{0:T(1024)} %param.14), kind=kOutput, calls=%fused_computation.17 | convolution fusion | flops 36721664 | bytes 4687360 | tf_op jit(solution)/shard_map/dot_general | solution.py:31
  3.9 0.1 broadcast_in_dim.6
  3.9 3.0 %collective-permute-start = (f32[8,2688]{1,0:T(8,128)S(1)}, f32[8,2688]{1,0:T(8,128)S(1)}, u32[]{:S(2)}, u32[]{:S(2)}) collective-permute-start(f32[8,2688]{1,0:T(8,128)S(1)} %pad_maximum_fusion.1.refs_0_.left_ref), channel_id=1, source_target_pairs={{0,1},{1,0},{2,3},{3,2},{4,5},{5,4},{6,7},{7,6},{8,9},{9,8},{10,11... | collective-permute-start | bytes 258056 | tf_op jit(solution)/shard_map/ppermute | solution.py:356
  6.9 3.4 %shard_map.127 = (bf16[2048,2048]{1,0:T(8,128)(2,1)S(1)}, f32[8,128]{1,0:T(8,128)S(1)}) custom-call(f32[8,2688]{1,0:T(8,128)S(1)} %pad_maximum_fusion.1.refs_0_.left_ref, bf16[2048,2048]{1,0:T(8,128)(2,1)} %refs_1_.7), custom_call_target="tpu_custom_call" | custom-call | bytes 8388608 | tf_op jit(solution)/shard_map/pallas_call | solution.py:82
  10.3 0.0 collective-permute-done.right_ref
  10.4 1.6 %collective-permute-start.1 = (f32[8,2688]{1,0:T(8,128)S(1)}, f32[8,2688]{1,0:T(8,128)S(1)}, u32[]{:S(2)}, u32[]{:S(2)}) collective-permute-start(f32[8,2688]{1,0:T(8,128)S(1)} %shard_map.128.refs_0_.left_ref), channel_id=1, source_target_pairs={{0,2},{1,3},{2,0},{3,1},{4,6},{5,7},{6,4},{7,5},{8,10},{9,11},{10,... | collective-permute-start | bytes 258056 | tf_op jit(solution)/shard_map/ppermute | solution.py:356
  12.0 2.0 %shard_map.129 = (bf16[1024,7168]{1,0:T(8,128)(2,1)S(1)}, f32[8,128]{1,0:T(8,128)S(1)}) custom-call(f32[8,2688]{1,0:T(8,128)S(1)} %shard_map.128.refs_0_.left_ref, bf16[2048,7168]{1,0:T(8,128)(2,1)} %w_hbm.1), custom_call_target="tpu_custom_call" | custom-call | bytes 3670016 | tf_op jit(solution)/shard_map/pallas_call | solution.py:105
  14.1 0.9 collective-permute-done.1.right_ref
  14.9 2.7 %collective-permute-start.2 = (f32[8,2688]{1,0:T(8,128)S(1)}, f32[8,2688]{1,0:T(8,128)S(1)}, u32[]{:S(2)}, u32[]{:S(2)}) collective-permute-start(f32[8,2688]{1,0:T(8,128)S(1)} %shard_map.130.refs_0_.left_ref), channel_id=1, source_target_pairs={{0,4},{1,5},{2,6},{3,7},{4,0},{5,1},{6,2},{7,3},{8,12},{9,13},{10,... | collective-permute-start | bytes 258056 | tf_op jit(solution)/shard_map/ppermute | solution.py:356
  17.6 0.0 copy-start.2
  17.6 2.1 %shard_map.131 = (bf16[1024,7168]{1,0:T(8,128)(2,1)S(1)}, f32[8,128]{1,0:T(8,128)S(1)}) custom-call(f32[8,2688]{1,0:T(8,128)S(1)} %shard_map.130.refs_0_.left_ref, bf16[2048,7168]{1,0:T(8,128)(2,1)} %w_hbm.1, bf16[1024,7168]{1,0:T(8,128)(2,1)S(1)} %get-tuple-element.27.refs_2_), custom_call_target="tpu_custom_call", output_to_operand_aliasing={{0}: (2, {})} | custom-call | bytes 3670016 | tf_op jit(solution)/shard_map/pallas_call | solution.py:105
  19.7 0.7 collective-permute-done.2.right_ref
  20.4 0.0 copy-done.2
  20.4 1.4 %shard_map.132 = (bf16[64,256]{1,0:T(8,128)(2,1)S(1)}, f32[8,512]{1,0:T(8,128)S(1)}) custom-call(f32[8,2688]{1,0:T(8,128)S(1)} %shard_map.130.refs_0_.left_ref, f32[8,2688]{1,0:T(8,128)S(1)} %collective-permute-done.2.right_ref, f32[8,128]{1,0:T(8,128)S(1)} %get-tuple-element.28.token_ref, f32[1,2048]{1,0:T(1,128)S(1)} %bitcast.15, ...), custom_call_target="tpu_custom_call" | custom-call | flops 67108864 | bytes 8388608 | tf_op jit(solution)/shard_map/pallas_call | solution.py:166
  21.8 2.7 %collective-permute-start.3 = (bf16[64,256]{1,0:T(8,128)(2,1)S(1)}, bf16[64,256]{1,0:T(8,128)(2,1)S(1)}, u32[]{:S(2)}, u32[]{:S(2)}) collective-permute-start(bf16[64,256]{1,0:T(8,128)(2,1)S(1)} %get-tuple-element.30.refs_0_.left_ref.query_ref), channel_id=1, source_target_pairs={{0,4},{1,5},{2,6},{3,7},{4,0},{5,1},{6,2},{7,3},{8,12},{9,13},{10,... | collective-permute-start | bytes 98312 | tf_op jit(solution)/shard_map/ppermute | solution.py:356
  24.5 2.0 %shard_map.133 = (bf16[1024,7168]{1,0:T(8,128)(2,1)S(1)}, f32[8,128]{1,0:T(8,128)S(1)}) custom-call(bf16[64,256]{1,0:T(8,128)(2,1)S(1)} %get-tuple-element.30.refs_0_.left_ref.query_ref, bf16[2048,7168]{1,0:T(8,128)(2,1)} %w_hbm.1, bf16[1024,7168]{1,0:T(8,128)(2,1)S(1)} %get-tuple-element.31.refs_2_), custom_call_target="tpu_custom_call", output_to_operand_aliasing={{0}: (2, {})} | custom-call | bytes 3670016 | tf_op jit(solution)/shard_map/pallas_call | solution.py:105
  26.6 0.1 collective-permute-done.3.right_ref
  26.6 2.3 %collective-permute-start.4 = (bf16[128,256]{1,0:T(8,128)(2,1)S(1)}, bf16[128,256]{1,0:T(8,128)(2,1)S(1)}, u32[]{:S(2)}, u32[]{:S(2)}) collective-permute-start(bf16[128,256]{1,0:T(8,128)(2,1)S(1)} %shard_map.134.refs_0_.left_ref), channel_id=1, source_target_pairs={{0,2},{1,3},{2,0},{3,1},{4,6},{5,7},{6,4},{7,5},{8,10},{9,11},{10,... | collective-permute-start | bytes 196616 | tf_op jit(solution)/shard_map/ppermute | solution.py:356
  28.9 0.0 copy-start.3
  28.9 2.1 %shard_map.135 = (bf16[1024,7168]{1,0:T(8,128)(2,1)S(1)}, f32[8,128]{1,0:T(8,128)S(1)}) custom-call(bf16[128,256]{1,0:T(8,128)(2,1)S(1)} %shard_map.134.refs_0_.left_ref, bf16[2048,7168]{1,0:T(8,128)(2,1)} %w_hbm.1, bf16[1024,7168]{1,0:T(8,128)(2,1)S(1)} %get-tuple-element.33.refs_2_), custom_call_target="tpu_custom_call", output_to_operand_aliasing={{0}: (2, {})} | custom-call | bytes 3670016 | tf_op jit(solution)/shard_map/pallas_call | solution.py:105
  31.0 0.0 copy-start
  31.0 5.2 %copy-done = bf16[1024,7168]{1,0:T(8,128)(2,1)} copy-done((bf16[1024,7168]{1,0:T(8,128)(2,1)}, bf16[1024,7168]{1,0:T(8,128)(2,1)S(1)}, u32[]{:S(2)}) %copy-start) | copy-done | bytes 14680088
  36.2 0.0 collective-permute-done.4.right_ref
  36.2 1.2 collective-permute-start.5
  37.5 2.2 %shard_map.137 = (bf16[8,512,256]{2,1,0:T(8,128)(2,1)S(1)}, bf16[8,512,256]{2,1,0:T(8,128)(2,1)S(1)}, f32[8,128]{1,0:T(8,128)S(1)}) custom-call(bf16[256,256]{1,0:T(8,128)(2,1)S(1)} %shard_map.136.refs_0_, bf16[8,512,256]{2,1,0:T(8,128)(2,1)} %refs_1_.12, bf16[8,512,256]{2,1,0:T(8,128)(2,1)} %refs_2_.1), custom_call_target="tpu_custom_call" | custom-call | bytes 4194304 | tf_op jit(solution)/shard_map/pallas_call | solution.py:82
  39.7 1.5 %collective-permute-done.5.refs_1_ = bf16[256,256]{1,0:T(8,128)(2,1)S(1)} collective-permute-done((bf16[256,256]{1,0:T(8,128)(2,1)S(1)}, bf16[256,256]{1,0:T(8,128)(2,1)S(1)}, u32[]{:S(2)}, u32[]{:S(2)}) %collective-permute-start.5) | collective-permute-done | bytes 131104 | tf_op jit(solution)/shard_map/ppermute | solution.py:356
  41.3 0.0 copy-done.3
  41.3 1.8 %shard_map.138 = bf16[8,80,256]{2,1,0:T(8,128)(2,1)S(1)} custom-call(s32[1]{0:T(128)} %bitcast.place_ref, s32[8]{0:T(128)S(1)} %copy-done.3, f32[8,128]{1,0:T(8,128)S(1)} %get-tuple-element.35.token_ref, bf16[256,256]{1,0:T(8,128)(2,1)S(1)} %shard_map.136.refs_0_, bf16[256,256]{1,0:T(8,128)(2,1)S(1)} %collective-permute-done.5.refs_1_, ...), custom_call_target="tpu_custom_call" | custom-call | flops 268435456 | bytes 4194304 | tf_op jit(solution)/shard_map/pallas_call | solution.py:237
  43.0 13.3 %all_to_all.20.sent_ref = bf16[8,80,256]{2,1,0:T(8,128)(2,1)S(1)} all-to-all(bf16[8,80,256]{2,1,0:T(8,128)(2,1)S(1)} %shard_map.138), channel_id=1, replica_groups=mesh['far'=2,'core'=2,'dev'=8] {'dev'}, dimensions={0} | all-to-all | bytes 655360 | tf_op jit(solution)/shard_map/all_to_all | solution.py:428
  56.3 0.0 copy-start.1
  56.3 5.2 %copy-done.1 = bf16[1024,7168]{1,0:T(8,128)(2,1)S(1)} copy-done((bf16[1024,7168]{1,0:T(8,128)(2,1)S(1)}, bf16[1024,7168]{1,0:T(8,128)(2,1)}, u32[]{:S(2)}) %copy-start.1) | copy-done | bytes 14680088
  61.5 0.0 copy-start.4
  61.5 0.0 copy-start.5
  61.5 8.2 %shard_map.139 = f32[8,8,896]{2,1,0:T(8,128)S(1)} custom-call(bf16[8,80,256]{2,1,0:T(8,128)(2,1)S(1)} %all_to_all.20.sent_ref, bf16[64,256]{1,0:T(8,128)(2,1)S(1)} %get-tuple-element.30.refs_0_.left_ref.query_ref, f32[8,512]{1,0:T(8,128)S(1)} %get-tuple-element.38.fresh_ref, bf16[1024,7168]{1,0:T(8,128)(2,1)S(1)} %copy-done.1, bf16[2048,7168]{1,0:T(8,128)(2,1)} %w_hbm.1), custom_call_target="tpu_custom_call" | custom-call | flops 234881024 | bytes 29360128 | tf_op jit(solution)/shard_map/pallas_call | solution.py:304
  69.7 10.3 %all_to_all.21 = bf16[8,8,896]{2,1,0:T(8,128)(2,1)S(1)} all-to-all(bf16[8,8,896]{2,1,0:T(8,128)(2,1)S(1)} %convert_element_type.27), channel_id=1, replica_groups=mesh['far'=2,'core'=2,'dev'=8] {'dev'}, dimensions={0} | all-to-all | bytes 229376 | tf_op jit(solution)/shard_map/all_to_all | solution.py:432
  80.1 0.0 copy-done.4
  80.1 0.0 copy-done.5
  80.1 0.1 broadcast_multiply_fusion
  80.2 0.1 broadcast_in_dim.7
  80.4 11.8 %all_to_all.22 = f32[8,8,1024]{2,1,0:T(8,128)S(1)} all-to-all(f32[8,8,1024]{2,1,0:T(8,128)S(1)} %broadcast_in_dim.8), channel_id=1, replica_groups=mesh['far'=2,'core'=2,'dev'=8] {'dev'}, dimensions={0} | all-to-all | bytes 524288 | tf_op jit(solution)/shard_map/all_to_all | solution.py:361
  92.1 0.1 slice_reduce_fusion
  92.3 0.1 fusion
  92.4 1.5 %collective-permute-start.6 = (bf16[8,7168]{1,0:T(8,128)(2,1)S(1)}, bf16[8,7168]{1,0:T(8,128)(2,1)S(1)}, u32[]{:S(2)}, u32[]{:S(2)}) collective-permute-start(bf16[8,7168]{1,0:T(8,128)(2,1)S(1)} %bitcast.12), channel_id=1, source_target_pairs={{0,16},{16,0},{1,17},{17,1},{2,18},{18,2},{3,19},{19,3},{4,20},{20... | collective-permute-start | bytes 344072 | tf_op jit(solution)/shard_map/ppermute | solution.py:356
  93.9 5.7 %shard_map.140 = (bf16[576,7168]{1,0:T(8,128)(2,1)S(1)}, bf16[576,7168]{1,0:T(8,128)(2,1)S(1)}, f32[8,128]{1,0:T(8,128)S(1)}) custom-call(bf16[8,7168]{1,0:T(8,128)(2,1)S(1)} %bitcast.13, bf16[576,7168]{1,0:T(8,128)(2,1)} %bitcast.16, bf16[576,7168]{1,0:T(8,128)(2,1)} %bitcast.17), custom_call_target="tpu_custom_call" | custom-call | bytes 16515072 | tf_op jit(solution)/shard_map/pallas_call | solution.py:82
  99.6 0.0 collective-permute-done.6.right_ref
  99.7 0.1 collective-permute-start.7
  99.8 3.4 %shard_map.142 = (bf16[576,7168]{1,0:T(8,128)(2,1)S(1)}, f32[8,128]{1,0:T(8,128)S(1)}) custom-call(bf16[16,7168]{1,0:T(8,128)(2,1)S(1)} %shard_map.141.refs_0_, bf16[576,7168]{1,0:T(8,128)(2,1)} %refs_1_.13), custom_call_target="tpu_custom_call" | custom-call | bytes 8257536 | tf_op jit(solution)/shard_map/pallas_call | solution.py:82
  103.1 0.0 collective-permute-done.7.refs_1_
  103.1 7.0 %shard_map.143 = f32[32,7168]{1,0:T(8,128)S(1)} custom-call(bf16[16,7168]{1,0:T(8,128)(2,1)S(1)} %shard_map.141.refs_0_, bf16[16,7168]{1,0:T(8,128)(2,1)S(1)} %collective-permute-done.7.refs_1_, f32[8,128]{1,0:T(8,128)S(1)} %get-tuple-element.41.refs_2_, bf16[576,7168]{1,0:T(8,128)(2,1)S(1)} %get-tuple-element.42.refs_3_, ...), custom_call_target="tpu_custom_call" | custom-call | flops 792723456 | bytes 24772608 | tf_op jit(solution)/shard_map/pallas_call | solution.py:343
  110.2 0.6 collective-permute-start.8
  110.7 1.4 %collective-permute-done.8 = f32[16,7168]{1,0:T(8,128)S(1)} collective-permute-done((f32[16,7168]{1,0:T(8,128)S(1)}, f32[16,7168]{1,0:T(8,128)S(1)}, u32[]{:S(2)}, u32[]{:S(2)}) %collective-permute-start.8) | collective-permute-done | bytes 458784 | tf_op jit(solution)/shard_map/ppermute | solution.py:356
  112.3 12.7 %all_to_all.23 = bf16[16,8,896]{2,1,0:T(8,128)(2,1)S(1)} all-to-all(bf16[16,8,896]{2,1,0:T(8,128)(2,1)S(1)} %bitcast.18), channel_id=1, replica_groups=mesh['far'=2,'core'=2,'dev'=8] {'far','dev'}, dimensions={0} | all-to-all | bytes 458752 | tf_op jit(solution)/shard_map/all_to_all | solution.py:458
  125.0 0.6 fusion.6
  (16 shorter events, 0.3 us)
Async XLA Ops:
  3.9 6.4 %collective-permute-start = (f32[8,2688]{1,0:T(8,128)S(1)}, f32[8,2688]{1,0:T(8,128)S(1)}, u32[]{:S(2)}, u32[]{:S(2)}) collective-permute-start(f32[8,2688]{1,0:T(8,128)S(1)} %pad_maximum_fusion.1.refs_0_.left_ref), channel_id=1, source_target_pairs={{0,1},{1,0},{2,3},{3,2},{4,5},{5,4},{6,7},{7,6},{8,9},{9,8},{10,11... | collective-permute-start | bytes 258056 | tf_op jit(solution)/shard_map/ppermute | solution.py:356
  10.4 4.6 %collective-permute-start.1 = (f32[8,2688]{1,0:T(8,128)S(1)}, f32[8,2688]{1,0:T(8,128)S(1)}, u32[]{:S(2)}, u32[]{:S(2)}) collective-permute-start(f32[8,2688]{1,0:T(8,128)S(1)} %shard_map.128.refs_0_.left_ref), channel_id=1, source_target_pairs={{0,2},{1,3},{2,0},{3,1},{4,6},{5,7},{6,4},{7,5},{8,10},{9,11},{10,... | collective-permute-start | bytes 258056 | tf_op jit(solution)/shard_map/ppermute | solution.py:356
  14.9 5.4 %collective-permute-start.2 = (f32[8,2688]{1,0:T(8,128)S(1)}, f32[8,2688]{1,0:T(8,128)S(1)}, u32[]{:S(2)}, u32[]{:S(2)}) collective-permute-start(f32[8,2688]{1,0:T(8,128)S(1)} %shard_map.130.refs_0_.left_ref), channel_id=1, source_target_pairs={{0,4},{1,5},{2,6},{3,7},{4,0},{5,1},{6,2},{7,3},{8,12},{9,13},{10,... | collective-permute-start | bytes 258056 | tf_op jit(solution)/shard_map/ppermute | solution.py:356
  17.6 2.8 %copy-start.2 = (f32[2048]{0:T(1024)S(1)}, f32[2048]{0:T(1024)}, u32[]{:S(2)}) copy-start(f32[2048]{0:T(1024)} %param.16) | copy-start | bytes 24580
  21.8 4.9 %collective-permute-start.3 = (bf16[64,256]{1,0:T(8,128)(2,1)S(1)}, bf16[64,256]{1,0:T(8,128)(2,1)S(1)}, u32[]{:S(2)}, u32[]{:S(2)}) collective-permute-start(bf16[64,256]{1,0:T(8,128)(2,1)S(1)} %get-tuple-element.30.refs_0_.left_ref.query_ref), channel_id=1, source_target_pairs={{0,4},{1,5},{2,6},{3,7},{4,0},{5,1},{6,2},{7,3},{8,12},{9,13},{10,... | collective-permute-start | bytes 98312 | tf_op jit(solution)/shard_map/ppermute | solution.py:356
  26.6 9.6 %collective-permute-start.4 = (bf16[128,256]{1,0:T(8,128)(2,1)S(1)}, bf16[128,256]{1,0:T(8,128)(2,1)S(1)}, u32[]{:S(2)}, u32[]{:S(2)}) collective-permute-start(bf16[128,256]{1,0:T(8,128)(2,1)S(1)} %shard_map.134.refs_0_.left_ref), channel_id=1, source_target_pairs={{0,2},{1,3},{2,0},{3,1},{4,6},{5,7},{6,4},{7,5},{8,10},{9,11},{10,... | collective-permute-start | bytes 196616 | tf_op jit(solution)/shard_map/ppermute | solution.py:356
  28.9 12.3 %copy-start.3 = (s32[8]{0:T(128)S(1)}, s32[8]{0:T(128)}, u32[]{:S(2)}) copy-start(s32[8]{0:T(128)} %lengths_ref.1) | copy-start | bytes 100
  31.0 5.2 %copy-start = (bf16[1024,7168]{1,0:T(8,128)(2,1)}, bf16[1024,7168]{1,0:T(8,128)(2,1)S(1)}, u32[]{:S(2)}) copy-start(bf16[1024,7168]{1,0:T(8,128)(2,1)S(1)} %get-tuple-element.39.held_ref) | copy-start | bytes 44040196
  36.2 5.0 %collective-permute-start.5 = (bf16[256,256]{1,0:T(8,128)(2,1)S(1)}, bf16[256,256]{1,0:T(8,128)(2,1)S(1)}, u32[]{:S(2)}, u32[]{:S(2)}) collective-permute-start(bf16[256,256]{1,0:T(8,128)(2,1)S(1)} %shard_map.136.refs_0_), channel_id=1, source_target_pairs={{0,1},{1,0},{2,3},{3,2},{4,5},{5,4},{6,7},{7,6},{8,9},{9,8},{10,11... | collective-permute-start | bytes 393224 | tf_op jit(solution)/shard_map/ppermute | solution.py:356
  56.3 5.2 %copy-start.1 = (bf16[1024,7168]{1,0:T(8,128)(2,1)S(1)}, bf16[1024,7168]{1,0:T(8,128)(2,1)}, u32[]{:S(2)}) copy-start(bf16[1024,7168]{1,0:T(8,128)(2,1)} %copy-done) | copy-start | bytes 44040196
  61.5 18.6 %copy-start.4 = (bf16[8,896]{1,0:T(8,128)(2,1)S(1)}, bf16[8,896]{1,0:T(8,128)(2,1)}, u32[]{:S(2)}) copy-start(bf16[8,896]{1,0:T(8,128)(2,1)} %param.13) | copy-start | bytes 43012
  61.5 18.6 %copy-start.5 = (f32[896]{0:T(1024)S(1)}, f32[896]{0:T(1024)}, u32[]{:S(2)}) copy-start(f32[896]{0:T(1024)} %param.22) | copy-start | bytes 10756
  92.4 7.3 %collective-permute-start.6 = (bf16[8,7168]{1,0:T(8,128)(2,1)S(1)}, bf16[8,7168]{1,0:T(8,128)(2,1)S(1)}, u32[]{:S(2)}, u32[]{:S(2)}) collective-permute-start(bf16[8,7168]{1,0:T(8,128)(2,1)S(1)} %bitcast.12), channel_id=1, source_target_pairs={{0,16},{16,0},{1,17},{17,1},{2,18},{18,2},{3,19},{19,3},{4,20},{20... | collective-permute-start | bytes 344072 | tf_op jit(solution)/shard_map/ppermute | solution.py:356
  99.7 3.4 %collective-permute-start.7 = (bf16[16,7168]{1,0:T(8,128)(2,1)S(1)}, bf16[16,7168]{1,0:T(8,128)(2,1)S(1)}, u32[]{:S(2)}, u32[]{:S(2)}) collective-permute-start(bf16[16,7168]{1,0:T(8,128)(2,1)S(1)} %shard_map.141.refs_0_), channel_id=1, source_target_pairs={{0,8},{8,0},{1,9},{9,1},{2,10},{10,2},{3,11},{11,3},{4,12},{12,4},... | collective-permute-start | bytes 688136 | tf_op jit(solution)/shard_map/ppermute | solution.py:356
  110.2 2.0 %collective-permute-start.8 = (f32[16,7168]{1,0:T(8,128)S(1)}, f32[16,7168]{1,0:T(8,128)S(1)}, u32[]{:S(2)}, u32[]{:S(2)}) collective-permute-start(f32[16,7168]{1,0:T(8,128)S(1)} %slice.19), channel_id=1, source_target_pairs={{0,8},{8,0},{1,9},{9,1},{2,10},{10,2},{3,11},{11,3},{4,12},{12,4},... | collective-permute-start | bytes 1376264 | tf_op jit(solution)/shard_map/ppermute | solution.py:356

commit v2 on v1

v2 whole, which is shorter than its diff:
```python
import functools
import math

import jax
import jax.numpy as jnp
from jax import lax
from jax.experimental import pallas as pl
from jax.experimental.pallas import tpu as pltpu
from jax.sharding import PartitionSpec as P

D = 7168
H = 64
HD = 256
QR = 2048
LATENT = QR + 2 * HD
LANES = 128
STATS = 16

EPS = 1e-05
NEG = -1e30

FAR, CORE, DEV = "far", "core", "dev"
POOL = (FAR, CORE)
F32, BF16 = jnp.float32, jnp.bfloat16
MIB = 1 << 20
VMEM = pl.BlockSpec(memory_space=pltpu.VMEM)
HBM = pl.BlockSpec(memory_space=pltpu.MemorySpace.HBM)


def dot(left, right, left_dim=1, right_dim=0):
    return lax.dot_general(
        left,
        right,
        (((left_dim,), (right_dim,)), ((), ())),
        preferred_element_type=F32,
    )


def whole(shape):
    return pl.BlockSpec(shape, lambda *_: (0,) * len(shape))


def params(mib):
    return pltpu.CompilerParams(vmem_limit_bytes=mib * MIB)


def streamed(weight):
    return pltpu.with_memory_space_constraint(weight, pltpu.MemorySpace.HBM)


def cost(flops, moved):
    return pl.CostEstimate(flops=flops, bytes_accessed=moved, transcendentals=0)


def started(source, target, sems, pieces, axis):
    width = source.shape[axis] // pieces
    copies = []
    for piece in range(pieces):
        span = pl.ds(piece * width, width)
        at = (slice(None),) * axis + (span,)
        copy = pltpu.make_async_copy(source.at[at], target.at[at], sems.at[piece])
        copy.start()
        copies.append(copy)
    return copies


def latent_kernel(hidden_ref, gain_hbm, w_hbm, out_ref, w_ref, gain_ref, sems, gain_sem):
    gain_copy = pltpu.make_async_copy(gain_hbm, gain_ref, gain_sem)
    gain_copy.start()
    copies = started(w_hbm, w_ref, sems, sems.shape[0], 1)
    hidden = hidden_ref[...].astype(F32)
    squares = jnp.sum(hidden * hidden, axis=1, keepdims=True)
    out_ref[:, LATENT:] = jnp.broadcast_to(squares, (hidden.shape[0], LANES))
    gain_copy.wait()
    scaled = (hidden * gain_ref[...][None, :]).astype(BF16)
    width = LATENT // len(copies)
    for step, copy in enumerate(copies):
        columns = slice(step * width, (step + 1) * width)
        copy.wait()
        out_ref[:, columns] = dot(scaled, w_ref[:, columns])


def latent_part(hidden, gain, w):
    rows, depth = hidden.shape
    return pl.pallas_call(
        latent_kernel,
        in_specs=[VMEM, HBM, HBM],
        out_specs=VMEM,
        out_shape=jax.ShapeDtypeStruct((rows, LATENT + LANES), F32),
        scratch_shapes=[
            pltpu.VMEM(w.shape, BF16),
            pltpu.VMEM(gain.shape, F32),
            pltpu.SemaphoreType.DMA((5,)),
            pltpu.SemaphoreType.DMA,
        ],
        compiler_params=params(8),
        cost_estimate=cost(2 * rows * depth * LATENT, 2 * depth * LATENT),
    )(hidden, streamed(gain), streamed(w))


def ahead_kernel(count, *refs):
    sources, targets = refs[1 : 1 + count], refs[1 + count : 1 + 2 * count]
    token_ref, sems = refs[-2:]
    copies = []
    for index, (source, target) in enumerate(zip(sources, targets)):
        copies.append(pltpu.make_async_copy(source, target, sems.at[index]))
        copies[-1].start()
    token_ref[...] = jnp.zeros_like(token_ref)
    for copy in copies:
        copy.wait()


def ahead(beside, weights):
    count = len(weights)
    shapes = [w.shape for w in weights]
    *copied, token = pl.pallas_call(
        functools.partial(ahead_kernel, count),
        in_specs=[pl.BlockSpec(memory_space=pl.ANY)] + [HBM] * count,
        out_specs=[VMEM] * (count + 1),
        out_shape=[pltpu.VMEM(shape, BF16) for shape in shapes]
        + [jax.ShapeDtypeStruct((8, LANES), F32)],
        scratch_shapes=[pltpu.SemaphoreType.DMA((count,))],
        compiler_params=params(1),
        cost_estimate=cost(0, sum(2 * math.prod(shape) for shape in shapes)),
    )(beside, *[streamed(w) for w in weights])
    return copied, token


def part_ahead(beside, weight, first, height, total, held):
    def kernel(*refs):
        source, (target, token_ref, sem) = refs[1], refs[-3:]
        rows = pl.ds(first, height)
        copy = pltpu.make_async_copy(source.at[rows], target.at[rows], sem)
        copy.start()
        token_ref[...] = jnp.zeros_like(token_ref)
        copy.wait()

    buffers = [] if held is None else [held]
    return pl.pallas_call(
        kernel,
        in_specs=[pl.BlockSpec(memory_space=pl.ANY), HBM] + [VMEM] * len(buffers),
        out_specs=[VMEM] * 2,
        out_shape=[
            pltpu.VMEM((total, weight.shape[1]), BF16),
            jax.ShapeDtypeStruct((8, LANES), F32),
        ],
        scratch_shapes=[pltpu.SemaphoreType.DMA],
        input_output_aliases={2: 0} if buffers else {},
        compiler_params=params(1),
        cost_estimate=cost(0, 2 * height * weight.shape[1]),
    )(beside, streamed(weight), *buffers)


def joined(left, right, token, add):
    def kernel(left_ref, right_ref, token_ref, out_ref):
        if add:
            out_ref[...] = left_ref[...] + right_ref[...]
        else:
            both = [left_ref[...].astype(F32), right_ref[...].astype(F32)]
            out_ref[...] = jnp.concatenate(both, axis=0).astype(out_ref.dtype)

    rows, cols = left.shape
    return pl.pallas_call(
        kernel,
        in_specs=[VMEM] * 3,
        out_specs=VMEM,
        out_shape=jax.ShapeDtypeStruct((rows if add else 2 * rows, cols), left.dtype),
        compiler_params=params(2),
        cost_estimate=cost(0, 3 * rows * cols * left.dtype.itemsize),
    )(left, right, token)


def summed(value, arrived, token):
    def kernel(value_ref, arrived_ref, token_ref, out_ref, sent_ref):
        total = value_ref[...] + arrived_ref[...].astype(F32)
        out_ref[...] = total
        sent_ref[...] = total.astype(BF16)

    shape = value.shape
    return pl.pallas_call(
        kernel,
        in_specs=[VMEM] * 3,
        out_specs=[VMEM] * 2,
        out_shape=[jax.ShapeDtypeStruct(shape, F32), jax.ShapeDtypeStruct(shape, BF16)],
        compiler_params=params(2),
        cost_estimate=cost(0, 12 * math.prod(shape)),
    )(value, arrived, token)


def normed_rows(place, value, arrived, token, hidden):
    rows, n_dev = value.shape[0], hidden.shape[0]
    cols = D // n_dev

    def kernel(place_ref, value_ref, arrived_ref, token_ref, hidden_ref, own_ref, normed_ref, wide_ref):
        squares = jnp.zeros((rows, 1), F32)
        for d in range(n_dev):
            span = slice(d * cols, (d + 1) * cols)
            attn = value_ref[:, span] + arrived_ref[:, span].astype(F32)
            residual = hidden_ref[d, :rows, :cols] + attn
            wide_ref[d] = residual
            squares += jnp.sum(residual * residual, axis=1, keepdims=True)
        factor = lax.rsqrt(squares / D + EPS)
        for d in range(n_dev):
            span = slice(d * cols, (d + 1) * cols)
            scaled = wide_ref[d] * factor * hidden_ref[d, rows : rows + 1, :cols]
            normed_ref[:, span] = scaled.astype(BF16)
        own_ref[...] = wide_ref[place_ref[0]]

    return pl.pallas_call(
        kernel,
        in_specs=[pl.BlockSpec(memory_space=pltpu.SMEM)] + [VMEM] * 4,
        out_specs=[VMEM] * 2,
        out_shape=[jax.ShapeDtypeStruct((rows, cols), F32), jax.ShapeDtypeStruct((rows, D), BF16)],
        scratch_shapes=[pltpu.VMEM((n_dev, rows, cols), F32)],
        compiler_params=params(3),
        cost_estimate=cost(0, 16 * rows * D),
    )(place, value, arrived, token, hidden)


def parts_of(value):
    high = value.astype(BF16).astype(F32)
    middle = (value - high).astype(BF16).astype(F32)
    return high, middle, value - high - middle


def query_kernel(
    left_ref, right_ref, token_ref, gain_ref, hidden_ref, next_ref, w_ref, query_ref, fresh_ref, wide_ref
):
    sums_ref = left_ref[...] + right_ref[...]
    rows, cols = hidden_ref.shape
    out = w_ref.shape[1]
    width = min(512, out)
    heads = out // HD
    factor = lax.rsqrt(sums_ref[:, LATENT : LATENT + 1] / D + EPS)
    query_latent = sums_ref[:, :QR] * factor
    mean = jnp.sum(query_latent * query_latent, axis=1, keepdims=True) / QR
    normed = (query_latent * lax.rsqrt(mean + EPS) * gain_ref[...]).astype(BF16)
    fresh = sums_ref[:, QR:LATENT] * factor
    fresh_ref[...] = fresh.astype(BF16).astype(F32)
    at = rows * heads
    hidden = hidden_ref[...].astype(F32)
    wide_ref[at:, :] = jnp.zeros((wide_ref.shape[0] - at, HD), F32)
    gains = parts_of(next_ref[...][None, :])
    for first in range(0, cols, HD):
        part = min(HD, cols - first)
        wide_ref[at : at + rows, :part] = hidden[:, first : first + part]
        at += rows
    for first in range(0, cols, HD):
        part = min(HD, cols - first)
        for gain in gains:
            wide_ref[at : at + 1, :part] = gain[:, first : first + part]
            at += 1
    for step in range(out // width):
        query = dot(normed, w_ref[:, step * width : (step + 1) * width])
        for part in range(width // HD):
            head = step * (width // HD) + part
            for row in range(rows):
                wide_ref[row * heads + head : row * heads + head + 1, :] = query[
                    row : row + 1, part * HD : (part + 1) * HD
                ]
    query_ref[...] = wide_ref[...].astype(BF16)


def queries(left, right, token, gain, hidden, next_gain, w):
    rows, cols = hidden.shape
    out = w.shape[1]
    heads = out // HD
    height = -(-(rows * heads + (rows + 3) * -(-cols // HD)) // 16) * 16
    return pl.pallas_call(
        query_kernel,
        in_specs=[VMEM] * 7,
        out_specs=[VMEM] * 2,
        out_shape=[
            jax.ShapeDtypeStruct((height, HD), BF16),
            jax.ShapeDtypeStruct((rows, 2 * HD), F32),
        ],
        scratch_shapes=[pltpu.VMEM((height, HD), F32)],
        compiler_params=params(2),
        cost_estimate=cost(2 * rows * QR * out, 2 * QR * out),
    )(left, right, token, gain.reshape(1, QR), hidden, next_gain, w)


def put_stats(ref, index, at, stats):
    heads = stats.shape[0]
    high, middle, low = parts_of(stats)
    ref[index, at:, :] = jnp.zeros((STATS, HD), F32)
    ref[index, at : at + heads, :LANES] = high
    ref[index, at : at + heads, LANES:] = middle
    ref[index, at + 8 : at + 8 + heads, :LANES] = low


def sent_stats(ref, index, at, heads):
    high = ref[index, at : at + heads, :LANES]
    middle = ref[index, at : at + heads, LANES:]
    return high + middle + ref[index, at + 8 : at + 8 + heads, :LANES]


def attend_kernel(codes, place_ref, lengths_ref, token_ref, *refs):
    n_dev = len(codes)
    pieces, refs = refs[:-8], refs[-8:]
    keys_ref, values_ref, own_ref, sent_ref, hidden_ref, wide_ref, parts_ref, weights_ref = refs
    rows, local_pos = keys_ref.shape[:2]
    heads = H // n_dev
    height = wide_ref.shape[0] // n_dev
    me = place_ref[0]
    at = 0
    for piece in pieces:
        size = piece.shape[0]
        wide_ref[at : at + size, :] = piece[...].astype(F32)
        at += size
    blocks = hidden_ref.shape[2] // HD
    for g in range(n_dev):
        first = g * height + rows * heads
        for block in range(blocks):
            span = slice(block * HD, (block + 1) * HD)
            at = first + block * rows
            hidden_ref[me ^ codes[g], :rows, span] = wide_ref[at : at + rows, :]
            at = first + blocks * rows + 3 * block
            gain = wide_ref[at : at + 1, :] + wide_ref[at + 1 : at + 2, :]
            hidden_ref[me ^ codes[g], rows : rows + 1, span] = gain + wide_ref[at + 2 : at + 3, :]
    lane = lax.broadcasted_iota(jnp.int32, (H, LANES), 1)
    columns = lax.broadcasted_iota(jnp.int32, (H, local_pos), 1) + me * local_pos
    stats = jnp.zeros((H, LANES), F32)
    for row in range(rows):
        query = jnp.concatenate(
            [
                wide_ref[g * height + row * heads : g * height + (row + 1) * heads, :]
                for g in range(n_dev)
            ],
            axis=0,
        ).astype(BF16)
        scores = dot(query, keys_ref[row], 1, 1) * (1.0 / math.sqrt(HD))
        valid = columns < lengths_ref[row]
        masked = jnp.where(valid, scores, NEG)
        top = jnp.max(masked, axis=1, keepdims=True)
        weights = jnp.where(valid, jnp.exp(masked - top), 0.0)
        mass = jnp.sum(weights, axis=1, keepdims=True)
        weights_ref[row] = weights.astype(BF16)
        stats = jnp.where(lane == row, top, stats)
        stats = jnp.where(lane == rows + row, mass, stats)
    half = n_dev // 2
    for row in range(rows):
        weighted = dot(weights_ref[row], values_ref[row])
        for g in range(n_dev):
            target = own_ref if g < half else parts_ref
            target[g % half, row * heads : (row + 1) * heads, :] = weighted[
                g * heads : (g + 1) * heads, :
            ]
    at = rows * heads
    for g in range(half):
        own_ref[g, at:, :] = jnp.zeros((STATS, HD), F32)
        own_ref[g, at : at + heads, :LANES] = stats[g * heads : (g + 1) * heads]
        put_stats(parts_ref, g, at, stats[(half + g) * heads : (half + g + 1) * heads])
    sent_ref[...] = parts_ref[...].astype(BF16)


def attend(codes, place, lengths, token, pieces, keys, values):
    rows, local_pos = keys.shape[:2]
    n_dev = len(codes)
    half = (n_dev // 2, rows * H // n_dev + STATS, HD)
    hidden_width = -(-D // n_dev // HD) * HD
    smem = pl.BlockSpec(memory_space=pltpu.SMEM)
    return pl.pallas_call(
        functools.partial(attend_kernel, codes),
        in_specs=[smem, smem] + [VMEM] * (3 + len(pieces)),
        out_specs=[VMEM] * 3,
        out_shape=[
            jax.ShapeDtypeStruct(half, F32),
            jax.ShapeDtypeStruct(half, BF16),
            jax.ShapeDtypeStruct((n_dev, rows + 8, hidden_width), F32),
        ],
        scratch_shapes=[
            pltpu.VMEM((sum(piece.shape[0] for piece in pieces), HD), F32),
            pltpu.VMEM(half, F32),
            pltpu.VMEM((rows, H, local_pos), BF16),
        ],
        compiler_params=params(5),
        cost_estimate=cost(4 * rows * H * local_pos * HD, 4 * rows * local_pos * HD),
    )(place, lengths, token, *pieces, keys, values)


def merge_kernel(rows, own_ref, arrived_ref, token_ref, out_ref, sent_ref, wide_ref, parts_ref):
    count, height, _ = own_ref.shape
    at = height - STATS
    heads = at // rows
    wide_ref[...] = arrived_ref[...].astype(F32)
    lane = lax.broadcasted_iota(jnp.int32, (heads, LANES), 1)
    half = count // 2
    for block in range(count):
        target = out_ref if block < half else parts_ref
        here = own_ref[block, at : at + heads, :LANES]
        there = sent_stats(wide_ref, block, at, heads)
        stats = jnp.zeros((heads, LANES), F32)
        for row in range(rows):
            span = slice(row * heads, (row + 1) * heads)
            top = jnp.maximum(here[:, row : row + 1], there[:, row : row + 1])
            left = jnp.exp(here[:, row : row + 1] - top)
            right = jnp.exp(there[:, row : row + 1] - top)
            mass = left * here[:, rows + row : rows + row + 1]
            mass = mass + right * there[:, rows + row : rows + row + 1]
            total = left * own_ref[block, span, :] + right * wide_ref[block, span, :]
            target[block % half, span, :] = total
            stats = jnp.where(lane == row, top, stats)
            stats = jnp.where(lane == rows + row, mass, stats)
        if block < half:
            target[block, at:, :] = jnp.zeros((STATS, HD), F32)
            target[block, at : at + heads, :LANES] = stats
        else:
            put_stats(target, block - half, at, stats)
    sent_ref[...] = parts_ref[...].astype(BF16)


def merge(rows, own, arrived, token):
    half = (own.shape[0] // 2, *own.shape[1:])
    return pl.pallas_call(
        functools.partial(merge_kernel, rows),
        in_specs=[VMEM] * 3,
        out_specs=[VMEM] * 2,
        out_shape=[jax.ShapeDtypeStruct(half, F32), jax.ShapeDtypeStruct(half, BF16)],
        scratch_shapes=[pltpu.VMEM(own.shape, F32), pltpu.VMEM(half, F32)],
        compiler_params=params(6),
        cost_estimate=cost(0, 12 * math.prod(own.shape)),
    )(own, arrived, token)


def project_kernel(
    own_ref, arrived_ref, token_ref, query_ref, fresh_ref, held_ref, w_hbm, out_ref, sent_ref, *scratch
):
    attended_ref, wide_ref, w_ref, sems = scratch
    held, steps = held_ref.shape[0], sems.shape[0]
    copies = started(w_hbm.at[held : held + w_ref.shape[0]], w_ref, sems, steps, 1)
    rows = fresh_ref.shape[0]
    at = own_ref.shape[1] - STATS
    heads = at // rows
    query = query_ref[...].astype(F32)
    wide_ref[...] = arrived_ref[...].astype(F32)
    parts = [
        (own_ref, own_ref[0, at : at + heads, :LANES]),
        (wide_ref, sent_stats(wide_ref, 0, at, heads)),
    ]
    for row in range(rows):
        span = slice(row * heads, (row + 1) * heads)
        key = fresh_ref[row : row + 1, :HD]
        value = fresh_ref[row : row + 1, HD:]
        score = jnp.sum(query[span] * key, axis=1, keepdims=True) * (1.0 / math.sqrt(HD))
        highest = score
        for _, stats in parts:
            highest = jnp.maximum(highest, stats[:, row : row + 1])
        weight = jnp.exp(score - highest)
        mass = weight
        total = weight.astype(BF16).astype(F32) * value
        for ref, stats in parts:
            factor = jnp.exp(stats[:, row : row + 1] - highest)
            mass = mass + factor * stats[:, rows + row : rows + row + 1]
            total = total + factor * ref[0, span, :]
        attended = total / mass
        for head in range(heads):
            attended_ref[row : row + 1, head * HD : (head + 1) * HD] = attended[
                head : head + 1, :
            ]
    width = D // steps
    attended = attended_ref[...].astype(BF16)
    for step, copy in enumerate(copies):
        columns = slice(step * width, (step + 1) * width)
        total = dot(attended[:, :held], held_ref[:, columns])
        copy.wait()
        total = total + dot(attended[:, held:], w_ref[:, columns])
        out_ref[:, columns] = total
        sent_ref[:, columns] = total.astype(BF16)


def project(own, arrived, token, query, fresh, held, w):
    rows = fresh.shape[0]
    depth = w.shape[0]
    return pl.pallas_call(
        project_kernel,
        in_specs=[VMEM] * 6 + [HBM],
        out_specs=[VMEM] * 2,
        out_shape=[jax.ShapeDtypeStruct((rows, D), F32), jax.ShapeDtypeStruct((rows, D), BF16)],
        scratch_shapes=[
            pltpu.VMEM((rows, depth), F32),
            pltpu.VMEM(own.shape, F32),
            pltpu.VMEM((depth - held.shape[0], D), BF16),
            pltpu.SemaphoreType.DMA((8,)),
        ],
        compiler_params=params(16),
        cost_estimate=cost(2 * rows * depth * D, 2 * depth * D),
    )(own, arrived, token, query, fresh, held, streamed(w))


def ffn_kernel(*refs):
    pieces, refs = refs[:-7], refs[-7:]
    token_ref, gate_ref, up_ref, down_ref, own_ref, other_ref, act_ref = refs
    half = own_ref.shape[0]
    rows = jnp.concatenate([piece[...] for piece in pieces], axis=0)
    units = gate_ref.shape[0]
    block = 144
    for step in range(units // block):
        span = slice(step * block, (step + 1) * block)
        gate = dot(gate_ref[span, :], rows, 1, 1)
        up = dot(up_ref[span, :], rows, 1, 1)
        act_ref[span, :] = gate / (1.0 + jnp.exp(-gate)) * up
    activated = act_ref[...].astype(BF16)
    width = down_ref.shape[1] // 8

    @pl.loop(0, 8)
    def _(step):
        columns = pl.ds(pl.multiple_of(step * width, width), width)
        term = dot(activated, down_ref[:, columns], 0, 0)
        own_ref[:, columns] = term[:half]
        other_ref[:, columns] = term[half:]


def ffn(pieces, token, gate_t, up_t, down):
    rows = sum(piece.shape[0] for piece in pieces)
    units, depth = gate_t.shape
    return pl.pallas_call(
        ffn_kernel,
        in_specs=[VMEM] * (len(pieces) + 4),
        out_specs=[VMEM] * 2,
        out_shape=[jax.ShapeDtypeStruct((rows // 2, depth), F32)] * 2,
        scratch_shapes=[pltpu.VMEM((units, rows), F32)],
        compiler_params=params(6),
        cost_estimate=cost(6 * rows * units * depth, 6 * units * depth),
    )(*pieces, token, gate_t, up_t, down)


def combined(far, own, arrived, n_far, n_dev):
    rows, cols = own.shape[0] // n_far, own.shape[1] // n_dev

    def kernel(far_ref, own_ref, arrived_ref, out_ref, wide_ref):
        for f in range(n_far):
            target = (far_ref[0] ^ f) * n_dev
            for d in range(n_dev):
                at = (slice(f * rows, (f + 1) * rows), slice(d * cols, (d + 1) * cols))
                wide_ref[target + d] = own_ref[at] + arrived_ref[at]
        out_ref[...] = wide_ref[...].astype(BF16)

    shape = (n_far * n_dev, rows, cols)
    return pl.pallas_call(
        kernel,
        in_specs=[pl.BlockSpec(memory_space=pltpu.SMEM)] + [VMEM] * 2,
        out_specs=VMEM,
        out_shape=jax.ShapeDtypeStruct(shape, BF16),
        scratch_shapes=[pltpu.VMEM(shape, F32)],
        compiler_params=params(4),
        cost_estimate=cost(0, 10 * math.prod(shape)),
    )(far, own, arrived)


def swapped(value, axis, bit):
    size = lax.axis_size(axis)
    return lax.ppermute(value, axis, [(i, i ^ bit) for i in range(size)])


def gathered(value, axis):
    size = lax.axis_size(axis)
    return lax.all_to_all(jnp.broadcast_to(value[None], (size, *value.shape)), axis, 0, 0)


def local(
    hidden_in,
    in_gain,
    w_latent,
    q_gain,
    w_query,
    cache_keys,
    cache_values,
    lengths,
    w_out,
    post_gain,
    w_gate,
    w_up,
    w_down,
):
    n_dev = lax.axis_size(DEV)
    place = lax.axis_index(DEV).astype(jnp.int32).reshape(1)
    rows, cols = hidden_in.shape

    sums = latent_part(hidden_in, in_gain, w_latent)
    copied = {}

    def copy_query(value):
        (copied["query"],), token = ahead(value, [w_query])
        return token


    def copy_out(first, height, total, value):
        held = copied.get("out")
        copied["out"], token = part_ahead(value, w_out, first, height, total, held)
        return token

    def copy_caches(value):
        copied["caches"], token = ahead(value, [cache_keys, cache_values])
        return token

    def copy_ffn(name, weight, value):
        (copied[name],), token = ahead(value, [weight])
        return token

    steps = n_dev.bit_length() - 1
    jobs = [copy_query] + [None] * (2 * steps - 2) + [copy_caches]
    block = w_out.shape[0] // 16
    heights = [4 * block, 3 * block, 3 * block] + [0] * (steps - 3)
    for step, height in enumerate(heights):
        first = sum(heights[:step])
        jobs.append(functools.partial(copy_out, first, height, sum(heights)) if height else None)
    for name, weight in (("gate", w_gate.T), ("up", w_up.T), ("down", w_down)):
        jobs.append(functools.partial(copy_ffn, name, weight))
    jobs += [None] * (steps - 3)

    def exchanged(value, bit):
        arrived = swapped(value, DEV, bit)
        job = jobs.pop(0)
        copied["token"] = job(value) if job else copied["token"]
        return arrived, copied["token"]

    bit = 1
    while bit < n_dev:
        arrived, token = exchanged(sums, bit)
        bit *= 2
        if bit < n_dev:
            sums = joined(sums, arrived, token, True)
    query, fresh = queries(
        sums, arrived, token, q_gain, hidden_in, post_gain, copied["query"]
    )

    held, codes = query, [0]
    bit = n_dev // 2
    while bit:
        arrived, token = exchanged(held, bit)
        codes = codes + [code ^ bit for code in codes]
        bit //= 2
        if bit:
            held = joined(held, arrived, token, False)
    own, sent, hidden = attend(
        codes, place, lengths, token, [held, arrived], *copied["caches"]
    )

    bit = 1
    while bit < n_dev:
        arrived, token = exchanged(sent, bit)
        bit *= 2
        if bit < n_dev:
            own, sent = merge(rows, own, arrived, token)
    attn, sent = project(own, arrived, token, query, fresh, copied["out"], w_out)

    bit = 1
    while bit < n_dev:
        arrived, token = exchanged(sent, bit)
        bit *= 2
        if bit < n_dev:
            attn, sent = summed(attn, arrived, token)
    residual, normed = normed_rows(place, attn, arrived, token, hidden)
    n_far = lax.axis_size(FAR)
    arrived = swapped(normed, FAR, 1)
    mine = joined(normed, arrived, token, False)
    other = swapped(mine, CORE, 1)
    own, other = ffn([mine, other], token, copied["gate"], copied["up"], copied["down"])

    far = lax.axis_index(FAR).astype(jnp.int32).reshape(1)
    ffn_term = combined(far, own, swapped(other, CORE, 1), n_far, n_dev)
    ffn_term = lax.all_to_all(ffn_term, (FAR, DEV), 0, 0)
    ffn_out = jnp.sum(ffn_term.astype(F32), axis=0)
    return residual + ffn_out


def solution(mesh):
    sizes = mesh.devices.shape
    mesh = jax.sharding.Mesh(
        mesh.devices.reshape(sizes[0] // 2, 2, sizes[1]), (FAR, CORE, DEV)
    )
    placed = (
        P(POOL, DEV),
        P(DEV),
        P(DEV, None),
        P(),
        P(None, DEV),
        P(POOL, DEV, None),
        P(POOL, DEV, None),
        P(POOL),
        P(DEV, None),
        P(DEV),
        P(None, (*POOL, DEV)),
        P(None, (*POOL, DEV)),
        P((*POOL, DEV), None),
    )
    return jax.shard_map(
        local, mesh=mesh, in_specs=placed, out_specs=P(POOL, DEV), check_vma=False
    )
```

time: 126 us -> 115 us (0.913)
  blocking collectives: 48.1 us -> 15.5 us
  waiting for transfers between devices: 4.66 us -> 22 us
  starting transfers between devices: 15.8 us -> 29.4 us
  local copies, waits for them, and re-layouts: 10.6 us -> 0.73 us
  Pallas kernels: 41.3 us -> 46.5 us
  matrix products: 3.03 us -> 0 us
  other arithmetic: 1.96 us -> 0.65 us
    all_to_all x4 -> x1, blocking collectives: 48.1 us -> 15.5 us  [local(): ffn_term = lax.all_to_all(ffn_term, (FAR, DEV), 0, 0)]
    ppermute x9 -> x15, waiting for transfers between devices: 4.66 us -> 22 us  [swapped(): return lax.ppermute(value, axis, [(i, i ^ bit) for i in range(size)])]
    ppermute x9 -> x15, starting transfers between devices: 15.8 us -> 29.4 us  [swapped(): return lax.ppermute(value, axis, [(i, i ^ bit) for i in range(size)])]
    unnamed x12 -> x8, local copies, waits for them, and re-layouts: 10.4 us -> 0.73 us
    pallas_call x2 -> x9, Pallas kernels: 9.58 us -> 13.8 us  [the longest x1 8.46 us: project(): pl.pallas_call(project_kernel, in_specs=[VMEM] * 6 + [HBM], out_specs=[VM...]
    dot_general x1 -> x0, matrix products: 3.03 us -> none  [dot(): lax.dot_general(left, right, (((left_dim,), (right_dim,)), ((), ())), pre...]
    pallas_call x4 -> x5, Pallas kernels: 14.7 us -> 15.7 us  [ahead(): pl.pallas_call(functools.partial(ahead_kernel, count), in_specs=[pl.Block...]
    pallas_call x4 -> x3, Pallas kernels: 8.21 us -> 8.23 us  [part_ahead(): pl.pallas_call(kernel, in_specs=[pl.BlockSpec(memory_space=pl.ANY), HBM]...]
  transfers between devices with their start and end apart: 9 -> 15, of which waited for: 5 -> 11; matrix products, arithmetic and copies ran while one was open for 0% -> 0% of each run, Pallas kernels for 18% -> 21%
where the time goes in v2:
time: 115 us
  Pallas kernels  46.5 us (40%)
  starting transfers between devices  29.4 us (26%)
  waiting for transfers between devices  22 us (19%)
  blocking collectives  15.5 us (13%)
    ppermute x15, starting transfers between devices, swapped(): return lax.ppermute(value, axis, [(i, i ^ bit) for i in range(size)])  29.4 us
    ppermute x15, waiting for transfers between devices, swapped(): return lax.ppermute(value, axis, [(i, i ^ bit) for i in range(size)])  22 us
    pallas_call x5, Pallas kernels, ahead(): pl.pallas_call(functools.partial(ahead_kernel, count), in_specs=[pl.Block...  15.7 us
    all_to_all x1, blocking collectives, local(): ffn_term = lax.all_to_all(ffn_term, (FAR, DEV), 0, 0)  15.5 us
    pallas_call x1, Pallas kernels, project(): pl.pallas_call(project_kernel, in_specs=[VMEM] * 6 + [HBM], out_specs=[VM...  8.46 us
    pallas_call x3, Pallas kernels, part_ahead(): pl.pallas_call(kernel, in_specs=[pl.BlockSpec(memory_space=pl.ANY), HBM]...  8.23 us
    pallas_call x1, Pallas kernels, ffn(): pl.pallas_call(ffn_kernel, in_specs=[VMEM] * (len(pieces) + 4), out_specs...  7 us
    pallas_call x1, Pallas kernels, latent_part(): pl.pallas_call(latent_kernel, in_specs=[VMEM, HBM, HBM], out_specs=VMEM,...  3.07 us
  transfers between devices with their start and end apart: 15, of which 11 were waited for; matrix products, arithmetic and copies ran while one was open for 0% of the time, Pallas kernels for 21%

profile of v2, /device:TPU:0, one launch (start us, length us, event | category | flops | bytes accessed | tf_op | source)
XLA Modules:
  0.0 115.0 jit_solution(8226485809636710476)
XLA Ops:
  0.0 0.0 copy-start
  0.0 0.7 copy-done
  0.7 0.0 copy-start.1
  0.7 0.0 copy-start.2
  0.7 3.1 %shard_map.127.refs_0_.left_ref = f32[8,2688]{1,0:T(8,128)S(1)} custom-call(bf16[8,896]{1,0:T(8,128)(2,1)S(1)} %copy-done, f32[896]{0:T(1024)} %gain_hbm.1, bf16[896,2560]{1,0:T(8,128)(2,1)} %w_hbm.2), custom_call_target="tpu_custom_call" | custom-call | flops 36700160 | bytes 4587520 | tf_op jit(solution)/shard_map/pallas_call | solution.py:85
  3.8 3.0 %collective-permute-start = (f32[8,2688]{1,0:T(8,128)S(1)}, f32[8,2688]{1,0:T(8,128)S(1)}, u32[]{:S(2)}, u32[]{:S(2)}) collective-permute-start(f32[8,2688]{1,0:T(8,128)S(1)} %shard_map.127.refs_0_.left_ref), channel_id=1, source_target_pairs={{0,1},{1,0},{2,3},{3,2},{4,5},{5,4},{6,7},{7,6},{8,9},{9,8},{10,11... | collective-permute-start | bytes 258056 | tf_op jit(solution)/shard_map/ppermute | solution.py:553
  6.8 3.4 %shard_map.128 = (bf16[2048,2048]{1,0:T(8,128)(2,1)S(1)}, f32[8,128]{1,0:T(8,128)S(1)}) custom-call(f32[8,2688]{1,0:T(8,128)S(1)} %shard_map.127.refs_0_.left_ref, bf16[2048,2048]{1,0:T(8,128)(2,1)} %refs_1_.6), custom_call_target="tpu_custom_call" | custom-call | bytes 8388608 | tf_op jit(solution)/shard_map/pallas_call | solution.py:116
  10.2 0.0 copy-start.3
  10.2 0.0 collective-permute-done.right_ref
  10.3 1.6 %collective-permute-start.1 = (f32[8,2688]{1,0:T(8,128)S(1)}, f32[8,2688]{1,0:T(8,128)S(1)}, u32[]{:S(2)}, u32[]{:S(2)}) collective-permute-start(f32[8,2688]{1,0:T(8,128)S(1)} %shard_map.129.left_ref), channel_id=1, source_target_pairs={{0,2},{1,3},{2,0},{3,1},{4,6},{5,7},{6,4},{7,5},{8,10},{9,11},{10,... | collective-permute-start | bytes 258056 | tf_op jit(solution)/shard_map/ppermute | solution.py:553
  11.9 2.9 %collective-permute-done.1.right_ref = f32[8,2688]{1,0:T(8,128)S(1)} collective-permute-done((f32[8,2688]{1,0:T(8,128)S(1)}, f32[8,2688]{1,0:T(8,128)S(1)}, u32[]{:S(2)}, u32[]{:S(2)}) %collective-permute-start.1) | collective-permute-done | bytes 86048 | tf_op jit(solution)/shard_map/ppermute | solution.py:553
  14.8 2.7 %collective-permute-start.2 = (f32[8,2688]{1,0:T(8,128)S(1)}, f32[8,2688]{1,0:T(8,128)S(1)}, u32[]{:S(2)}, u32[]{:S(2)}) collective-permute-start(f32[8,2688]{1,0:T(8,128)S(1)} %shard_map.130.left_ref), channel_id=1, source_target_pairs={{0,4},{1,5},{2,6},{3,7},{4,0},{5,1},{6,2},{7,3},{8,12},{9,13},{10,... | collective-permute-start | bytes 258056 | tf_op jit(solution)/shard_map/ppermute | solution.py:553
  17.5 2.8 %collective-permute-done.2.right_ref = f32[8,2688]{1,0:T(8,128)S(1)} collective-permute-done((f32[8,2688]{1,0:T(8,128)S(1)}, f32[8,2688]{1,0:T(8,128)S(1)}, u32[]{:S(2)}, u32[]{:S(2)}) %collective-permute-start.2) | collective-permute-done | bytes 86048 | tf_op jit(solution)/shard_map/ppermute | solution.py:553
  20.3 0.0 copy-done.1
  20.3 0.0 copy-done.2
  20.3 1.4 %shard_map.131 = (bf16[112,256]{1,0:T(8,128)(2,1)S(1)}, f32[8,512]{1,0:T(8,128)S(1)}) custom-call(f32[8,2688]{1,0:T(8,128)S(1)} %shard_map.130.left_ref, f32[8,2688]{1,0:T(8,128)S(1)} %collective-permute-done.2.right_ref, f32[8,128]{1,0:T(8,128)S(1)} %get-tuple-element.41.token_ref, f32[1,2048]{1,0:T(1,128)S(1)} %bitcast.5, bf16[8,896]{1,0:T(8,128)(2,1)S(1)} %copy-done, ...), custom_call_target="tpu_custom_call" | custom-call | flops 67108864 | bytes 8388608 | tf_op jit(solution)/shard_map/pallas_call | solution.py:269
  21.7 2.7 %collective-permute-start.3 = (bf16[112,256]{1,0:T(8,128)(2,1)S(1)}, bf16[112,256]{1,0:T(8,128)(2,1)S(1)}, u32[]{:S(2)}, u32[]{:S(2)}) collective-permute-start(bf16[112,256]{1,0:T(8,128)(2,1)S(1)} %get-tuple-element.43.left_ref.query_ref), channel_id=1, source_target_pairs={{0,4},{1,5},{2,6},{3,7},{4,0},{5,1},{6,2},{7,3},{8,12},{9,13},{10,... | collective-permute-start | bytes 172040 | tf_op jit(solution)/shard_map/ppermute | solution.py:553
  24.4 2.5 %collective-permute-done.3.right_ref = bf16[112,256]{1,0:T(8,128)(2,1)S(1)} collective-permute-done((bf16[112,256]{1,0:T(8,128)(2,1)S(1)}, bf16[112,256]{1,0:T(8,128)(2,1)S(1)}, u32[]{:S(2)}, u32[]{:S(2)}) %collective-permute-start.3) | collective-permute-done | bytes 57376 | tf_op jit(solution)/shard_map/ppermute | solution.py:553
  26.9 2.1 %collective-permute-start.4 = (bf16[224,256]{1,0:T(8,128)(2,1)S(1)}, bf16[224,256]{1,0:T(8,128)(2,1)S(1)}, u32[]{:S(2)}, u32[]{:S(2)}) collective-permute-start(bf16[224,256]{1,0:T(8,128)(2,1)S(1)} %shard_map.132.left_ref), channel_id=1, source_target_pairs={{0,2},{1,3},{2,0},{3,1},{4,6},{5,7},{6,4},{7,5},{8,10},{9,11},{10,... | collective-permute-start | bytes 344072 | tf_op jit(solution)/shard_map/ppermute | solution.py:553
  29.0 2.8 %collective-permute-done.4.right_ref = bf16[224,256]{1,0:T(8,128)(2,1)S(1)} collective-permute-done((bf16[224,256]{1,0:T(8,128)(2,1)S(1)}, bf16[224,256]{1,0:T(8,128)(2,1)S(1)}, u32[]{:S(2)}, u32[]{:S(2)}) %collective-permute-start.4) | collective-permute-done | bytes 114720 | tf_op jit(solution)/shard_map/ppermute | solution.py:553
  31.8 1.6 %collective-permute-start.5 = (bf16[448,256]{1,0:T(8,128)(2,1)S(1)}, bf16[448,256]{1,0:T(8,128)(2,1)S(1)}, u32[]{:S(2)}, u32[]{:S(2)}) collective-permute-start(bf16[448,256]{1,0:T(8,128)(2,1)S(1)} %shard_map.133.refs_0_), channel_id=1, source_target_pairs={{0,1},{1,0},{2,3},{3,2},{4,5},{5,4},{6,7},{7,6},{8,9},{9,8},{10,11... | collective-permute-start | bytes 688136 | tf_op jit(solution)/shard_map/ppermute | solution.py:553
  33.4 2.2 %shard_map.134 = (bf16[8,512,256]{2,1,0:T(8,128)(2,1)S(1)}, bf16[8,512,256]{2,1,0:T(8,128)(2,1)S(1)}, f32[8,128]{1,0:T(8,128)S(1)}) custom-call(bf16[448,256]{1,0:T(8,128)(2,1)S(1)} %shard_map.133.refs_0_, bf16[8,512,256]{2,1,0:T(8,128)(2,1)} %refs_1_.7, bf16[8,512,256]{2,1,0:T(8,128)(2,1)} %refs_2_.1), custom_call_target="tpu_custom_call" | custom-call | bytes 4194304 | tf_op jit(solution)/shard_map/pallas_call | solution.py:116
  35.7 2.9 %collective-permute-done.5.refs_1_ = bf16[448,256]{1,0:T(8,128)(2,1)S(1)} collective-permute-done((bf16[448,256]{1,0:T(8,128)(2,1)S(1)}, bf16[448,256]{1,0:T(8,128)(2,1)S(1)}, u32[]{:S(2)}, u32[]{:S(2)}) %collective-permute-start.5) | collective-permute-done | bytes 229408 | tf_op jit(solution)/shard_map/ppermute | solution.py:553
  38.6 0.0 copy-done.3
  38.6 1.7 %shard_map.135 = (f32[4,80,256]{2,1,0:T(8,128)S(1)}, bf16[4,80,256]{2,1,0:T(8,128)(2,1)S(1)}, f32[8,16,1024]{2,1,0:T(8,128)S(1)}) custom-call(s32[1]{0:T(128)} %bitcast.place_ref, s32[8]{0:T(128)S(1)} %copy-done.3, f32[8,128]{1,0:T(8,128)S(1)} %get-tuple-element.44.token_ref, bf16[448,256]{1,0:T(8,128)(2,1)S(1)} %shard_map.133.refs_0_, ...), custom_call_target="tpu_custom_call" | custom-call | flops 268435456 | bytes 4194304 | tf_op jit(solution)/shard_map/pallas_call | solution.py:363
  40.3 2.5 %collective-permute-start.6 = (bf16[4,80,256]{2,1,0:T(8,128)(2,1)S(1)}, bf16[4,80,256]{2,1,0:T(8,128)(2,1)S(1)}, u32[]{:S(2)}, u32[]{:S(2)}) collective-permute-start(bf16[4,80,256]{2,1,0:T(8,128)(2,1)S(1)} %get-tuple-element.48.refs_0_), channel_id=1, source_target_pairs={{0,1},{1,0},{2,3},{3,2},{4,5},{5,4},{6,7},{7,6},{8,9},{9,8},{10,11... | collective-permute-start | bytes 491528 | tf_op jit(solution)/shard_map/ppermute | solution.py:553
  42.9 3.1 %shard_map.136 = (bf16[1280,7168]{1,0:T(8,128)(2,1)S(1)}, f32[8,128]{1,0:T(8,128)S(1)}) custom-call(bf16[4,80,256]{2,1,0:T(8,128)(2,1)S(1)} %get-tuple-element.48.refs_0_, bf16[2048,7168]{1,0:T(8,128)(2,1)} %w_hbm.3), custom_call_target="tpu_custom_call" | custom-call | bytes 7340032 | tf_op jit(solution)/shard_map/pallas_call | solution.py:139
  46.0 0.2 collective-permute-done.6.arrived_ref
  46.2 0.4 shard_map.137
  46.6 2.1 %collective-permute-start.7 = (bf16[2,80,256]{2,1,0:T(8,128)(2,1)S(1)}, bf16[2,80,256]{2,1,0:T(8,128)(2,1)S(1)}, u32[]{:S(2)}, u32[]{:S(2)}) collective-permute-start(bf16[2,80,256]{2,1,0:T(8,128)(2,1)S(1)} %get-tuple-element.51.refs_0_), channel_id=1, source_target_pairs={{0,2},{1,3},{2,0},{3,1},{4,6},{5,7},{6,4},{7,5},{8,10},{9,11},{10,... | collective-permute-start | bytes 245768 | tf_op jit(solution)/shard_map/ppermute | solution.py:553
  48.7 2.6 %shard_map.138 = (bf16[1280,7168]{1,0:T(8,128)(2,1)S(1)}, f32[8,128]{1,0:T(8,128)S(1)}) custom-call(bf16[2,80,256]{2,1,0:T(8,128)(2,1)S(1)} %get-tuple-element.51.refs_0_, bf16[2048,7168]{1,0:T(8,128)(2,1)} %w_hbm.3, bf16[1280,7168]{1,0:T(8,128)(2,1)S(1)} %get-tuple-element.52.refs_2_), custom_call_target="tpu_custom_call", output_to_operand_aliasing={{0}: (2, {})} | custom-call | bytes 5505024 | tf_op jit(solution)/shard_map/pallas_call | solution.py:139
  51.3 0.0 collective-permute-done.7.arrived_ref
  51.3 0.2 shard_map.139
  51.5 3.5 %collective-permute-start.8 = (bf16[1,80,256]{2,1,0:T(8,128)(2,1)S(1)}, bf16[1,80,256]{2,1,0:T(8,128)(2,1)S(1)}, u32[]{:S(2)}, u32[]{:S(2)}) collective-permute-start(bf16[1,80,256]{2,1,0:T(8,128)(2,1)S(1)} %get-tuple-element.55.refs_0_), channel_id=1, source_target_pairs={{0,4},{1,5},{2,6},{3,7},{4,0},{5,1},{6,2},{7,3},{8,12},{9,13},{10,... | collective-permute-start | bytes 122888 | tf_op jit(solution)/shard_map/ppermute | solution.py:553
  55.0 2.6 %shard_map.140 = (bf16[1280,7168]{1,0:T(8,128)(2,1)S(1)}, f32[8,128]{1,0:T(8,128)S(1)}) custom-call(bf16[1,80,256]{2,1,0:T(8,128)(2,1)S(1)} %get-tuple-element.55.refs_0_, bf16[2048,7168]{1,0:T(8,128)(2,1)} %w_hbm.3, bf16[1280,7168]{1,0:T(8,128)(2,1)S(1)} %get-tuple-element.56.refs_2_), custom_call_target="tpu_custom_call", output_to_operand_aliasing={{0}: (2, {})} | custom-call | bytes 5505024 | tf_op jit(solution)/shard_map/pallas_call | solution.py:139
  57.6 0.0 collective-permute-done.8.arrived_ref
  57.6 8.5 %shard_map.141 = (f32[8,7168]{1,0:T(8,128)S(1)}, bf16[8,7168]{1,0:T(8,128)(2,1)S(1)}) custom-call(f32[1,80,256]{2,1,0:T(8,128)S(1)} %get-tuple-element.54.own_ref, bf16[1,80,256]{2,1,0:T(8,128)(2,1)S(1)} %collective-permute-done.8.arrived_ref, f32[8,128]{1,0:T(8,128)S(1)} %get-tuple-element.57.token_ref, ...), custom_call_target="tpu_custom_call" | custom-call | flops 234881024 | bytes 29360128 | tf_op jit(solution)/shard_map/pallas_call | solution.py:475
  66.1 1.3 %collective-permute-start.9 = (bf16[8,7168]{1,0:T(8,128)(2,1)S(1)}, bf16[8,7168]{1,0:T(8,128)(2,1)S(1)}, u32[]{:S(2)}, u32[]{:S(2)}) collective-permute-start(bf16[8,7168]{1,0:T(8,128)(2,1)S(1)} %get-tuple-element.61.refs_0_), channel_id=1, source_target_pairs={{0,1},{1,0},{2,3},{3,2},{4,5},{5,4},{6,7},{7,6},{8,9},{9,8},{10,11... | collective-permute-start | bytes 344072 | tf_op jit(solution)/shard_map/ppermute | solution.py:553
  67.4 3.4 %shard_map.142 = (bf16[576,7168]{1,0:T(8,128)(2,1)S(1)}, f32[8,128]{1,0:T(8,128)S(1)}) custom-call(bf16[8,7168]{1,0:T(8,128)(2,1)S(1)} %get-tuple-element.61.refs_0_, bf16[576,7168]{1,0:T(8,128)(2,1)} %bitcast.6), custom_call_target="tpu_custom_call" | custom-call | bytes 8257536 | tf_op jit(solution)/shard_map/pallas_call | solution.py:116
  70.7 0.2 collective-permute-done.9.arrived_ref
  71.0 1.9 %collective-permute-start.10 = (bf16[8,7168]{1,0:T(8,128)(2,1)S(1)}, bf16[8,7168]{1,0:T(8,128)(2,1)S(1)}, u32[]{:S(2)}, u32[]{:S(2)}) collective-permute-start(bf16[8,7168]{1,0:T(8,128)(2,1)S(1)} %get-tuple-element.64.refs_0_), channel_id=1, source_target_pairs={{0,2},{1,3},{2,0},{3,1},{4,6},{5,7},{6,4},{7,5},{8,10},{9,11},{10,... | collective-permute-start | bytes 344072 | tf_op jit(solution)/shard_map/ppermute | solution.py:553
  72.9 3.4 %shard_map.144 = (bf16[576,7168]{1,0:T(8,128)(2,1)S(1)}, f32[8,128]{1,0:T(8,128)S(1)}) custom-call(bf16[8,7168]{1,0:T(8,128)(2,1)S(1)} %get-tuple-element.64.refs_0_, bf16[576,7168]{1,0:T(8,128)(2,1)} %bitcast.7), custom_call_target="tpu_custom_call" | custom-call | bytes 8257536 | tf_op jit(solution)/shard_map/pallas_call | solution.py:116
  76.3 0.0 collective-permute-done.10.arrived_ref
  76.3 2.4 %collective-permute-start.11 = (bf16[8,7168]{1,0:T(8,128)(2,1)S(1)}, bf16[8,7168]{1,0:T(8,128)(2,1)S(1)}, u32[]{:S(2)}, u32[]{:S(2)}) collective-permute-start(bf16[8,7168]{1,0:T(8,128)(2,1)S(1)} %get-tuple-element.67.refs_0_), channel_id=1, source_target_pairs={{0,4},{1,5},{2,6},{3,7},{4,0},{5,1},{6,2},{7,3},{8,12},{9,13},{10,... | collective-permute-start | bytes 344072 | tf_op jit(solution)/shard_map/ppermute | solution.py:553
  78.7 3.4 %shard_map.146 = (bf16[576,7168]{1,0:T(8,128)(2,1)S(1)}, f32[8,128]{1,0:T(8,128)S(1)}) custom-call(bf16[8,7168]{1,0:T(8,128)(2,1)S(1)} %get-tuple-element.67.refs_0_, bf16[576,7168]{1,0:T(8,128)(2,1)} %refs_1_.11), custom_call_target="tpu_custom_call" | custom-call | bytes 8257536 | tf_op jit(solution)/shard_map/pallas_call | solution.py:116
  82.1 1.2 %collective-permute-done.11.arrived_ref = bf16[8,7168]{1,0:T(8,128)(2,1)S(1)} collective-permute-done((bf16[8,7168]{1,0:T(8,128)(2,1)S(1)}, bf16[8,7168]{1,0:T(8,128)(2,1)S(1)}, u32[]{:S(2)}, u32[]{:S(2)}) %collective-permute-start.11) | collective-permute-done | bytes 114720 | tf_op jit(solution)/shard_map/ppermute | solution.py:553
  83.3 0.2 shard_map.147
  83.5 1.6 %collective-permute-start.12 = (bf16[8,7168]{1,0:T(8,128)(2,1)S(1)}, bf16[8,7168]{1,0:T(8,128)(2,1)S(1)}, u32[]{:S(2)}, u32[]{:S(2)}) collective-permute-start(bf16[8,7168]{1,0:T(8,128)(2,1)S(1)} %get-tuple-element.71.left_ref), channel_id=1, source_target_pairs={{0,16},{16,0},{1,17},{17,1},{2,18},{18,2},{3,19},{19,3},{4,20},{20... | collective-permute-start | bytes 344072 | tf_op jit(solution)/shard_map/ppermute | solution.py:553
  85.0 3.3 %collective-permute-done.12.right_ref = bf16[8,7168]{1,0:T(8,128)(2,1)S(1)} collective-permute-done((bf16[8,7168]{1,0:T(8,128)(2,1)S(1)}, bf16[8,7168]{1,0:T(8,128)(2,1)S(1)}, u32[]{:S(2)}, u32[]{:S(2)}) %collective-permute-start.12) | collective-permute-done | bytes 114720 | tf_op jit(solution)/shard_map/ppermute | solution.py:553
  88.3 0.1 collective-permute-start.13
  88.4 1.5 %collective-permute-done.13.refs_1_ = bf16[16,7168]{1,0:T(8,128)(2,1)S(1)} collective-permute-done((bf16[16,7168]{1,0:T(8,128)(2,1)S(1)}, bf16[16,7168]{1,0:T(8,128)(2,1)S(1)}, u32[]{:S(2)}, u32[]{:S(2)}) %collective-permute-start.13) | collective-permute-done | bytes 229408 | tf_op jit(solution)/shard_map/ppermute | solution.py:553
  89.9 7.0 %shard_map.149 = (f32[16,7168]{1,0:T(8,128)S(1)}, f32[16,7168]{1,0:T(8,128)S(1)}) custom-call(bf16[16,7168]{1,0:T(8,128)(2,1)S(1)} %shard_map.148.refs_0_, bf16[16,7168]{1,0:T(8,128)(2,1)S(1)} %collective-permute-done.13.refs_1_, f32[8,128]{1,0:T(8,128)S(1)} %get-tuple-element.68.token_ref.refs_2_, bf16[576,7168]{1,0:T(8,128)(2,1)S(1)} %get-tuple-element.72.refs_3_, ...), custom_call_target="tpu_custom_call" | custom-call | flops 792723456 | bytes 24772608 | tf_op jit(solution)/shard_map/pallas_call | solution.py:517
  96.9 0.2 collective-permute-start.14
  97.1 1.7 %collective-permute-done.14.arrived_ref = f32[16,7168]{1,0:T(8,128)S(1)} collective-permute-done((f32[16,7168]{1,0:T(8,128)S(1)}, f32[16,7168]{1,0:T(8,128)S(1)}, u32[]{:S(2)}, u32[]{:S(2)}) %collective-permute-start.14) | collective-permute-done | bytes 458784 | tf_op jit(solution)/shard_map/ppermute | solution.py:553
  98.8 0.1 shard_map.150
  98.9 15.5 %all_to_all.5 = bf16[16,8,896]{2,1,0:T(8,128)(2,1)S(1)} all-to-all(bf16[16,8,896]{2,1,0:T(8,128)(2,1)S(1)} %shard_map.150), channel_id=1, replica_groups=mesh['far'=2,'core'=2,'dev'=8] {'far','dev'}, dimensions={0} | all-to-all | bytes 458752 | tf_op jit(solution)/shard_map/all_to_all | solution.py:663
  114.4 0.6 add.3
  (8 shorter events, 0.2 us)
Async XLA Ops:
  0.0 0.7 copy-start
  0.7 19.6 %copy-start.1 = (f32[2048]{0:T(1024)S(1)}, f32[2048]{0:T(1024)}, u32[]{:S(2)}) copy-start(f32[2048]{0:T(1024)} %param.16) | copy-start | bytes 24580
  0.7 19.6 %copy-start.2 = (f32[896]{0:T(1024)S(1)}, f32[896]{0:T(1024)}, u32[]{:S(2)}) copy-start(f32[896]{0:T(1024)} %next_ref.1) | copy-start | bytes 10756
  3.8 6.4 %collective-permute-start = (f32[8,2688]{1,0:T(8,128)S(1)}, f32[8,2688]{1,0:T(8,128)S(1)}, u32[]{:S(2)}, u32[]{:S(2)}) collective-permute-start(f32[8,2688]{1,0:T(8,128)S(1)} %shard_map.127.refs_0_.left_ref), channel_id=1, source_target_pairs={{0,1},{1,0},{2,3},{3,2},{4,5},{5,4},{6,7},{7,6},{8,9},{9,8},{10,11... | collective-permute-start | bytes 258056 | tf_op jit(solution)/shard_map/ppermute | solution.py:553
  10.2 28.4 %copy-start.3 = (s32[8]{0:T(128)S(1)}, s32[8]{0:T(128)}, u32[]{:S(2)}) copy-start(s32[8]{0:T(128)} %lengths_ref.1) | copy-start | bytes 100
  10.3 4.6 %collective-permute-start.1 = (f32[8,2688]{1,0:T(8,128)S(1)}, f32[8,2688]{1,0:T(8,128)S(1)}, u32[]{:S(2)}, u32[]{:S(2)}) collective-permute-start(f32[8,2688]{1,0:T(8,128)S(1)} %shard_map.129.left_ref), channel_id=1, source_target_pairs={{0,2},{1,3},{2,0},{3,1},{4,6},{5,7},{6,4},{7,5},{8,10},{9,11},{10,... | collective-permute-start | bytes 258056 | tf_op jit(solution)/shard_map/ppermute | solution.py:553
  14.8 5.4 %collective-permute-start.2 = (f32[8,2688]{1,0:T(8,128)S(1)}, f32[8,2688]{1,0:T(8,128)S(1)}, u32[]{:S(2)}, u32[]{:S(2)}) collective-permute-start(f32[8,2688]{1,0:T(8,128)S(1)} %shard_map.130.left_ref), channel_id=1, source_target_pairs={{0,4},{1,5},{2,6},{3,7},{4,0},{5,1},{6,2},{7,3},{8,12},{9,13},{10,... | collective-permute-start | bytes 258056 | tf_op jit(solution)/shard_map/ppermute | solution.py:553
  21.7 5.2 %collective-permute-start.3 = (bf16[112,256]{1,0:T(8,128)(2,1)S(1)}, bf16[112,256]{1,0:T(8,128)(2,1)S(1)}, u32[]{:S(2)}, u32[]{:S(2)}) collective-permute-start(bf16[112,256]{1,0:T(8,128)(2,1)S(1)} %get-tuple-element.43.left_ref.query_ref), channel_id=1, source_target_pairs={{0,4},{1,5},{2,6},{3,7},{4,0},{5,1},{6,2},{7,3},{8,12},{9,13},{10,... | collective-permute-start | bytes 172040 | tf_op jit(solution)/shard_map/ppermute | solution.py:553
  26.9 4.9 %collective-permute-start.4 = (bf16[224,256]{1,0:T(8,128)(2,1)S(1)}, bf16[224,256]{1,0:T(8,128)(2,1)S(1)}, u32[]{:S(2)}, u32[]{:S(2)}) collective-permute-start(bf16[224,256]{1,0:T(8,128)(2,1)S(1)} %shard_map.132.left_ref), channel_id=1, source_target_pairs={{0,2},{1,3},{2,0},{3,1},{4,6},{5,7},{6,4},{7,5},{8,10},{9,11},{10,... | collective-permute-start | bytes 344072 | tf_op jit(solution)/shard_map/ppermute | solution.py:553
  31.8 6.8 %collective-permute-start.5 = (bf16[448,256]{1,0:T(8,128)(2,1)S(1)}, bf16[448,256]{1,0:T(8,128)(2,1)S(1)}, u32[]{:S(2)}, u32[]{:S(2)}) collective-permute-start(bf16[448,256]{1,0:T(8,128)(2,1)S(1)} %shard_map.133.refs_0_), channel_id=1, source_target_pairs={{0,1},{1,0},{2,3},{3,2},{4,5},{5,4},{6,7},{7,6},{8,9},{9,8},{10,11... | collective-permute-start | bytes 688136 | tf_op jit(solution)/shard_map/ppermute | solution.py:553
  40.3 5.8 %collective-permute-start.6 = (bf16[4,80,256]{2,1,0:T(8,128)(2,1)S(1)}, bf16[4,80,256]{2,1,0:T(8,128)(2,1)S(1)}, u32[]{:S(2)}, u32[]{:S(2)}) collective-permute-start(bf16[4,80,256]{2,1,0:T(8,128)(2,1)S(1)} %get-tuple-element.48.refs_0_), channel_id=1, source_target_pairs={{0,1},{1,0},{2,3},{3,2},{4,5},{5,4},{6,7},{7,6},{8,9},{9,8},{10,11... | collective-permute-start | bytes 491528 | tf_op jit(solution)/shard_map/ppermute | solution.py:553
  46.6 4.7 %collective-permute-start.7 = (bf16[2,80,256]{2,1,0:T(8,128)(2,1)S(1)}, bf16[2,80,256]{2,1,0:T(8,128)(2,1)S(1)}, u32[]{:S(2)}, u32[]{:S(2)}) collective-permute-start(bf16[2,80,256]{2,1,0:T(8,128)(2,1)S(1)} %get-tuple-element.51.refs_0_), channel_id=1, source_target_pairs={{0,2},{1,3},{2,0},{3,1},{4,6},{5,7},{6,4},{7,5},{8,10},{9,11},{10,... | collective-permute-start | bytes 245768 | tf_op jit(solution)/shard_map/ppermute | solution.py:553
  51.5 6.1 %collective-permute-start.8 = (bf16[1,80,256]{2,1,0:T(8,128)(2,1)S(1)}, bf16[1,80,256]{2,1,0:T(8,128)(2,1)S(1)}, u32[]{:S(2)}, u32[]{:S(2)}) collective-permute-start(bf16[1,80,256]{2,1,0:T(8,128)(2,1)S(1)} %get-tuple-element.55.refs_0_), channel_id=1, source_target_pairs={{0,4},{1,5},{2,6},{3,7},{4,0},{5,1},{6,2},{7,3},{8,12},{9,13},{10,... | collective-permute-start | bytes 122888 | tf_op jit(solution)/shard_map/ppermute | solution.py:553
  66.1 4.9 %collective-permute-start.9 = (bf16[8,7168]{1,0:T(8,128)(2,1)S(1)}, bf16[8,7168]{1,0:T(8,128)(2,1)S(1)}, u32[]{:S(2)}, u32[]{:S(2)}) collective-permute-start(bf16[8,7168]{1,0:T(8,128)(2,1)S(1)} %get-tuple-element.61.refs_0_), channel_id=1, source_target_pairs={{0,1},{1,0},{2,3},{3,2},{4,5},{5,4},{6,7},{7,6},{8,9},{9,8},{10,11... | collective-permute-start | bytes 344072 | tf_op jit(solution)/shard_map/ppermute | solution.py:553
  71.0 5.3 %collective-permute-start.10 = (bf16[8,7168]{1,0:T(8,128)(2,1)S(1)}, bf16[8,7168]{1,0:T(8,128)(2,1)S(1)}, u32[]{:S(2)}, u32[]{:S(2)}) collective-permute-start(bf16[8,7168]{1,0:T(8,128)(2,1)S(1)} %get-tuple-element.64.refs_0_), channel_id=1, source_target_pairs={{0,2},{1,3},{2,0},{3,1},{4,6},{5,7},{6,4},{7,5},{8,10},{9,11},{10,... | collective-permute-start | bytes 344072 | tf_op jit(solution)/shard_map/ppermute | solution.py:553
  76.3 7.0 %collective-permute-start.11 = (bf16[8,7168]{1,0:T(8,128)(2,1)S(1)}, bf16[8,7168]{1,0:T(8,128)(2,1)S(1)}, u32[]{:S(2)}, u32[]{:S(2)}) collective-permute-start(bf16[8,7168]{1,0:T(8,128)(2,1)S(1)} %get-tuple-element.67.refs_0_), channel_id=1, source_target_pairs={{0,4},{1,5},{2,6},{3,7},{4,0},{5,1},{6,2},{7,3},{8,12},{9,13},{10,... | collective-permute-start | bytes 344072 | tf_op jit(solution)/shard_map/ppermute | solution.py:553
  83.5 4.9 %collective-permute-start.12 = (bf16[8,7168]{1,0:T(8,128)(2,1)S(1)}, bf16[8,7168]{1,0:T(8,128)(2,1)S(1)}, u32[]{:S(2)}, u32[]{:S(2)}) collective-permute-start(bf16[8,7168]{1,0:T(8,128)(2,1)S(1)} %get-tuple-element.71.left_ref), channel_id=1, source_target_pairs={{0,16},{16,0},{1,17},{17,1},{2,18},{18,2},{3,19},{19,3},{4,20},{20... | collective-permute-start | bytes 344072 | tf_op jit(solution)/shard_map/ppermute | solution.py:553
  88.3 1.6 %collective-permute-start.13 = (bf16[16,7168]{1,0:T(8,128)(2,1)S(1)}, bf16[16,7168]{1,0:T(8,128)(2,1)S(1)}, u32[]{:S(2)}, u32[]{:S(2)}) collective-permute-start(bf16[16,7168]{1,0:T(8,128)(2,1)S(1)} %shard_map.148.refs_0_), channel_id=1, source_target_pairs={{0,8},{8,0},{1,9},{9,1},{2,10},{10,2},{3,11},{11,3},{4,12},{12,4},... | collective-permute-start | bytes 688136 | tf_op jit(solution)/shard_map/ppermute | solution.py:553
  96.9 1.9 %collective-permute-start.14 = (f32[16,7168]{1,0:T(8,128)S(1)}, f32[16,7168]{1,0:T(8,128)S(1)}, u32[]{:S(2)}, u32[]{:S(2)}) collective-permute-start(f32[16,7168]{1,0:T(8,128)S(1)} %get-tuple-element.76), channel_id=1, source_target_pairs={{0,8},{8,0},{1,9},{9,1},{2,10},{10,2},{3,11},{11,3},{4,12},{12,4},... | collective-permute-start | bytes 1376264 | tf_op jit(solution)/shard_map/ppermute | solution.py:553

commit v3 on v2

--- a/solution.py
+++ b/solution.py
@@ -103,16 +103,17 @@
     token_ref, sems = refs[-2:]
     copies = []
     for index, (source, target) in enumerate(zip(sources, targets)):
-        copies.append(pltpu.make_async_copy(source, target, sems.at[index]))
+        view = source if source.shape == target.shape else source.at[:, : target.shape[1]]
+        copies.append(pltpu.make_async_copy(view, target, sems.at[index]))
         copies[-1].start()
     token_ref[...] = jnp.zeros_like(token_ref)
     for copy in copies:
         copy.wait()
 
 
-def ahead(beside, weights):
+def ahead(beside, weights, columns=None):
     count = len(weights)
-    shapes = [w.shape for w in weights]
+    shapes = [w.shape if columns is None else (w.shape[0], columns) for w in weights]
     *copied, token = pl.pallas_call(
         functools.partial(ahead_kernel, count),
         in_specs=[pl.BlockSpec(memory_space=pl.ANY)] + [HBM] * count,
@@ -124,31 +125,6 @@
         cost_estimate=cost(0, sum(2 * math.prod(shape) for shape in shapes)),
     )(beside, *[streamed(w) for w in weights])
     return copied, token
-
-
-def part_ahead(beside, weight, first, height, total, held):
-    def kernel(*refs):
-        source, (target, token_ref, sem) = refs[1], refs[-3:]
-        rows = pl.ds(first, height)
-        copy = pltpu.make_async_copy(source.at[rows], target.at[rows], sem)
-        copy.start()
-        token_ref[...] = jnp.zeros_like(token_ref)
-        copy.wait()
-
-    buffers = [] if held is None else [held]
-    return pl.pallas_call(
-        kernel,
-        in_specs=[pl.BlockSpec(memory_space=pl.ANY), HBM] + [VMEM] * len(buffers),
-        out_specs=[VMEM] * 2,
-        out_shape=[
-            pltpu.VMEM((total, weight.shape[1]), BF16),
-            jax.ShapeDtypeStruct((8, LANES), F32),
-        ],
-        scratch_shapes=[pltpu.SemaphoreType.DMA],
-        input_output_aliases={2: 0} if buffers else {},
-        compiler_params=params(1),
-        cost_estimate=cost(0, 2 * height * weight.shape[1]),
-    )(beside, streamed(weight), *buffers)
 
 
 def joined(left, right, token, add):
@@ -280,25 +256,10 @@
     )(left, right, token, gain.reshape(1, QR), hidden, next_gain, w)
 
 
-def put_stats(ref, index, at, stats):
-    heads = stats.shape[0]
-    high, middle, low = parts_of(stats)
-    ref[index, at:, :] = jnp.zeros((STATS, HD), F32)
-    ref[index, at : at + heads, :LANES] = high
-    ref[index, at : at + heads, LANES:] = middle
-    ref[index, at + 8 : at + 8 + heads, :LANES] = low
-
-
-def sent_stats(ref, index, at, heads):
-    high = ref[index, at : at + heads, :LANES]
-    middle = ref[index, at : at + heads, LANES:]
-    return high + middle + ref[index, at + 8 : at + 8 + heads, :LANES]
-
-
 def attend_kernel(codes, place_ref, lengths_ref, token_ref, *refs):
     n_dev = len(codes)
-    pieces, refs = refs[:-8], refs[-8:]
-    keys_ref, values_ref, own_ref, sent_ref, hidden_ref, wide_ref, parts_ref, weights_ref = refs
+    pieces, refs = refs[:-7], refs[-7:]
+    keys_ref, values_ref, out_ref, hidden_ref, wide_ref, parts_ref, weights_ref = refs
     rows, local_pos = keys_ref.shape[:2]
     heads = H // n_dev
     height = wide_ref.shape[0] // n_dev
@@ -338,40 +299,40 @@
         weights_ref[row] = weights.astype(BF16)
         stats = jnp.where(lane == row, top, stats)
         stats = jnp.where(lane == rows + row, mass, stats)
-    half = n_dev // 2
     for row in range(rows):
         weighted = dot(weights_ref[row], values_ref[row])
         for g in range(n_dev):
-            target = own_ref if g < half else parts_ref
-            target[g % half, row * heads : (row + 1) * heads, :] = weighted[
+            parts_ref[me ^ codes[g], row * heads : (row + 1) * heads, :] = weighted[
                 g * heads : (g + 1) * heads, :
             ]
+    high, middle, low = parts_of(stats)
     at = rows * heads
-    for g in range(half):
-        own_ref[g, at:, :] = jnp.zeros((STATS, HD), F32)
-        own_ref[g, at : at + heads, :LANES] = stats[g * heads : (g + 1) * heads]
-        put_stats(parts_ref, g, at, stats[(half + g) * heads : (half + g + 1) * heads])
-    sent_ref[...] = parts_ref[...].astype(BF16)
+    parts_ref[:, at:, :] = jnp.zeros((n_dev, STATS, HD), F32)
+    for g in range(n_dev):
+        span = slice(g * heads, (g + 1) * heads)
+        parts_ref[me ^ codes[g], at : at + heads, :LANES] = high[span]
+        parts_ref[me ^ codes[g], at : at + heads, LANES:] = middle[span]
+        parts_ref[me ^ codes[g], at + 8 : at + 8 + heads, :LANES] = low[span]
+    out_ref[...] = parts_ref[...].astype(BF16)
 
 
 def attend(codes, place, lengths, token, pieces, keys, values):
     rows, local_pos = keys.shape[:2]
     n_dev = len(codes)
-    half = (n_dev // 2, rows * H // n_dev + STATS, HD)
+    height = rows * H // n_dev + STATS
     hidden_width = -(-D // n_dev // HD) * HD
     smem = pl.BlockSpec(memory_space=pltpu.SMEM)
     return pl.pallas_call(
         functools.partial(attend_kernel, codes),
         in_specs=[smem, smem] + [VMEM] * (3 + len(pieces)),
-        out_specs=[VMEM] * 3,
+        out_specs=[VMEM] * 2,
         out_shape=[
-            jax.ShapeDtypeStruct(half, F32),
-            jax.ShapeDtypeStruct(half, BF16),
+            jax.ShapeDtypeStruct((n_dev, height, HD), BF16),
             jax.ShapeDtypeStruct((n_dev, rows + 8, hidden_width), F32),
         ],
         scratch_shapes=[
             pltpu.VMEM((sum(piece.shape[0] for piece in pieces), HD), F32),
-            pltpu.VMEM(half, F32),
+            pltpu.VMEM((n_dev, height, HD), F32),
             pltpu.VMEM((rows, H, local_pos), BF16),
         ],
         compiler_params=params(5),
@@ -379,64 +340,22 @@
     )(place, lengths, token, *pieces, keys, values)
 
 
-def merge_kernel(rows, own_ref, arrived_ref, token_ref, out_ref, sent_ref, wide_ref, parts_ref):
-    count, height, _ = own_ref.shape
-    at = height - STATS
-    heads = at // rows
-    wide_ref[...] = arrived_ref[...].astype(F32)
-    lane = lax.broadcasted_iota(jnp.int32, (heads, LANES), 1)
-    half = count // 2
-    for block in range(count):
-        target = out_ref if block < half else parts_ref
-        here = own_ref[block, at : at + heads, :LANES]
-        there = sent_stats(wide_ref, block, at, heads)
-        stats = jnp.zeros((heads, LANES), F32)
-        for row in range(rows):
-            span = slice(row * heads, (row + 1) * heads)
-            top = jnp.maximum(here[:, row : row + 1], there[:, row : row + 1])
-            left = jnp.exp(here[:, row : row + 1] - top)
-            right = jnp.exp(there[:, row : row + 1] - top)
-            mass = left * here[:, rows + row : rows + row + 1]
-            mass = mass + right * there[:, rows + row : rows + row + 1]
-            total = left * own_ref[block, span, :] + right * wide_ref[block, span, :]
-            target[block % half, span, :] = total
-            stats = jnp.where(lane == row, top, stats)
-            stats = jnp.where(lane == rows + row, mass, stats)
-        if block < half:
-            target[block, at:, :] = jnp.zeros((STATS, HD), F32)
-            target[block, at : at + heads, :LANES] = stats
-        else:
-            put_stats(target, block - half, at, stats)
-    sent_ref[...] = parts_ref[...].astype(BF16)
-
-
-def merge(rows, own, arrived, token):
-    half = (own.shape[0] // 2, *own.shape[1:])
-    return pl.pallas_call(
-        functools.partial(merge_kernel, rows),
-        in_specs=[VMEM] * 3,
-        out_specs=[VMEM] * 2,
-        out_shape=[jax.ShapeDtypeStruct(half, F32), jax.ShapeDtypeStruct(half, BF16)],
-        scratch_shapes=[pltpu.VMEM(own.shape, F32), pltpu.VMEM(half, F32)],
-        compiler_params=params(6),
-        cost_estimate=cost(0, 12 * math.prod(own.shape)),
-    )(own, arrived, token)
-
-
 def project_kernel(
-    own_ref, arrived_ref, token_ref, query_ref, fresh_ref, held_ref, w_hbm, out_ref, sent_ref, *scratch
+    sent_ref, query_ref, fresh_ref, held_ref, w_hbm, out_ref, half_ref, attended_ref, parts_ref, w_ref, sems
 ):
-    attended_ref, wide_ref, w_ref, sems = scratch
-    held, steps = held_ref.shape[0], sems.shape[0]
-    copies = started(w_hbm.at[held : held + w_ref.shape[0]], w_ref, sems, steps, 1)
+    n_dev = sent_ref.shape[0]
+    held, width = held_ref.shape[1], D // 8
+    copies = started(w_hbm.at[:, held:], w_ref, sems, sems.shape[0], 1)
     rows = fresh_ref.shape[0]
-    at = own_ref.shape[1] - STATS
-    heads = at // rows
+    heads = H // n_dev
     query = query_ref[...].astype(F32)
-    wide_ref[...] = arrived_ref[...].astype(F32)
-    parts = [
-        (own_ref, own_ref[0, at : at + heads, :LANES]),
-        (wide_ref, sent_stats(wide_ref, 0, at, heads)),
+    parts_ref[...] = sent_ref[...].astype(F32)
+    at = rows * heads
+    stats = [
+        parts_ref[d, at : at + heads, :LANES]
+        + parts_ref[d, at : at + heads, LANES:]
+        + parts_ref[d, at + 8 : at + 8 + heads, :LANES]
+        for d in range(n_dev)
     ]
     for row in range(rows):
         span = slice(row * heads, (row + 1) * heads)
@@ -444,48 +363,51 @@
         value = fresh_ref[row : row + 1, HD:]
         score = jnp.sum(query[span] * key, axis=1, keepdims=True) * (1.0 / math.sqrt(HD))
         highest = score
-        for _, stats in parts:
-            highest = jnp.maximum(highest, stats[:, row : row + 1])
+        for d in range(n_dev):
+            highest = jnp.maximum(highest, stats[d][:, row : row + 1])
         weight = jnp.exp(score - highest)
         mass = weight
         total = weight.astype(BF16).astype(F32) * value
-        for ref, stats in parts:
-            factor = jnp.exp(stats[:, row : row + 1] - highest)
-            mass = mass + factor * stats[:, rows + row : rows + row + 1]
-            total = total + factor * ref[0, span, :]
+        for d in range(n_dev):
+            factor = jnp.exp(stats[d][:, row : row + 1] - highest)
+            mass = mass + factor * stats[d][:, rows + row : rows + row + 1]
+            total = total + factor * parts_ref[d, span, :]
         attended = total / mass
         for head in range(heads):
             attended_ref[row : row + 1, head * HD : (head + 1) * HD] = attended[
                 head : head + 1, :
             ]
-    width = D // steps
+
     attended = attended_ref[...].astype(BF16)
-    for step, copy in enumerate(copies):
-        columns = slice(step * width, (step + 1) * width)
-        total = dot(attended[:, :held], held_ref[:, columns])
-        copy.wait()
-        total = total + dot(attended[:, held:], w_ref[:, columns])
+    for first in range(0, D, width):
+        columns = slice(first, first + width)
+        if first < held:
+            total = dot(attended, held_ref[:, columns])
+        else:
+            copies[(first - held) // width].wait()
+            total = dot(attended, w_ref[:, first - held : first - held + width])
         out_ref[:, columns] = total
-        sent_ref[:, columns] = total.astype(BF16)
-
-
-def project(own, arrived, token, query, fresh, held, w):
+        half_ref[:, columns] = total.astype(BF16)
+
+
+def project(parts, query, fresh, held, w):
     rows = fresh.shape[0]
     depth = w.shape[0]
+    width = D // 8
     return pl.pallas_call(
         project_kernel,
-        in_specs=[VMEM] * 6 + [HBM],
+        in_specs=[VMEM] * 4 + [HBM],
         out_specs=[VMEM] * 2,
         out_shape=[jax.ShapeDtypeStruct((rows, D), F32), jax.ShapeDtypeStruct((rows, D), BF16)],
         scratch_shapes=[
             pltpu.VMEM((rows, depth), F32),
-            pltpu.VMEM(own.shape, F32),
-            pltpu.VMEM((depth - held.shape[0], D), BF16),
-            pltpu.SemaphoreType.DMA((8,)),
+            pltpu.VMEM(parts.shape, F32),
+            pltpu.VMEM((depth, D - held.shape[1]), BF16),
+            pltpu.SemaphoreType.DMA(((D - held.shape[1]) // width,)),
         ],
-        compiler_params=params(16),
+        compiler_params=params(28),
         cost_estimate=cost(2 * rows * depth * D, 2 * depth * D),
-    )(own, arrived, token, query, fresh, held, streamed(w))
+    )(parts, query, fresh, held, streamed(w))
 
 
 def ffn_kernel(*refs):
@@ -584,10 +506,8 @@
         (copied["query"],), token = ahead(value, [w_query])
         return token
 
-
-    def copy_out(first, height, total, value):
-        held = copied.get("out")
-        copied["out"], token = part_ahead(value, w_out, first, height, total, held)
+    def copy_out(value):
+        (copied["out"],), token = ahead(value, [w_out], D // 8 * 3)
         return token
 
     def copy_caches(value):
@@ -599,12 +519,7 @@
         return token
 
     steps = n_dev.bit_length() - 1
-    jobs = [copy_query] + [None] * (2 * steps - 2) + [copy_caches]
-    block = w_out.shape[0] // 16
-    heights = [4 * block, 3 * block, 3 * block] + [0] * (steps - 3)
-    for step, height in enumerate(heights):
-        first = sum(heights[:step])
-        jobs.append(functools.partial(copy_out, first, height, sum(heights)) if height else None)
+    jobs = [copy_query] + [None] * (2 * steps - 3) + [copy_caches, copy_out]
     for name, weight in (("gate", w_gate.T), ("up", w_up.T), ("down", w_down)):
         jobs.append(functools.partial(copy_ffn, name, weight))
     jobs += [None] * (steps - 3)
@@ -633,17 +548,11 @@
         bit //= 2
         if bit:
             held = joined(held, arrived, token, False)
-    own, sent, hidden = attend(
+    parts, hidden = attend(
         codes, place, lengths, token, [held, arrived], *copied["caches"]
     )
-
-    bit = 1
-    while bit < n_dev:
-        arrived, token = exchanged(sent, bit)
-        bit *= 2
-        if bit < n_dev:
-            own, sent = merge(rows, own, arrived, token)
-    attn, sent = project(own, arrived, token, query, fresh, copied["out"], w_out)
+    parts = lax.all_to_all(parts, DEV, 0, 0)
+    attn, sent = project(parts, query, fresh, copied["out"], w_out)
 
     bit = 1
     while bit < n_dev:

time: 115 us -> 109 us (0.948)
  starting transfers between devices: 29.4 us -> 17.1 us
  blocking collectives: 15.5 us -> 27.1 us
  Pallas kernels: 46.5 us -> 40.9 us
  waiting for transfers between devices: 22 us -> 19.9 us
  local copies, waits for them, and re-layouts: 0.73 us -> 2.34 us
    all_to_all x0 -> x1, blocking collectives: none -> 13.9 us  [local(): parts = lax.all_to_all(parts, DEV, 0, 0)]
    ppermute x15 -> x12, starting transfers between devices: 29.4 us -> 17.1 us  [swapped(): return lax.ppermute(value, axis, [(i, i ^ bit) for i in range(size)])]
    pallas_call x6 -> x1, Pallas kernels: 17.3 us -> 7.3 us  [project(): pl.pallas_call(project_kernel, in_specs=[VMEM] * 4 + [HBM], out_specs=[VM...]
    pallas_call x5 -> x6, Pallas kernels: 15.7 us -> 20 us  [ahead(): pl.pallas_call(functools.partial(ahead_kernel, count), in_specs=[pl.Block...]
    all_to_all x1, blocking collectives: 15.5 us -> 13.2 us  [local(): ffn_term = lax.all_to_all(ffn_term, (FAR, DEV), 0, 0)]
    ppermute x15 -> x12, waiting for transfers between devices: 22 us -> 19.9 us  [swapped(): return lax.ppermute(value, axis, [(i, i ^ bit) for i in range(size)])]
    unnamed x8 -> x12, local copies, waits for them, and re-layouts: 0.73 us -> 2.34 us
  transfers between devices with their start and end apart: 15 -> 12, of which waited for: 11 -> 10; matrix products, arithmetic and copies ran while one was open for 0% -> 0% of each run, Pallas kernels for 21% -> 18%
where the time goes in v3:
time: 109 us; the launch traced here: 108 us
  Pallas kernels  40.9 us (38%)
  blocking collectives  27.1 us (25%)
  waiting for transfers between devices  19.9 us (18%)
  starting transfers between devices  17.1 us (16%)
  local copies, waits for them, and re-layouts  2.34 us (2%)
    pallas_call x6, Pallas kernels, ahead(): pl.pallas_call(functools.partial(ahead_kernel, count), in_specs=[pl.Block...  20 us
    ppermute x12, waiting for transfers between devices, swapped(): return lax.ppermute(value, axis, [(i, i ^ bit) for i in range(size)])  19.9 us
    ppermute x12, starting transfers between devices, swapped(): return lax.ppermute(value, axis, [(i, i ^ bit) for i in range(size)])  17.1 us
    all_to_all x1, blocking collectives, local(): parts = lax.all_to_all(parts, DEV, 0, 0)  13.9 us
    all_to_all x1, blocking collectives, local(): ffn_term = lax.all_to_all(ffn_term, (FAR, DEV), 0, 0)  13.2 us
    pallas_call x1, Pallas kernels, project(): pl.pallas_call(project_kernel, in_specs=[VMEM] * 4 + [HBM], out_specs=[VM...  7.3 us
    pallas_call x1, Pallas kernels, ffn(): pl.pallas_call(ffn_kernel, in_specs=[VMEM] * (len(pieces) + 4), out_specs...  7 us
    pallas_call x1, Pallas kernels, latent_part(): pl.pallas_call(latent_kernel, in_specs=[VMEM, HBM, HBM], out_specs=VMEM,...  3.07 us
  transfers between devices with their start and end apart: 12, of which 10 were waited for; matrix products, arithmetic and copies ran while one was open for 0% of the time, Pallas kernels for 18%

profile of v3, /device:TPU:0, one launch (start us, length us, event | category | flops | bytes accessed | tf_op | source)
XLA Modules:
  0.0 108.2 jit_solution(17170034023675451176)
XLA Ops:
  0.0 0.0 copy-start.2
  0.0 0.7 copy-done.2
  0.7 0.0 copy-start.3
  0.7 0.0 copy-start.4
  0.7 3.1 %shard_map.127.refs_0_.left_ref = f32[8,2688]{1,0:T(8,128)S(1)} custom-call(bf16[8,896]{1,0:T(8,128)(2,1)S(1)} %copy-done.2, f32[896]{0:T(1024)} %gain_hbm.1, bf16[896,2560]{1,0:T(8,128)(2,1)} %w_hbm.2), custom_call_target="tpu_custom_call" | custom-call | flops 36700160 | bytes 4587520 | tf_op jit(solution)/shard_map/pallas_call | solution.py:85
  3.8 3.0 %collective-permute-start = (f32[8,2688]{1,0:T(8,128)S(1)}, f32[8,2688]{1,0:T(8,128)S(1)}, u32[]{:S(2)}, u32[]{:S(2)}) collective-permute-start(f32[8,2688]{1,0:T(8,128)S(1)} %shard_map.127.refs_0_.left_ref), channel_id=1, source_target_pairs={{0,1},{1,0},{2,3},{3,2},{4,5},{5,4},{6,7},{7,6},{8,9},{9,8},{10,11... | collective-permute-start | bytes 258056 | tf_op jit(solution)/shard_map/ppermute | solution.py:475
  6.8 3.4 %shard_map.128 = (bf16[2048,2048]{1,0:T(8,128)(2,1)S(1)}, f32[8,128]{1,0:T(8,128)S(1)}) custom-call(f32[8,2688]{1,0:T(8,128)S(1)} %shard_map.127.refs_0_.left_ref, bf16[2048,2048]{1,0:T(8,128)(2,1)} %refs_1_.4), custom_call_target="tpu_custom_call" | custom-call | bytes 8388608 | tf_op jit(solution)/shard_map/pallas_call | solution.py:117
  10.2 0.0 collective-permute-done.right_ref
  10.3 1.6 %collective-permute-start.1 = (f32[8,2688]{1,0:T(8,128)S(1)}, f32[8,2688]{1,0:T(8,128)S(1)}, u32[]{:S(2)}, u32[]{:S(2)}) collective-permute-start(f32[8,2688]{1,0:T(8,128)S(1)} %shard_map.129.left_ref), channel_id=1, source_target_pairs={{0,2},{1,3},{2,0},{3,1},{4,6},{5,7},{6,4},{7,5},{8,10},{9,11},{10,... | collective-permute-start | bytes 258056 | tf_op jit(solution)/shard_map/ppermute | solution.py:475
  11.9 2.9 %collective-permute-done.1.right_ref = f32[8,2688]{1,0:T(8,128)S(1)} collective-permute-done((f32[8,2688]{1,0:T(8,128)S(1)}, f32[8,2688]{1,0:T(8,128)S(1)}, u32[]{:S(2)}, u32[]{:S(2)}) %collective-permute-start.1) | collective-permute-done | bytes 86048 | tf_op jit(solution)/shard_map/ppermute | solution.py:475
  14.8 2.7 %collective-permute-start.2 = (f32[8,2688]{1,0:T(8,128)S(1)}, f32[8,2688]{1,0:T(8,128)S(1)}, u32[]{:S(2)}, u32[]{:S(2)}) collective-permute-start(f32[8,2688]{1,0:T(8,128)S(1)} %shard_map.130.left_ref), channel_id=1, source_target_pairs={{0,4},{1,5},{2,6},{3,7},{4,0},{5,1},{6,2},{7,3},{8,12},{9,13},{10,... | collective-permute-start | bytes 258056 | tf_op jit(solution)/shard_map/ppermute | solution.py:475
  17.5 2.8 %collective-permute-done.2.right_ref = f32[8,2688]{1,0:T(8,128)S(1)} collective-permute-done((f32[8,2688]{1,0:T(8,128)S(1)}, f32[8,2688]{1,0:T(8,128)S(1)}, u32[]{:S(2)}, u32[]{:S(2)}) %collective-permute-start.2) | collective-permute-done | bytes 86048 | tf_op jit(solution)/shard_map/ppermute | solution.py:475
  20.3 0.0 copy-done.3
  20.3 0.0 copy-done.4
  20.3 1.4 %shard_map.131 = (bf16[112,256]{1,0:T(8,128)(2,1)S(1)}, f32[8,512]{1,0:T(8,128)S(1)}) custom-call(f32[8,2688]{1,0:T(8,128)S(1)} %shard_map.130.left_ref, f32[8,2688]{1,0:T(8,128)S(1)} %collective-permute-done.2.right_ref, f32[8,128]{1,0:T(8,128)S(1)} %get-tuple-element.32.token_ref, f32[1,2048]{1,0:T(1,128)S(1)} %bitcast.5, bf16[8,896]{1,0:T(8,128)(2,1)S(1)} %copy-done.2, ...), custom_call_target="tpu_custom_call" | custom-call | flops 67108864 | bytes 8388608 | tf_op jit(solution)/shard_map/pallas_call | solution.py:245
  21.6 2.7 %collective-permute-start.3 = (bf16[112,256]{1,0:T(8,128)(2,1)S(1)}, bf16[112,256]{1,0:T(8,128)(2,1)S(1)}, u32[]{:S(2)}, u32[]{:S(2)}) collective-permute-start(bf16[112,256]{1,0:T(8,128)(2,1)S(1)} %get-tuple-element.34.left_ref.query_ref), channel_id=1, source_target_pairs={{0,4},{1,5},{2,6},{3,7},{4,0},{5,1},{6,2},{7,3},{8,12},{9,13},{10,... | collective-permute-start | bytes 172040 | tf_op jit(solution)/shard_map/ppermute | solution.py:475
  24.4 2.5 %collective-permute-done.3.right_ref = bf16[112,256]{1,0:T(8,128)(2,1)S(1)} collective-permute-done((bf16[112,256]{1,0:T(8,128)(2,1)S(1)}, bf16[112,256]{1,0:T(8,128)(2,1)S(1)}, u32[]{:S(2)}, u32[]{:S(2)}) %collective-permute-start.3) | collective-permute-done | bytes 57376 | tf_op jit(solution)/shard_map/ppermute | solution.py:475
  26.9 2.1 %collective-permute-start.4 = (bf16[224,256]{1,0:T(8,128)(2,1)S(1)}, bf16[224,256]{1,0:T(8,128)(2,1)S(1)}, u32[]{:S(2)}, u32[]{:S(2)}) collective-permute-start(bf16[224,256]{1,0:T(8,128)(2,1)S(1)} %shard_map.132.refs_0_.left_ref), channel_id=1, source_target_pairs={{0,2},{1,3},{2,0},{3,1},{4,6},{5,7},{6,4},{7,5},{8,10},{9,11},{10,... | collective-permute-start | bytes 344072 | tf_op jit(solution)/shard_map/ppermute | solution.py:475
  29.0 2.2 %shard_map.133 = (bf16[8,512,256]{2,1,0:T(8,128)(2,1)S(1)}, bf16[8,512,256]{2,1,0:T(8,128)(2,1)S(1)}, f32[8,128]{1,0:T(8,128)S(1)}) custom-call(bf16[224,256]{1,0:T(8,128)(2,1)S(1)} %shard_map.132.refs_0_.left_ref, bf16[8,512,256]{2,1,0:T(8,128)(2,1)} %refs_1_.5, bf16[8,512,256]{2,1,0:T(8,128)(2,1)} %refs_2_.1), custom_call_target="tpu_custom_call" | custom-call | bytes 4194304 | tf_op jit(solution)/shard_map/pallas_call | solution.py:117
  31.3 0.0 copy-start
  31.3 1.3 %copy-done = bf16[8,512,256]{2,1,0:T(8,128)(2,1)} copy-done((bf16[8,512,256]{2,1,0:T(8,128)(2,1)}, bf16[8,512,256]{2,1,0:T(8,128)(2,1)S(1)}, u32[]{:S(2)}) %copy-start) | copy-done | bytes 2097176
  32.6 0.0 collective-permute-done.4.right_ref
  32.6 1.6 %collective-permute-start.5 = (bf16[448,256]{1,0:T(8,128)(2,1)S(1)}, bf16[448,256]{1,0:T(8,128)(2,1)S(1)}, u32[]{:S(2)}, u32[]{:S(2)}) collective-permute-start(bf16[448,256]{1,0:T(8,128)(2,1)S(1)} %shard_map.134.refs_0_), channel_id=1, source_target_pairs={{0,1},{1,0},{2,3},{3,2},{4,5},{5,4},{6,7},{7,6},{8,9},{9,8},{10,11... | collective-permute-start | bytes 688136 | tf_op jit(solution)/shard_map/ppermute | solution.py:475
  34.3 0.0 copy-start.1
  34.3 0.0 copy-start.5
  34.3 4.3 %shard_map.135 = (bf16[2048,2688]{1,0:T(8,128)(2,1)S(1)}, f32[8,128]{1,0:T(8,128)S(1)}) custom-call(bf16[448,256]{1,0:T(8,128)(2,1)S(1)} %shard_map.134.refs_0_, bf16[2048,7168]{1,0:T(8,128)(2,1)} %w_hbm.3), custom_call_target="tpu_custom_call" | custom-call | bytes 11010048 | tf_op jit(solution)/shard_map/pallas_call | solution.py:117
  38.6 0.1 collective-permute-done.5.refs_1_
  38.7 0.3 copy-done.1
  39.0 0.0 copy-done.5
  39.0 1.8 %shard_map.136 = (bf16[8,80,256]{2,1,0:T(8,128)(2,1)S(1)}, f32[8,16,1024]{2,1,0:T(8,128)S(1)}) custom-call(s32[1]{0:T(128)} %bitcast.place_ref, s32[8]{0:T(128)S(1)} %copy-done.5, f32[8,128]{1,0:T(8,128)S(1)} %get-tuple-element.36.token_ref, bf16[448,256]{1,0:T(8,128)(2,1)S(1)} %shard_map.134.refs_0_, bf16[448,256]{1,0:T(8,128)(2,1)S(1)} %collective-permute-done.5.refs_1_, ...), custom_call_target="tpu_custom_call" | custom-call | flops 268435456 | bytes 4194304 | tf_op jit(solution)/shard_map/pallas_call | solution.py:325
  40.8 13.9 %all_to_all.10.sent_ref = bf16[8,80,256]{2,1,0:T(8,128)(2,1)S(1)} all-to-all(bf16[8,80,256]{2,1,0:T(8,128)(2,1)S(1)} %get-tuple-element.39), channel_id=1, replica_groups=mesh['far'=2,'core'=2,'dev'=8] {'dev'}, dimensions={0} | all-to-all | bytes 655360 | tf_op jit(solution)/shard_map/all_to_all | solution.py:554
  54.7 7.3 %shard_map.137 = (f32[8,7168]{1,0:T(8,128)S(1)}, bf16[8,7168]{1,0:T(8,128)(2,1)S(1)}) custom-call(bf16[8,80,256]{2,1,0:T(8,128)(2,1)S(1)} %all_to_all.10.sent_ref, bf16[112,256]{1,0:T(8,128)(2,1)S(1)} %get-tuple-element.34.left_ref.query_ref, f32[8,512]{1,0:T(8,128)S(1)} %get-tuple-element.40.fresh_ref, bf16[2048,2688]{1,0:T(8,128)(2,1)S(1)} %get-tuple-element.41.held_ref, ...), custom_call_target="tpu_custom_call" | custom-call | flops 234881024 | bytes 29360128 | tf_op jit(solution)/shard_map/pallas_call | solution.py:397
  62.1 0.5 collective-permute-start.6
  62.6 3.4 %shard_map.138 = (bf16[576,7168]{1,0:T(8,128)(2,1)S(1)}, f32[8,128]{1,0:T(8,128)S(1)}) custom-call(bf16[8,7168]{1,0:T(8,128)(2,1)S(1)} %get-tuple-element.43.refs_0_, bf16[576,7168]{1,0:T(8,128)(2,1)} %bitcast.6), custom_call_target="tpu_custom_call" | custom-call | bytes 8257536 | tf_op jit(solution)/shard_map/pallas_call | solution.py:117
  65.9 1.0 collective-permute-done.6.arrived_ref
  66.9 0.3 collective-permute-start.7
  67.3 3.4 %shard_map.140 = (bf16[576,7168]{1,0:T(8,128)(2,1)S(1)}, f32[8,128]{1,0:T(8,128)S(1)}) custom-call(bf16[8,7168]{1,0:T(8,128)(2,1)S(1)} %get-tuple-element.46.refs_0_, bf16[576,7168]{1,0:T(8,128)(2,1)} %bitcast.7), custom_call_target="tpu_custom_call" | custom-call | bytes 8257536 | tf_op jit(solution)/shard_map/pallas_call | solution.py:117
  70.7 1.2 %collective-permute-done.7.arrived_ref = bf16[8,7168]{1,0:T(8,128)(2,1)S(1)} collective-permute-done((bf16[8,7168]{1,0:T(8,128)(2,1)S(1)}, bf16[8,7168]{1,0:T(8,128)(2,1)S(1)}, u32[]{:S(2)}, u32[]{:S(2)}) %collective-permute-start.7) | collective-permute-done | bytes 114720 | tf_op jit(solution)/shard_map/ppermute | solution.py:475
  71.8 0.6 collective-permute-start.8
  72.5 3.4 %shard_map.142 = (bf16[576,7168]{1,0:T(8,128)(2,1)S(1)}, f32[8,128]{1,0:T(8,128)S(1)}) custom-call(bf16[8,7168]{1,0:T(8,128)(2,1)S(1)} %get-tuple-element.49.refs_0_, bf16[576,7168]{1,0:T(8,128)(2,1)} %refs_1_.7), custom_call_target="tpu_custom_call" | custom-call | bytes 8257536 | tf_op jit(solution)/shard_map/pallas_call | solution.py:117
  75.8 3.0 %collective-permute-done.8.arrived_ref = bf16[8,7168]{1,0:T(8,128)(2,1)S(1)} collective-permute-done((bf16[8,7168]{1,0:T(8,128)(2,1)S(1)}, bf16[8,7168]{1,0:T(8,128)(2,1)S(1)}, u32[]{:S(2)}, u32[]{:S(2)}) %collective-permute-start.8) | collective-permute-done | bytes 114720 | tf_op jit(solution)/shard_map/ppermute | solution.py:475
  78.8 0.2 shard_map.143
  79.0 1.6 %collective-permute-start.9 = (bf16[8,7168]{1,0:T(8,128)(2,1)S(1)}, bf16[8,7168]{1,0:T(8,128)(2,1)S(1)}, u32[]{:S(2)}, u32[]{:S(2)}) collective-permute-start(bf16[8,7168]{1,0:T(8,128)(2,1)S(1)} %get-tuple-element.53.left_ref), channel_id=1, source_target_pairs={{0,16},{16,0},{1,17},{17,1},{2,18},{18,2},{3,19},{19,3},{4,20},{20... | collective-permute-start | bytes 344072 | tf_op jit(solution)/shard_map/ppermute | solution.py:475
  80.5 3.3 %collective-permute-done.9.right_ref = bf16[8,7168]{1,0:T(8,128)(2,1)S(1)} collective-permute-done((bf16[8,7168]{1,0:T(8,128)(2,1)S(1)}, bf16[8,7168]{1,0:T(8,128)(2,1)S(1)}, u32[]{:S(2)}, u32[]{:S(2)}) %collective-permute-start.9) | collective-permute-done | bytes 114720 | tf_op jit(solution)/shard_map/ppermute | solution.py:475
  83.9 0.1 collective-permute-start.10
  84.0 1.5 %collective-permute-done.10.refs_1_ = bf16[16,7168]{1,0:T(8,128)(2,1)S(1)} collective-permute-done((bf16[16,7168]{1,0:T(8,128)(2,1)S(1)}, bf16[16,7168]{1,0:T(8,128)(2,1)S(1)}, u32[]{:S(2)}, u32[]{:S(2)}) %collective-permute-start.10) | collective-permute-done | bytes 229408 | tf_op jit(solution)/shard_map/ppermute | solution.py:475
  85.4 7.0 %shard_map.145 = (f32[16,7168]{1,0:T(8,128)S(1)}, f32[16,7168]{1,0:T(8,128)S(1)}) custom-call(bf16[16,7168]{1,0:T(8,128)(2,1)S(1)} %shard_map.144.refs_0_, bf16[16,7168]{1,0:T(8,128)(2,1)S(1)} %collective-permute-done.10.refs_1_, f32[8,128]{1,0:T(8,128)S(1)} %get-tuple-element.50.token_ref.refs_2_, bf16[576,7168]{1,0:T(8,128)(2,1)S(1)} %get-tuple-element.54.refs_3_, ...), custom_call_target="tpu_custom_call" | custom-call | flops 792723456 | bytes 24772608 | tf_op jit(solution)/shard_map/pallas_call | solution.py:439
  92.4 0.2 collective-permute-start.11
  92.6 1.7 %collective-permute-done.11.arrived_ref = f32[16,7168]{1,0:T(8,128)S(1)} collective-permute-done((f32[16,7168]{1,0:T(8,128)S(1)}, f32[16,7168]{1,0:T(8,128)S(1)}, u32[]{:S(2)}, u32[]{:S(2)}) %collective-permute-start.11) | collective-permute-done | bytes 458784 | tf_op jit(solution)/shard_map/ppermute | solution.py:475
  94.3 0.1 shard_map.146
  94.4 13.2 %all_to_all.11 = bf16[16,8,896]{2,1,0:T(8,128)(2,1)S(1)} all-to-all(bf16[16,8,896]{2,1,0:T(8,128)(2,1)S(1)} %shard_map.146), channel_id=1, replica_groups=mesh['far'=2,'core'=2,'dev'=8] {'far','dev'}, dimensions={0} | all-to-all | bytes 458752 | tf_op jit(solution)/shard_map/all_to_all | solution.py:572
  107.6 0.6 add.3
  (8 shorter events, 0.2 us)
Async XLA Ops:
  0.0 0.7 copy-start.2
  0.7 19.6 %copy-start.3 = (f32[2048]{0:T(1024)S(1)}, f32[2048]{0:T(1024)}, u32[]{:S(2)}) copy-start(f32[2048]{0:T(1024)} %param.16) | copy-start | bytes 24580
  0.7 19.6 %copy-start.4 = (f32[896]{0:T(1024)S(1)}, f32[896]{0:T(1024)}, u32[]{:S(2)}) copy-start(f32[896]{0:T(1024)} %next_ref.1) | copy-start | bytes 10756
  3.8 6.4 %collective-permute-start = (f32[8,2688]{1,0:T(8,128)S(1)}, f32[8,2688]{1,0:T(8,128)S(1)}, u32[]{:S(2)}, u32[]{:S(2)}) collective-permute-start(f32[8,2688]{1,0:T(8,128)S(1)} %shard_map.127.refs_0_.left_ref), channel_id=1, source_target_pairs={{0,1},{1,0},{2,3},{3,2},{4,5},{5,4},{6,7},{7,6},{8,9},{9,8},{10,11... | collective-permute-start | bytes 258056 | tf_op jit(solution)/shard_map/ppermute | solution.py:475
  10.3 4.6 %collective-permute-start.1 = (f32[8,2688]{1,0:T(8,128)S(1)}, f32[8,2688]{1,0:T(8,128)S(1)}, u32[]{:S(2)}, u32[]{:S(2)}) collective-permute-start(f32[8,2688]{1,0:T(8,128)S(1)} %shard_map.129.left_ref), channel_id=1, source_target_pairs={{0,2},{1,3},{2,0},{3,1},{4,6},{5,7},{6,4},{7,5},{8,10},{9,11},{10,... | collective-permute-start | bytes 258056 | tf_op jit(solution)/shard_map/ppermute | solution.py:475
  14.8 5.4 %collective-permute-start.2 = (f32[8,2688]{1,0:T(8,128)S(1)}, f32[8,2688]{1,0:T(8,128)S(1)}, u32[]{:S(2)}, u32[]{:S(2)}) collective-permute-start(f32[8,2688]{1,0:T(8,128)S(1)} %shard_map.130.left_ref), channel_id=1, source_target_pairs={{0,4},{1,5},{2,6},{3,7},{4,0},{5,1},{6,2},{7,3},{8,12},{9,13},{10,... | collective-permute-start | bytes 258056 | tf_op jit(solution)/shard_map/ppermute | solution.py:475
  21.6 5.2 %collective-permute-start.3 = (bf16[112,256]{1,0:T(8,128)(2,1)S(1)}, bf16[112,256]{1,0:T(8,128)(2,1)S(1)}, u32[]{:S(2)}, u32[]{:S(2)}) collective-permute-start(bf16[112,256]{1,0:T(8,128)(2,1)S(1)} %get-tuple-element.34.left_ref.query_ref), channel_id=1, source_target_pairs={{0,4},{1,5},{2,6},{3,7},{4,0},{5,1},{6,2},{7,3},{8,12},{9,13},{10,... | collective-permute-start | bytes 172040 | tf_op jit(solution)/shard_map/ppermute | solution.py:475
  26.9 5.7 %collective-permute-start.4 = (bf16[224,256]{1,0:T(8,128)(2,1)S(1)}, bf16[224,256]{1,0:T(8,128)(2,1)S(1)}, u32[]{:S(2)}, u32[]{:S(2)}) collective-permute-start(bf16[224,256]{1,0:T(8,128)(2,1)S(1)} %shard_map.132.refs_0_.left_ref), channel_id=1, source_target_pairs={{0,2},{1,3},{2,0},{3,1},{4,6},{5,7},{6,4},{7,5},{8,10},{9,11},{10,... | collective-permute-start | bytes 344072 | tf_op jit(solution)/shard_map/ppermute | solution.py:475
  31.3 1.3 %copy-start = (bf16[8,512,256]{2,1,0:T(8,128)(2,1)}, bf16[8,512,256]{2,1,0:T(8,128)(2,1)S(1)}, u32[]{:S(2)}) copy-start(bf16[8,512,256]{2,1,0:T(8,128)(2,1)S(1)} %get-tuple-element.38.refs_3_) | copy-start | bytes 6291460
  32.6 6.1 %collective-permute-start.5 = (bf16[448,256]{1,0:T(8,128)(2,1)S(1)}, bf16[448,256]{1,0:T(8,128)(2,1)S(1)}, u32[]{:S(2)}, u32[]{:S(2)}) collective-permute-start(bf16[448,256]{1,0:T(8,128)(2,1)S(1)} %shard_map.134.refs_0_), channel_id=1, source_target_pairs={{0,1},{1,0},{2,3},{3,2},{4,5},{5,4},{6,7},{7,6},{8,9},{9,8},{10,11... | collective-permute-start | bytes 688136 | tf_op jit(solution)/shard_map/ppermute | solution.py:475
  34.3 4.7 %copy-start.1 = (bf16[8,512,256]{2,1,0:T(8,128)(2,1)S(1)}, bf16[8,512,256]{2,1,0:T(8,128)(2,1)}, u32[]{:S(2)}) copy-start(bf16[8,512,256]{2,1,0:T(8,128)(2,1)} %copy-done) | copy-start | bytes 6291460
  34.3 4.7 %copy-start.5 = (s32[8]{0:T(128)S(1)}, s32[8]{0:T(128)}, u32[]{:S(2)}) copy-start(s32[8]{0:T(128)} %lengths_ref.1) | copy-start | bytes 100
  62.1 4.9 %collective-permute-start.6 = (bf16[8,7168]{1,0:T(8,128)(2,1)S(1)}, bf16[8,7168]{1,0:T(8,128)(2,1)S(1)}, u32[]{:S(2)}, u32[]{:S(2)}) collective-permute-start(bf16[8,7168]{1,0:T(8,128)(2,1)S(1)} %get-tuple-element.43.refs_0_), channel_id=1, source_target_pairs={{0,1},{1,0},{2,3},{3,2},{4,5},{5,4},{6,7},{7,6},{8,9},{9,8},{10,11... | collective-permute-start | bytes 344072 | tf_op jit(solution)/shard_map/ppermute | solution.py:475
  66.9 4.9 %collective-permute-start.7 = (bf16[8,7168]{1,0:T(8,128)(2,1)S(1)}, bf16[8,7168]{1,0:T(8,128)(2,1)S(1)}, u32[]{:S(2)}, u32[]{:S(2)}) collective-permute-start(bf16[8,7168]{1,0:T(8,128)(2,1)S(1)} %get-tuple-element.46.refs_0_), channel_id=1, source_target_pairs={{0,2},{1,3},{2,0},{3,1},{4,6},{5,7},{6,4},{7,5},{8,10},{9,11},{10,... | collective-permute-start | bytes 344072 | tf_op jit(solution)/shard_map/ppermute | solution.py:475
  71.8 7.0 %collective-permute-start.8 = (bf16[8,7168]{1,0:T(8,128)(2,1)S(1)}, bf16[8,7168]{1,0:T(8,128)(2,1)S(1)}, u32[]{:S(2)}, u32[]{:S(2)}) collective-permute-start(bf16[8,7168]{1,0:T(8,128)(2,1)S(1)} %get-tuple-element.49.refs_0_), channel_id=1, source_target_pairs={{0,4},{1,5},{2,6},{3,7},{4,0},{5,1},{6,2},{7,3},{8,12},{9,13},{10,... | collective-permute-start | bytes 344072 | tf_op jit(solution)/shard_map/ppermute | solution.py:475
  79.0 4.9 %collective-permute-start.9 = (bf16[8,7168]{1,0:T(8,128)(2,1)S(1)}, bf16[8,7168]{1,0:T(8,128)(2,1)S(1)}, u32[]{:S(2)}, u32[]{:S(2)}) collective-permute-start(bf16[8,7168]{1,0:T(8,128)(2,1)S(1)} %get-tuple-element.53.left_ref), channel_id=1, source_target_pairs={{0,16},{16,0},{1,17},{17,1},{2,18},{18,2},{3,19},{19,3},{4,20},{20... | collective-permute-start | bytes 344072 | tf_op jit(solution)/shard_map/ppermute | solution.py:475
  83.9 1.6 %collective-permute-start.10 = (bf16[16,7168]{1,0:T(8,128)(2,1)S(1)}, bf16[16,7168]{1,0:T(8,128)(2,1)S(1)}, u32[]{:S(2)}, u32[]{:S(2)}) collective-permute-start(bf16[16,7168]{1,0:T(8,128)(2,1)S(1)} %shard_map.144.refs_0_), channel_id=1, source_target_pairs={{0,8},{8,0},{1,9},{9,1},{2,10},{10,2},{3,11},{11,3},{4,12},{12,4},... | collective-permute-start | bytes 688136 | tf_op jit(solution)/shard_map/ppermute | solution.py:475
  92.4 1.9 %collective-permute-start.11 = (f32[16,7168]{1,0:T(8,128)S(1)}, f32[16,7168]{1,0:T(8,128)S(1)}, u32[]{:S(2)}, u32[]{:S(2)}) collective-permute-start(f32[16,7168]{1,0:T(8,128)S(1)} %get-tuple-element.58), channel_id=1, source_target_pairs={{0,8},{8,0},{1,9},{9,1},{2,10},{10,2},{3,11},{11,3},{4,12},{12,4},... | collective-permute-start | bytes 1376264 | tf_op jit(solution)/shard_map/ppermute | solution.py:475

commit v4 on v3

--- a/solution.py
+++ b/solution.py
@@ -411,24 +411,24 @@
 
 
 def ffn_kernel(*refs):
-    pieces, refs = refs[:-7], refs[-7:]
-    token_ref, gate_ref, up_ref, down_ref, own_ref, other_ref, act_ref = refs
-    half = own_ref.shape[0]
-    rows = jnp.concatenate([piece[...] for piece in pieces], axis=0)
-    units = gate_ref.shape[0]
-    block = 144
-    for step in range(units // block):
-        span = slice(step * block, (step + 1) * block)
-        gate = dot(gate_ref[span, :], rows, 1, 1)
-        up = dot(up_ref[span, :], rows, 1, 1)
-        act_ref[span, :] = gate / (1.0 + jnp.exp(-gate)) * up
-    activated = act_ref[...].astype(BF16)
-    width = down_ref.shape[1] // 8
-
-    @pl.loop(0, 8)
+    pieces, refs = refs[:-8], refs[-8:]
+    token_ref, gate_ref, up_ref, down_ref, own_ref, other_ref, sum_ref, act_ref = refs
+    half, depth = own_ref.shape
+    steps = 8
+    width = depth // steps
+    for step in range(steps):
+        columns = slice(step * width, (step + 1) * width)
+        rows = jnp.concatenate([piece[:, columns] for piece in pieces], axis=0)
+        for weight_ref, target_ref in ((gate_ref, sum_ref), (up_ref, act_ref)):
+            term = dot(weight_ref[:, columns], rows, 1, 1)
+            target_ref[...] = term if step == 0 else target_ref[...] + term
+    gate = sum_ref[...]
+    activated = (gate / (1.0 + jnp.exp(-gate)) * act_ref[...]).T.astype(BF16)
+
+    @pl.loop(0, steps)
     def _(step):
         columns = pl.ds(pl.multiple_of(step * width, width), width)
-        term = dot(activated, down_ref[:, columns], 0, 0)
+        term = dot(activated, down_ref[:, columns])
         own_ref[:, columns] = term[:half]
         other_ref[:, columns] = term[half:]
 
@@ -441,7 +441,7 @@
         in_specs=[VMEM] * (len(pieces) + 4),
         out_specs=[VMEM] * 2,
         out_shape=[jax.ShapeDtypeStruct((rows // 2, depth), F32)] * 2,
-        scratch_shapes=[pltpu.VMEM((units, rows), F32)],
+        scratch_shapes=[pltpu.VMEM((units, rows), F32)] * 2,
         compiler_params=params(6),
         cost_estimate=cost(6 * rows * units * depth, 6 * units * depth),
     )(*pieces, token, gate_t, up_t, down)

time: 109 us -> 108 us (level)
  transfers between devices with their start and end apart: 12 -> 12, of which waited for: 10 -> 10; matrix products, arithmetic and copies ran while one was open for 0% -> 0% of each run, Pallas kernels for 18% -> 19%
where the time goes in v4:
time: 108 us
  Pallas kernels  40.5 us (38%)
  blocking collectives  27.1 us (25%)
  waiting for transfers between devices  19.9 us (18%)
  starting transfers between devices  17.1 us (16%)
  local copies, waits for them, and re-layouts  2.34 us (2%)
    pallas_call x6, Pallas kernels, ahead(): pl.pallas_call(functools.partial(ahead_kernel, count), in_specs=[pl.Block...  20 us
    ppermute x12, waiting for transfers between devices, swapped(): return lax.ppermute(value, axis, [(i, i ^ bit) for i in range(size)])  19.9 us
    ppermute x12, starting transfers between devices, swapped(): return lax.ppermute(value, axis, [(i, i ^ bit) for i in range(size)])  17.1 us
    all_to_all x1, blocking collectives, local(): parts = lax.all_to_all(parts, DEV, 0, 0)  13.9 us
    all_to_all x1, blocking collectives, local(): ffn_term = lax.all_to_all(ffn_term, (FAR, DEV), 0, 0)  13.2 us
    pallas_call x1, Pallas kernels, project(): pl.pallas_call(project_kernel, in_specs=[VMEM] * 4 + [HBM], out_specs=[VM...  7.3 us
    pallas_call x1, Pallas kernels, ffn(): pl.pallas_call(ffn_kernel, in_specs=[VMEM] * (len(pieces) + 4), out_specs...  6.69 us
    pallas_call x1, Pallas kernels, latent_part(): pl.pallas_call(latent_kernel, in_specs=[VMEM, HBM, HBM], out_specs=VMEM,...  3.07 us
  transfers between devices with their start and end apart: 12, of which 10 were waited for; matrix products, arithmetic and copies ran while one was open for 0% of the time, Pallas kernels for 19%

profile of v4, /device:TPU:0, one launch (start us, length us, event | category | flops | bytes accessed | tf_op | source)
XLA Modules:
  0.0 107.9 jit_solution(6718291467143123519)
XLA Ops:
  0.0 0.0 copy-start.2
  0.0 0.7 copy-done.2
  0.7 0.0 copy-start.3
  0.7 0.0 copy-start.4
  0.7 3.1 %shard_map.127.refs_0_.left_ref = f32[8,2688]{1,0:T(8,128)S(1)} custom-call(bf16[8,896]{1,0:T(8,128)(2,1)S(1)} %copy-done.2, f32[896]{0:T(1024)} %gain_hbm.1, bf16[896,2560]{1,0:T(8,128)(2,1)} %w_hbm.2), custom_call_target="tpu_custom_call" | custom-call | flops 36700160 | bytes 4587520 | tf_op jit(solution)/shard_map/pallas_call | solution.py:85
  3.8 3.0 %collective-permute-start = (f32[8,2688]{1,0:T(8,128)S(1)}, f32[8,2688]{1,0:T(8,128)S(1)}, u32[]{:S(2)}, u32[]{:S(2)}) collective-permute-start(f32[8,2688]{1,0:T(8,128)S(1)} %shard_map.127.refs_0_.left_ref), channel_id=1, source_target_pairs={{0,1},{1,0},{2,3},{3,2},{4,5},{5,4},{6,7},{7,6},{8,9},{9,8},{10,11... | collective-permute-start | bytes 258056 | tf_op jit(solution)/shard_map/ppermute | solution.py:475
  6.8 3.4 %shard_map.128 = (bf16[2048,2048]{1,0:T(8,128)(2,1)S(1)}, f32[8,128]{1,0:T(8,128)S(1)}) custom-call(f32[8,2688]{1,0:T(8,128)S(1)} %shard_map.127.refs_0_.left_ref, bf16[2048,2048]{1,0:T(8,128)(2,1)} %refs_1_.4), custom_call_target="tpu_custom_call" | custom-call | bytes 8388608 | tf_op jit(solution)/shard_map/pallas_call | solution.py:117
  10.2 0.0 collective-permute-done.right_ref
  10.3 1.6 %collective-permute-start.1 = (f32[8,2688]{1,0:T(8,128)S(1)}, f32[8,2688]{1,0:T(8,128)S(1)}, u32[]{:S(2)}, u32[]{:S(2)}) collective-permute-start(f32[8,2688]{1,0:T(8,128)S(1)} %shard_map.129.left_ref), channel_id=1, source_target_pairs={{0,2},{1,3},{2,0},{3,1},{4,6},{5,7},{6,4},{7,5},{8,10},{9,11},{10,... | collective-permute-start | bytes 258056 | tf_op jit(solution)/shard_map/ppermute | solution.py:475
  11.9 2.9 %collective-permute-done.1.right_ref = f32[8,2688]{1,0:T(8,128)S(1)} collective-permute-done((f32[8,2688]{1,0:T(8,128)S(1)}, f32[8,2688]{1,0:T(8,128)S(1)}, u32[]{:S(2)}, u32[]{:S(2)}) %collective-permute-start.1) | collective-permute-done | bytes 86048 | tf_op jit(solution)/shard_map/ppermute | solution.py:475
  14.8 2.7 %collective-permute-start.2 = (f32[8,2688]{1,0:T(8,128)S(1)}, f32[8,2688]{1,0:T(8,128)S(1)}, u32[]{:S(2)}, u32[]{:S(2)}) collective-permute-start(f32[8,2688]{1,0:T(8,128)S(1)} %shard_map.130.left_ref), channel_id=1, source_target_pairs={{0,4},{1,5},{2,6},{3,7},{4,0},{5,1},{6,2},{7,3},{8,12},{9,13},{10,... | collective-permute-start | bytes 258056 | tf_op jit(solution)/shard_map/ppermute | solution.py:475
  17.5 2.8 %collective-permute-done.2.right_ref = f32[8,2688]{1,0:T(8,128)S(1)} collective-permute-done((f32[8,2688]{1,0:T(8,128)S(1)}, f32[8,2688]{1,0:T(8,128)S(1)}, u32[]{:S(2)}, u32[]{:S(2)}) %collective-permute-start.2) | collective-permute-done | bytes 86048 | tf_op jit(solution)/shard_map/ppermute | solution.py:475
  20.3 0.0 copy-done.3
  20.3 0.0 copy-done.4
  20.3 1.4 %shard_map.131 = (bf16[112,256]{1,0:T(8,128)(2,1)S(1)}, f32[8,512]{1,0:T(8,128)S(1)}) custom-call(f32[8,2688]{1,0:T(8,128)S(1)} %shard_map.130.left_ref, f32[8,2688]{1,0:T(8,128)S(1)} %collective-permute-done.2.right_ref, f32[8,128]{1,0:T(8,128)S(1)} %get-tuple-element.32.token_ref, f32[1,2048]{1,0:T(1,128)S(1)} %bitcast.5, bf16[8,896]{1,0:T(8,128)(2,1)S(1)} %copy-done.2, ...), custom_call_target="tpu_custom_call" | custom-call | flops 67108864 | bytes 8388608 | tf_op jit(solution)/shard_map/pallas_call | solution.py:245
  21.6 2.7 %collective-permute-start.3 = (bf16[112,256]{1,0:T(8,128)(2,1)S(1)}, bf16[112,256]{1,0:T(8,128)(2,1)S(1)}, u32[]{:S(2)}, u32[]{:S(2)}) collective-permute-start(bf16[112,256]{1,0:T(8,128)(2,1)S(1)} %get-tuple-element.34.left_ref.query_ref), channel_id=1, source_target_pairs={{0,4},{1,5},{2,6},{3,7},{4,0},{5,1},{6,2},{7,3},{8,12},{9,13},{10,... | collective-permute-start | bytes 172040 | tf_op jit(solution)/shard_map/ppermute | solution.py:475
  24.4 2.5 %collective-permute-done.3.right_ref = bf16[112,256]{1,0:T(8,128)(2,1)S(1)} collective-permute-done((bf16[112,256]{1,0:T(8,128)(2,1)S(1)}, bf16[112,256]{1,0:T(8,128)(2,1)S(1)}, u32[]{:S(2)}, u32[]{:S(2)}) %collective-permute-start.3) | collective-permute-done | bytes 57376 | tf_op jit(solution)/shard_map/ppermute | solution.py:475
  26.9 2.1 %collective-permute-start.4 = (bf16[224,256]{1,0:T(8,128)(2,1)S(1)}, bf16[224,256]{1,0:T(8,128)(2,1)S(1)}, u32[]{:S(2)}, u32[]{:S(2)}) collective-permute-start(bf16[224,256]{1,0:T(8,128)(2,1)S(1)} %shard_map.132.refs_0_.left_ref), channel_id=1, source_target_pairs={{0,2},{1,3},{2,0},{3,1},{4,6},{5,7},{6,4},{7,5},{8,10},{9,11},{10,... | collective-permute-start | bytes 344072 | tf_op jit(solution)/shard_map/ppermute | solution.py:475
  29.0 2.2 %shard_map.133 = (bf16[8,512,256]{2,1,0:T(8,128)(2,1)S(1)}, bf16[8,512,256]{2,1,0:T(8,128)(2,1)S(1)}, f32[8,128]{1,0:T(8,128)S(1)}) custom-call(bf16[224,256]{1,0:T(8,128)(2,1)S(1)} %shard_map.132.refs_0_.left_ref, bf16[8,512,256]{2,1,0:T(8,128)(2,1)} %refs_1_.5, bf16[8,512,256]{2,1,0:T(8,128)(2,1)} %refs_2_.1), custom_call_target="tpu_custom_call" | custom-call | bytes 4194304 | tf_op jit(solution)/shard_map/pallas_call | solution.py:117
  31.3 0.0 copy-start
  31.3 1.3 %copy-done = bf16[8,512,256]{2,1,0:T(8,128)(2,1)} copy-done((bf16[8,512,256]{2,1,0:T(8,128)(2,1)}, bf16[8,512,256]{2,1,0:T(8,128)(2,1)S(1)}, u32[]{:S(2)}) %copy-start) | copy-done | bytes 2097176
  32.6 0.0 collective-permute-done.4.right_ref
  32.6 1.6 %collective-permute-start.5 = (bf16[448,256]{1,0:T(8,128)(2,1)S(1)}, bf16[448,256]{1,0:T(8,128)(2,1)S(1)}, u32[]{:S(2)}, u32[]{:S(2)}) collective-permute-start(bf16[448,256]{1,0:T(8,128)(2,1)S(1)} %shard_map.134.refs_0_), channel_id=1, source_target_pairs={{0,1},{1,0},{2,3},{3,2},{4,5},{5,4},{6,7},{7,6},{8,9},{9,8},{10,11... | collective-permute-start | bytes 688136 | tf_op jit(solution)/shard_map/ppermute | solution.py:475
  34.3 0.0 copy-start.1
  34.3 0.0 copy-start.5
  34.3 4.3 %shard_map.135 = (bf16[2048,2688]{1,0:T(8,128)(2,1)S(1)}, f32[8,128]{1,0:T(8,128)S(1)}) custom-call(bf16[448,256]{1,0:T(8,128)(2,1)S(1)} %shard_map.134.refs_0_, bf16[2048,7168]{1,0:T(8,128)(2,1)} %w_hbm.3), custom_call_target="tpu_custom_call" | custom-call | bytes 11010048 | tf_op jit(solution)/shard_map/pallas_call | solution.py:117
  38.6 0.1 collective-permute-done.5.refs_1_
  38.7 0.3 copy-done.1
  39.0 0.0 copy-done.5
  39.0 1.8 %shard_map.136 = (bf16[8,80,256]{2,1,0:T(8,128)(2,1)S(1)}, f32[8,16,1024]{2,1,0:T(8,128)S(1)}) custom-call(s32[1]{0:T(128)} %bitcast.place_ref, s32[8]{0:T(128)S(1)} %copy-done.5, f32[8,128]{1,0:T(8,128)S(1)} %get-tuple-element.36.token_ref, bf16[448,256]{1,0:T(8,128)(2,1)S(1)} %shard_map.134.refs_0_, bf16[448,256]{1,0:T(8,128)(2,1)S(1)} %collective-permute-done.5.refs_1_, ...), custom_call_target="tpu_custom_call" | custom-call | flops 268435456 | bytes 4194304 | tf_op jit(solution)/shard_map/pallas_call | solution.py:325
  40.8 13.9 %all_to_all.10.sent_ref = bf16[8,80,256]{2,1,0:T(8,128)(2,1)S(1)} all-to-all(bf16[8,80,256]{2,1,0:T(8,128)(2,1)S(1)} %get-tuple-element.39), channel_id=1, replica_groups=mesh['far'=2,'core'=2,'dev'=8] {'dev'}, dimensions={0} | all-to-all | bytes 655360 | tf_op jit(solution)/shard_map/all_to_all | solution.py:554
  54.7 7.3 %shard_map.137 = (f32[8,7168]{1,0:T(8,128)S(1)}, bf16[8,7168]{1,0:T(8,128)(2,1)S(1)}) custom-call(bf16[8,80,256]{2,1,0:T(8,128)(2,1)S(1)} %all_to_all.10.sent_ref, bf16[112,256]{1,0:T(8,128)(2,1)S(1)} %get-tuple-element.34.left_ref.query_ref, f32[8,512]{1,0:T(8,128)S(1)} %get-tuple-element.40.fresh_ref, bf16[2048,2688]{1,0:T(8,128)(2,1)S(1)} %get-tuple-element.41.held_ref, ...), custom_call_target="tpu_custom_call" | custom-call | flops 234881024 | bytes 29360128 | tf_op jit(solution)/shard_map/pallas_call | solution.py:397
  62.1 0.5 collective-permute-start.6
  62.6 3.4 %shard_map.138 = (bf16[576,7168]{1,0:T(8,128)(2,1)S(1)}, f32[8,128]{1,0:T(8,128)S(1)}) custom-call(bf16[8,7168]{1,0:T(8,128)(2,1)S(1)} %get-tuple-element.43.refs_0_, bf16[576,7168]{1,0:T(8,128)(2,1)} %bitcast.6), custom_call_target="tpu_custom_call" | custom-call | bytes 8257536 | tf_op jit(solution)/shard_map/pallas_call | solution.py:117
  65.9 1.0 collective-permute-done.6.arrived_ref
  66.9 0.3 collective-permute-start.7
  67.3 3.4 %shard_map.140 = (bf16[576,7168]{1,0:T(8,128)(2,1)S(1)}, f32[8,128]{1,0:T(8,128)S(1)}) custom-call(bf16[8,7168]{1,0:T(8,128)(2,1)S(1)} %get-tuple-element.46.refs_0_, bf16[576,7168]{1,0:T(8,128)(2,1)} %bitcast.7), custom_call_target="tpu_custom_call" | custom-call | bytes 8257536 | tf_op jit(solution)/shard_map/pallas_call | solution.py:117
  70.7 1.2 %collective-permute-done.7.arrived_ref = bf16[8,7168]{1,0:T(8,128)(2,1)S(1)} collective-permute-done((bf16[8,7168]{1,0:T(8,128)(2,1)S(1)}, bf16[8,7168]{1,0:T(8,128)(2,1)S(1)}, u32[]{:S(2)}, u32[]{:S(2)}) %collective-permute-start.7) | collective-permute-done | bytes 114720 | tf_op jit(solution)/shard_map/ppermute | solution.py:475
  71.8 0.6 collective-permute-start.8
  72.5 3.4 %shard_map.142 = (bf16[576,7168]{1,0:T(8,128)(2,1)S(1)}, f32[8,128]{1,0:T(8,128)S(1)}) custom-call(bf16[8,7168]{1,0:T(8,128)(2,1)S(1)} %get-tuple-element.49.refs_0_, bf16[576,7168]{1,0:T(8,128)(2,1)} %refs_1_.7), custom_call_target="tpu_custom_call" | custom-call | bytes 8257536 | tf_op jit(solution)/shard_map/pallas_call | solution.py:117
  75.8 3.0 %collective-permute-done.8.arrived_ref = bf16[8,7168]{1,0:T(8,128)(2,1)S(1)} collective-permute-done((bf16[8,7168]{1,0:T(8,128)(2,1)S(1)}, bf16[8,7168]{1,0:T(8,128)(2,1)S(1)}, u32[]{:S(2)}, u32[]{:S(2)}) %collective-permute-start.8) | collective-permute-done | bytes 114720 | tf_op jit(solution)/shard_map/ppermute | solution.py:475
  78.8 0.2 shard_map.143
  79.0 1.6 %collective-permute-start.9 = (bf16[8,7168]{1,0:T(8,128)(2,1)S(1)}, bf16[8,7168]{1,0:T(8,128)(2,1)S(1)}, u32[]{:S(2)}, u32[]{:S(2)}) collective-permute-start(bf16[8,7168]{1,0:T(8,128)(2,1)S(1)} %get-tuple-element.53.left_ref), channel_id=1, source_target_pairs={{0,16},{16,0},{1,17},{17,1},{2,18},{18,2},{3,19},{19,3},{4,20},{20... | collective-permute-start | bytes 344072 | tf_op jit(solution)/shard_map/ppermute | solution.py:475
  80.5 3.3 %collective-permute-done.9.right_ref = bf16[8,7168]{1,0:T(8,128)(2,1)S(1)} collective-permute-done((bf16[8,7168]{1,0:T(8,128)(2,1)S(1)}, bf16[8,7168]{1,0:T(8,128)(2,1)S(1)}, u32[]{:S(2)}, u32[]{:S(2)}) %collective-permute-start.9) | collective-permute-done | bytes 114720 | tf_op jit(solution)/shard_map/ppermute | solution.py:475
  83.9 0.1 collective-permute-start.10
  84.0 1.5 %collective-permute-done.10.refs_1_ = bf16[16,7168]{1,0:T(8,128)(2,1)S(1)} collective-permute-done((bf16[16,7168]{1,0:T(8,128)(2,1)S(1)}, bf16[16,7168]{1,0:T(8,128)(2,1)S(1)}, u32[]{:S(2)}, u32[]{:S(2)}) %collective-permute-start.10) | collective-permute-done | bytes 229408 | tf_op jit(solution)/shard_map/ppermute | solution.py:475
  85.4 6.7 %shard_map.145 = (f32[16,7168]{1,0:T(8,128)S(1)}, f32[16,7168]{1,0:T(8,128)S(1)}) custom-call(bf16[16,7168]{1,0:T(8,128)(2,1)S(1)} %shard_map.144.refs_0_, bf16[16,7168]{1,0:T(8,128)(2,1)S(1)} %collective-permute-done.10.refs_1_, f32[8,128]{1,0:T(8,128)S(1)} %get-tuple-element.50.token_ref.refs_2_, bf16[576,7168]{1,0:T(8,128)(2,1)S(1)} %get-tuple-element.54.refs_3_, ...), custom_call_target="tpu_custom_call" | custom-call | flops 792723456 | bytes 24772608 | tf_op jit(solution)/shard_map/pallas_call | solution.py:439
  92.1 0.2 collective-permute-start.11
  92.3 1.7 %collective-permute-done.11.arrived_ref = f32[16,7168]{1,0:T(8,128)S(1)} collective-permute-done((f32[16,7168]{1,0:T(8,128)S(1)}, f32[16,7168]{1,0:T(8,128)S(1)}, u32[]{:S(2)}, u32[]{:S(2)}) %collective-permute-start.11) | collective-permute-done | bytes 458784 | tf_op jit(solution)/shard_map/ppermute | solution.py:475
  94.0 0.1 shard_map.146
  94.1 13.2 %all_to_all.11 = bf16[16,8,896]{2,1,0:T(8,128)(2,1)S(1)} all-to-all(bf16[16,8,896]{2,1,0:T(8,128)(2,1)S(1)} %shard_map.146), channel_id=1, replica_groups=mesh['far'=2,'core'=2,'dev'=8] {'far','dev'}, dimensions={0} | all-to-all | bytes 458752 | tf_op jit(solution)/shard_map/all_to_all | solution.py:572
  107.3 0.6 add.3
  (8 shorter events, 0.2 us)
Async XLA Ops:
  0.0 0.7 copy-start.2
  0.7 19.6 %copy-start.3 = (f32[2048]{0:T(1024)S(1)}, f32[2048]{0:T(1024)}, u32[]{:S(2)}) copy-start(f32[2048]{0:T(1024)} %param.16) | copy-start | bytes 24580
  0.7 19.6 %copy-start.4 = (f32[896]{0:T(1024)S(1)}, f32[896]{0:T(1024)}, u32[]{:S(2)}) copy-start(f32[896]{0:T(1024)} %next_ref.1) | copy-start | bytes 10756
  3.8 6.4 %collective-permute-start = (f32[8,2688]{1,0:T(8,128)S(1)}, f32[8,2688]{1,0:T(8,128)S(1)}, u32[]{:S(2)}, u32[]{:S(2)}) collective-permute-start(f32[8,2688]{1,0:T(8,128)S(1)} %shard_map.127.refs_0_.left_ref), channel_id=1, source_target_pairs={{0,1},{1,0},{2,3},{3,2},{4,5},{5,4},{6,7},{7,6},{8,9},{9,8},{10,11... | collective-permute-start | bytes 258056 | tf_op jit(solution)/shard_map/ppermute | solution.py:475
  10.3 4.6 %collective-permute-start.1 = (f32[8,2688]{1,0:T(8,128)S(1)}, f32[8,2688]{1,0:T(8,128)S(1)}, u32[]{:S(2)}, u32[]{:S(2)}) collective-permute-start(f32[8,2688]{1,0:T(8,128)S(1)} %shard_map.129.left_ref), channel_id=1, source_target_pairs={{0,2},{1,3},{2,0},{3,1},{4,6},{5,7},{6,4},{7,5},{8,10},{9,11},{10,... | collective-permute-start | bytes 258056 | tf_op jit(solution)/shard_map/ppermute | solution.py:475
  14.8 5.4 %collective-permute-start.2 = (f32[8,2688]{1,0:T(8,128)S(1)}, f32[8,2688]{1,0:T(8,128)S(1)}, u32[]{:S(2)}, u32[]{:S(2)}) collective-permute-start(f32[8,2688]{1,0:T(8,128)S(1)} %shard_map.130.left_ref), channel_id=1, source_target_pairs={{0,4},{1,5},{2,6},{3,7},{4,0},{5,1},{6,2},{7,3},{8,12},{9,13},{10,... | collective-permute-start | bytes 258056 | tf_op jit(solution)/shard_map/ppermute | solution.py:475
  21.6 5.2 %collective-permute-start.3 = (bf16[112,256]{1,0:T(8,128)(2,1)S(1)}, bf16[112,256]{1,0:T(8,128)(2,1)S(1)}, u32[]{:S(2)}, u32[]{:S(2)}) collective-permute-start(bf16[112,256]{1,0:T(8,128)(2,1)S(1)} %get-tuple-element.34.left_ref.query_ref), channel_id=1, source_target_pairs={{0,4},{1,5},{2,6},{3,7},{4,0},{5,1},{6,2},{7,3},{8,12},{9,13},{10,... | collective-permute-start | bytes 172040 | tf_op jit(solution)/shard_map/ppermute | solution.py:475
  26.9 5.7 %collective-permute-start.4 = (bf16[224,256]{1,0:T(8,128)(2,1)S(1)}, bf16[224,256]{1,0:T(8,128)(2,1)S(1)}, u32[]{:S(2)}, u32[]{:S(2)}) collective-permute-start(bf16[224,256]{1,0:T(8,128)(2,1)S(1)} %shard_map.132.refs_0_.left_ref), channel_id=1, source_target_pairs={{0,2},{1,3},{2,0},{3,1},{4,6},{5,7},{6,4},{7,5},{8,10},{9,11},{10,... | collective-permute-start | bytes 344072 | tf_op jit(solution)/shard_map/ppermute | solution.py:475
  31.3 1.3 %copy-start = (bf16[8,512,256]{2,1,0:T(8,128)(2,1)}, bf16[8,512,256]{2,1,0:T(8,128)(2,1)S(1)}, u32[]{:S(2)}) copy-start(bf16[8,512,256]{2,1,0:T(8,128)(2,1)S(1)} %get-tuple-element.38.refs_3_) | copy-start | bytes 6291460
  32.6 6.1 %collective-permute-start.5 = (bf16[448,256]{1,0:T(8,128)(2,1)S(1)}, bf16[448,256]{1,0:T(8,128)(2,1)S(1)}, u32[]{:S(2)}, u32[]{:S(2)}) collective-permute-start(bf16[448,256]{1,0:T(8,128)(2,1)S(1)} %shard_map.134.refs_0_), channel_id=1, source_target_pairs={{0,1},{1,0},{2,3},{3,2},{4,5},{5,4},{6,7},{7,6},{8,9},{9,8},{10,11... | collective-permute-start | bytes 688136 | tf_op jit(solution)/shard_map/ppermute | solution.py:475
  34.3 4.7 %copy-start.1 = (bf16[8,512,256]{2,1,0:T(8,128)(2,1)S(1)}, bf16[8,512,256]{2,1,0:T(8,128)(2,1)}, u32[]{:S(2)}) copy-start(bf16[8,512,256]{2,1,0:T(8,128)(2,1)} %copy-done) | copy-start | bytes 6291460
  34.3 4.7 %copy-start.5 = (s32[8]{0:T(128)S(1)}, s32[8]{0:T(128)}, u32[]{:S(2)}) copy-start(s32[8]{0:T(128)} %lengths_ref.1) | copy-start | bytes 100
  62.1 4.9 %collective-permute-start.6 = (bf16[8,7168]{1,0:T(8,128)(2,1)S(1)}, bf16[8,7168]{1,0:T(8,128)(2,1)S(1)}, u32[]{:S(2)}, u32[]{:S(2)}) collective-permute-start(bf16[8,7168]{1,0:T(8,128)(2,1)S(1)} %get-tuple-element.43.refs_0_), channel_id=1, source_target_pairs={{0,1},{1,0},{2,3},{3,2},{4,5},{5,4},{6,7},{7,6},{8,9},{9,8},{10,11... | collective-permute-start | bytes 344072 | tf_op jit(solution)/shard_map/ppermute | solution.py:475
  66.9 4.9 %collective-permute-start.7 = (bf16[8,7168]{1,0:T(8,128)(2,1)S(1)}, bf16[8,7168]{1,0:T(8,128)(2,1)S(1)}, u32[]{:S(2)}, u32[]{:S(2)}) collective-permute-start(bf16[8,7168]{1,0:T(8,128)(2,1)S(1)} %get-tuple-element.46.refs_0_), channel_id=1, source_target_pairs={{0,2},{1,3},{2,0},{3,1},{4,6},{5,7},{6,4},{7,5},{8,10},{9,11},{10,... | collective-permute-start | bytes 344072 | tf_op jit(solution)/shard_map/ppermute | solution.py:475
  71.8 7.0 %collective-permute-start.8 = (bf16[8,7168]{1,0:T(8,128)(2,1)S(1)}, bf16[8,7168]{1,0:T(8,128)(2,1)S(1)}, u32[]{:S(2)}, u32[]{:S(2)}) collective-permute-start(bf16[8,7168]{1,0:T(8,128)(2,1)S(1)} %get-tuple-element.49.refs_0_), channel_id=1, source_target_pairs={{0,4},{1,5},{2,6},{3,7},{4,0},{5,1},{6,2},{7,3},{8,12},{9,13},{10,... | collective-permute-start | bytes 344072 | tf_op jit(solution)/shard_map/ppermute | solution.py:475
  79.0 4.9 %collective-permute-start.9 = (bf16[8,7168]{1,0:T(8,128)(2,1)S(1)}, bf16[8,7168]{1,0:T(8,128)(2,1)S(1)}, u32[]{:S(2)}, u32[]{:S(2)}) collective-permute-start(bf16[8,7168]{1,0:T(8,128)(2,1)S(1)} %get-tuple-element.53.left_ref), channel_id=1, source_target_pairs={{0,16},{16,0},{1,17},{17,1},{2,18},{18,2},{3,19},{19,3},{4,20},{20... | collective-permute-start | bytes 344072 | tf_op jit(solution)/shard_map/ppermute | solution.py:475
  83.9 1.6 %collective-permute-start.10 = (bf16[16,7168]{1,0:T(8,128)(2,1)S(1)}, bf16[16,7168]{1,0:T(8,128)(2,1)S(1)}, u32[]{:S(2)}, u32[]{:S(2)}) collective-permute-start(bf16[16,7168]{1,0:T(8,128)(2,1)S(1)} %shard_map.144.refs_0_), channel_id=1, source_target_pairs={{0,8},{8,0},{1,9},{9,1},{2,10},{10,2},{3,11},{11,3},{4,12},{12,4},... | collective-permute-start | bytes 688136 | tf_op jit(solution)/shard_map/ppermute | solution.py:475
  92.1 1.9 %collective-permute-start.11 = (f32[16,7168]{1,0:T(8,128)S(1)}, f32[16,7168]{1,0:T(8,128)S(1)}, u32[]{:S(2)}, u32[]{:S(2)}) collective-permute-start(f32[16,7168]{1,0:T(8,128)S(1)} %get-tuple-element.58), channel_id=1, source_target_pairs={{0,8},{8,0},{1,9},{9,1},{2,10},{10,2},{3,11},{11,3},{4,12},{12,4},... | collective-permute-start | bytes 1376264 | tf_op jit(solution)/shard_map/ppermute | solution.py:475
